TPU v7x, 32 devices: a whole 2x2x4 slice. The times are simulated.
32 devices in a mesh: row: 4 (over y, x), col: 8 (over z, core).
Axes of the slice: x: 2, y: 2, z: 4, core: 2. Of those that a mesh axis runs over, the one named last changes fastest.
Arguments:
- grad_out: bfloat16 [4096, 128], P(('row', 'col')), may hold values from -6 to 6
- pre_act: bfloat16 [4096, 128], P(('row', 'col')), may hold values from -6 to 6
- features: bfloat16 [4096, 128], P(('row', 'col')), may hold values from -6 to 6
- weight: bfloat16 [128, 128], replicated, may hold values from -0.5 to 0.5
- blocks: bfloat16 [4, 8, 8, 2, 128, 128], P('row', 'col'), may hold values from -0.125 to 0.125
- block_cols: int32 [4, 8, 8, 2], P('row', 'col'), may hold values from 0 to 3
- block_counts: int32 [4, 8, 8], P('row', 'col'), may hold values from 0 to 2, as said below
- order: int32 [4096], P(('row', 'col')), may hold values from 0 to 127, as said below
Outputs:
- grad_feat: bfloat16 [4096, 128], P(('row', 'col'))
- weight_grad: float32 [128, 128], replicated
Inputs may be any that keep to these rules, and one draw needn't show every extreme that they name: `block_counts`: every device's slice has at least one row block with 2 nonzero blocks. `order`: each slab of 128 entries is a permutation of 0 to 127.
All inputs are finite; a program needn't handle non-finite values.
Results may differ from a plain program's by a relative error of at most 0.019.
Values may be sent and summed in bfloat16 or wider, within the bound.
No kernel may reach another device: no remote copies, remote signals or barrier semaphores. Data moves between devices by JAX's collectives and lax.ppermute only.
A program may use at most 64 MiB of HBM per device.

v0:
```python
import jax
import jax.numpy as jnp
from jax import lax
from jax.sharding import PartitionSpec as P

F = 128
B = 128
K = 2


def shards(grad_out, pre_act, features, weight, blocks, block_cols, block_counts, order):
    slab_rows = grad_out.shape[0]
    row_count = lax.axis_size("row")
    col_count = lax.axis_size("col")
    targets = row_count * (slab_rows // B)
    masked = jnp.where(pre_act > 0, grad_out, jnp.zeros_like(grad_out))
    masked_block = jnp.take(masked, order, axis=0)
    feat_block = jnp.take(features, order, axis=0)
    block_vals = blocks[0, 0]
    columns = block_cols[0, 0]
    counts = block_counts[0, 0]
    filled = jnp.arange(K, dtype=jnp.int32)[None, :] < counts[:, None]
    hits = columns[:, :, None] == jnp.arange(targets, dtype=jnp.int32)[None, None, :]
    selector = jnp.where(hits & filled[:, :, None], 1.0, 0.0).astype(jnp.float32)
    region = lax.all_gather(masked_block, "col", axis=0, tiled=True)
    count_rows = region.shape[0]
    blk_count = count_rows // B
    panel_rows = region.reshape(blk_count, B, F)
    products = jnp.einsum(
        "ikrc,irf->ikcf", block_vals, panel_rows, preferred_element_type=jnp.float32
    )
    partial_value = jnp.einsum("ikj,ikcf->jcf", selector, products, precision=lax.Precision.HIGHEST)
    owned_sum = lax.psum_scatter(
        partial_value.reshape(targets * B, F).astype(jnp.bfloat16),
        "row",
        scatter_dimension=0,
        tiled=True,
    )
    grad_block = lax.dot_general(
        owned_sum, weight, (((1,), (1,)), ((), ())), preferred_element_type=jnp.float32
    ).astype(jnp.bfloat16)
    grad_feat = jnp.zeros_like(grad_block).at[order].set(grad_block)
    partial_w = lax.dot_general(
        feat_block, owned_sum, (((0,), (0,)), ((), ())), preferred_element_type=jnp.float32
    )
    summed_w = lax.psum(partial_w, ("row", "col"))
    node_total = slab_rows * row_count * col_count
    return (grad_feat, summed_w * node_total ** (-0.5))


def solution(mesh):
    placed = (
        P(("row", "col"), None),
        P(("row", "col"), None),
        P(("row", "col"), None),
        P(),
        P("row", "col", None, None, None, None),
        P("row", "col", None, None),
        P("row", "col", None),
        P(("row", "col")),
    )
    return jax.shard_map(
        shards,
        mesh=mesh,
        in_specs=placed,
        out_specs=(P(("row", "col"), None), P()),
        check_vma=False,
    )
```

profile of v0, /device:TPU:0, one launch (start us, length us, event | category | flops | bytes accessed | tf_op | source)
XLA Modules:
  0.0 187.1 jit_solution(13226615708826678045)
XLA Ops:
  7.2 0.0 reduce-scatter.2.cloned.1.call-start
  7.2 0.7 compare_select_fusion.1
  8.0 0.8 compare_select_fusion
  8.7 0.7 gather_fusion
  9.5 0.1 broadcast_select_fusion
  9.6 15.9 %all_gather.3 = bf16[1024,128]{1,0:T(8,128)(2,1)S(1)} all-gather(bf16[128,128]{1,0:T(8,128)(2,1)S(1)} %broadcast_select_fusion), channel_id=1, replica_groups=mesh['row'=4,'col'=8] {'col'}, dimensions={0}, use_global_device_ids=true | all-gather | bytes 294912 | tf_op jit(solution)/shard_map/all_gather | solution.py:25
  25.4 0.3 fusion.2
  25.8 0.5 copy.12
  26.3 0.6 copy-done.6
  27.0 0.7 copy-done.4
  27.7 0.8 fusion
  28.4 0.7 copy.10
  29.1 0.0 reduce-scatter.2.cloned.1.call-update
  29.1 0.0 all-reduce.2.cloned.1.call-start
  29.2 0.7 copy-done.1
  29.9 0.7 gather_fusion.1
  30.6 23.6 %reduce-scatter.2.cloned.1.call-done = bf16[128,128]{1,0:T(8,128)(2,1)} async-done(((bf16[512,128]{1,0:T(8,128)(2,1)}), bf16[128,128]{1,0:T(8,128)(2,1)}) %reduce-scatter.2.cloned.1.call-update) | async-done | bytes 32784 | tf_op jit(solution)/shard_map/reduce_scatter | solution.py:33
  54.2 1.6 fusion.4
  55.8 0.0 all-reduce.2.cloned.1.call-update
  55.9 0.7 copy-done.2
  56.6 0.1 convolution_convert_fusion
  56.7 1.5 scatter_custom_fusion
  58.2 120.6 %all-reduce.2.cloned.1.call-done = f32[128,128]{1,0:T(8,128)} async-done(((f32[128,128]{1,0:T(8,128)}), f32[128,128]{1,0:T(8,128)}) %all-reduce.2.cloned.1.call-update) | async-done | bytes 65552 | tf_op jit(solution)/shard_map/psum | solution.py:46
  178.8 1.5 broadcast_multiply_fusion
  (13 shorter events, 0.1 us)
Async XLA Ops:
  7.2 18.3 %copy-start = (bf16[1,1,8,2,128,128]{5,4,3,2,1,0:T(8,128)(2,1)S(1)}, bf16[1,1,8,2,128,128]{5,4,3,2,1,0:T(8,128)(2,1)}, u32[]{:S(2)}) copy-start(bf16[1,1,8,2,128,128]{5,4,3,2,1,0:T(8,128)(2,1)} %param.14) | copy-start | bytes 1572868
  7.2 0.8 copy-start.5
  7.2 47.0 %reduce-scatter.2.cloned.1.call-start = ((), (), s32[]{:S(2)}) async-start(), calls=%async_computation.1 | async-start | bytes 163840 | tf_op jit(solution)/shard_map/reduce_scatter | solution.py:33
  26.3 0.7 copy-start.6
  27.0 0.7 copy-start.4
  29.1 0.8 copy-start.1
  29.1 149.7 %all-reduce.2.cloned.1.call-start = ((), (), s32[]{:S(2)}) async-start(), calls=%async_computation.2 | async-start | bytes 131072 | tf_op jit(solution)/shard_map/psum | solution.py:46
  55.8 0.8 copy-start.2
  55.8 0.8 copy-start.3
Sparse Core Ops, SparseCore 0:
  29.2 24.9 reduce-scatter.1
  61.3 117.5 all-reduce.1
where the time goes:
time: 189 us; the launch traced here: 187 us
  waiting for transfers between devices  144 us (76%)
  blocking collectives  15.9 us (8%)
  between operations  14.1 us (7%)
  local copies, waits for them, and re-layouts  6.84 us (4%)
  other arithmetic  3.07 us (2%)
  matrix products  2.89 us (2%)
    psum x1, waiting for transfers between devices, shards(): summed_w = lax.psum(partial_w, ('row', 'col'))  121 us
    reduce_scatter x1, waiting for transfers between devices, shards(): lax.psum_scatter(partial_value.reshape(targets * B, F).astype(jnp.bfloat1...  23.6 us
    all_gather x1, blocking collectives, shards(): region = lax.all_gather(masked_block, 'col', axis=0, tiled=True)  15.9 us
  transfers between devices with their start and end apart: 2, of which 2 were waited for; matrix products, arithmetic and copies ran while one was open for 1% of the time, Pallas kernels for 0%

commit v1 on v0

v1 whole, which is shorter than its diff:
```python
import functools

import jax
import jax.numpy as jnp
from jax import lax
from jax.experimental import pallas as pl
from jax.experimental.pallas import tpu as pltpu
from jax.sharding import PartitionSpec as P

F = 128
B = 128
K = 2
BF = jnp.bfloat16
F32 = jnp.float32
VMEM = pl.BlockSpec(memory_space=pltpu.VMEM)
SMEM = pl.BlockSpec(memory_space=pltpu.SMEM)


def swaps(size):
    return size & (size - 1) == 0


def target_of(index, step, size):
    return index ^ step if swaps(size) else (index + step) % size


def source_of(index, step, size):
    return index ^ step if swaps(size) else lax.rem(index + (size - step), size)


def dot(a, b, contract):
    return lax.dot_general(a, b, (contract, ((), ())), preferred_element_type=F32)


def call(body, outs, args, scalars=(), scratch=()):
    return pl.pallas_call(
        body,
        out_shape=outs,
        in_specs=[SMEM] * len(scalars) + [VMEM] * len(args),
        out_specs=[VMEM] * len(outs),
        scratch_shapes=list(scratch),
    )(*scalars, *args)


def spread(order_row):
    n = order_row.shape[1]
    return (lax.broadcasted_iota(jnp.int32, (n, n), 0) == order_row).astype(BF)


def first_kernel(grad_ref, pre_ref, feat_ref, order_ref, keep_ref, give_ref):
    core = lax.rem(lax.axis_index("col"), 2)
    place = spread(order_ref[...])
    grad = grad_ref[...]
    masked = jnp.where(pre_ref[...].astype(F32) > 0, grad.astype(F32), 0.0).astype(BF)
    masked = dot(place, masked, ((0,), (0,))).astype(BF)
    feat = dot(place, feat_ref[...], ((0,), (0,))).astype(BF)
    even = core == 0
    keep_ref[...] = jnp.where(even, masked, feat)
    give_ref[...] = jnp.where(even, feat, masked)


def product_kernel(rows, depth, *refs):
    steps = max(rows, depth)
    cols_ref, counts_ref = refs[0], refs[1]
    blocks_ref = refs[2]
    own, other = refs[3 : 3 + steps], refs[3 + steps : 3 + 2 * steps]
    outs = refs[3 + 2 * steps : -1]
    total = refs[-1]
    r = lax.axis_index("row")
    c = lax.axis_index("col")
    z, even = lax.div(c, 2), lax.rem(c, 2) == 0
    total[...] = jnp.zeros_like(total)
    for step in range(depth):
        pair = jnp.where(even, own[step][...], other[step][...])
        chip = source_of(z, step, depth)
        for core in range(2):
            i = 2 * chip + core
            panel = pair[core * B : (core + 1) * B]
            for k in range(K):
                j = jnp.where(k < counts_ref[0, 0, i], cols_ref[0, 0, i, k], rows)
                total[j] += dot(blocks_ref[0, 0, i, k], panel, ((0,), (0,)))
    terms = [total[source_of(r, step, rows)].astype(BF) for step in range(rows)]
    weight = jnp.zeros((F, F), F32)
    for step in range(rows):
        feat = jnp.where(even, other[step][B : 2 * B], own[step][0:B])
        weight += dot(feat, terms[step], ((0,), (0,)))
    weight = weight.astype(BF)
    outs[0][0:B] = terms[0]
    outs[0][B : 2 * B] = weight
    for step in range(1, rows):
        out = terms[step] if swaps(rows) else terms[rows - step]
        outs[step][0:B] = out
        outs[step][B : 2 * B] = weight


def sum_in_order(values, index, size):
    values = [v.astype(F32) for v in values]
    if swaps(size):
        while len(values) > 1:
            values = [a + b for a, b in zip(values[0::2], values[1::2])]
        return values[0]
    places = jnp.stack([source_of(index, step, size) for step in range(size)])
    held = jnp.zeros((size,) + values[0].shape, F32).at[places].set(jnp.stack(values))
    return functools.reduce(lambda a, b: a + b, [held[i] for i in range(size)])


def feature_kernel(count, order_ref, weight_ref, *refs):
    terms, out_ref = refs[:count], refs[count]
    total = terms[0][0:B].astype(F32)
    for term in terms[1:]:
        total += term[0:B].astype(F32)
    grad = dot(total.astype(BF), weight_ref[...], ((1,), (1,))).astype(BF)
    out_ref[...] = dot(spread(order_ref[...]), grad, ((1,), (0,))).astype(BF)


def shards(grad_out, pre_act, features, weight, blocks, block_cols, block_counts, order):
    slab_rows = grad_out.shape[0]
    rows = lax.axis_size("row")
    cols = lax.axis_size("col")
    depth = cols // 2
    axes = ("row", "col")
    r, z = lax.axis_index("row"), lax.div(lax.axis_index("col"), 2)
    order_row = order.reshape(1, slab_rows)
    slab = jax.ShapeDtypeStruct((B, F), BF)
    pair = jax.ShapeDtypeStruct((2 * B, F), BF)

    def across(value):
        return lax.ppermute(value, "col", [(i, i ^ 1) for i in range(cols)])

    def along_row(value, step):
        return lax.ppermute(value, "row", [(i, target_of(i, step, rows)) for i in range(rows)])

    def along_depth(value, step):
        pairs = [(i, 2 * target_of(i // 2, step, depth) + i % 2) for i in range(cols)]
        return lax.ppermute(value, "col", pairs)

    def both(value, step):
        pairs = []
        for i in range(rows):
            for j in range(depth):
                if step < depth:
                    pairs.append((i * cols + 2 * j, i * cols + 2 * target_of(j, step, depth)))
                if step < rows:
                    pairs.append((i * cols + 2 * j + 1, target_of(i, step, rows) * cols + 2 * j + 1))
        return lax.ppermute(value, axes, pairs)

    keep, give = call(first_kernel, [slab, slab], (grad_out, pre_act, features, order_row))
    message = jnp.concatenate([keep, across(give)], axis=0)
    steps = max(rows, depth)
    own = [message] + [both(message, step) for step in reversed(range(1, steps))][::-1]
    other = [across(value) for value in own]
    out = call(
        functools.partial(product_kernel, rows, depth),
        [pair] * rows,
        (blocks, *own, *other),
        scalars=(block_cols, block_counts),
        scratch=[pltpu.VMEM((rows + 1, B, F), F32)],
    )
    terms = [out[0]] + [along_row(out[step], step) for step in range(1, rows)]
    total = sum_in_order([term[B:] for term in terms], r, rows)
    total = (total + across(total)).astype(BF)
    (grad_feat,) = call(functools.partial(feature_kernel, rows), [slab], (order_row, weight, *terms))
    totals = [total] + [along_depth(total, step) for step in range(1, depth)]
    summed = sum_in_order(totals, z, depth)
    return grad_feat, summed * (slab_rows * rows * cols) ** (-0.5)


def solution(mesh):
    placed = (
        P(("row", "col"), None),
        P(("row", "col"), None),
        P(("row", "col"), None),
        P(),
        P("row", "col", None, None, None, None),
        P("row", "col", None, None),
        P("row", "col", None),
        P(("row", "col")),
    )
    return jax.shard_map(
        shards,
        mesh=mesh,
        in_specs=placed,
        out_specs=(P(("row", "col"), None), P()),
        check_vma=False,
    )
```

time: 189 us -> 37.2 us (0.20)
  waiting for transfers between devices: 144 us -> 11.5 us
  blocking collectives: 15.9 us -> 0 us
  starting transfers between devices: 0.08 us -> 14.6 us
  between operations: 14.1 us -> 0.72 us
  Pallas kernels: 0 us -> 5.98 us
  local copies, waits for them, and re-layouts: 6.84 us -> 2.56 us
  matrix products: 2.89 us -> 0 us
    psum x1 -> x0, waiting for transfers between devices: 121 us -> none  [shards(): summed_w = lax.psum(partial_w, ('row', 'col'))]
    reduce_scatter x1 -> x0, waiting for transfers between devices: 23.6 us -> none  [shards(): lax.psum_scatter(partial_value.reshape(targets * B, F).astype(jnp.bfloat1...]
    all_gather x1 -> x0, blocking collectives: 15.9 us -> none  [shards(): region = lax.all_gather(masked_block, 'col', axis=0, tiled=True)]
    ppermute x0 -> x15, starting transfers between devices: none -> 14.6 us  [the longest x3 5.65 us: both(): return lax.ppermute(value, axes, pairs)]
    ppermute x0 -> x15, waiting for transfers between devices: none -> 11.5 us  [the longest x3 4.9 us: along_row(): lax.ppermute(value, 'row', [(i, target_of(i, step, rows)) for i in range(...]
    pallas_call x0 -> x3, Pallas kernels: none -> 5.98 us  [call(): pl.pallas_call(body, out_shape=outs, in_specs=[SMEM] * len(scalars) + [VM...]
    dot_general x4 -> x0, matrix products: 2.89 us -> none  [the longest x1 1.64 us: shards(): lax.dot_general(feat_block, owned_sum, (((0,), (0,)), ((), ())), preferre...]
  transfers between devices with their start and end apart: 2 -> 15, of which waited for: 2 -> 9; matrix products, arithmetic and copies ran while one was open for 1% -> 4% of each run, Pallas kernels for 0% -> 5%
where the time goes in v1:
time: 37.2 us; the launch traced here: 36.8 us
  starting transfers between devices  14.6 us (39%)
  waiting for transfers between devices  11.5 us (31%)
  Pallas kernels  5.98 us (16%)
  local copies, waits for them, and re-layouts  2.56 us (7%)
  other arithmetic  1.44 us (4%)
  between operations  0.72 us (2%)
    pallas_call x3, Pallas kernels, call(): pl.pallas_call(body, out_shape=outs, in_specs=[SMEM] * len(scalars) + [VM...  5.98 us
    ppermute x3, starting transfers between devices, both(): return lax.ppermute(value, axes, pairs)  5.65 us
    ppermute x3, waiting for transfers between devices, along_row(): lax.ppermute(value, 'row', [(i, target_of(i, step, rows)) for i in range(...  4.9 us
    ppermute x3, waiting for transfers between devices, both(): return lax.ppermute(value, axes, pairs)  4.52 us
    ppermute x3, starting transfers between devices, along_depth(): return lax.ppermute(value, 'col', pairs)  4.45 us
    ppermute x3, starting transfers between devices, along_row(): lax.ppermute(value, 'row', [(i, target_of(i, step, rows)) for i in range(...  3.49 us
    unnamed x26, local copies, waits for them, and re-layouts  2.55 us
    ppermute x6, waiting for transfers between devices, across(): return lax.ppermute(value, 'col', [(i, i ^ 1) for i in range(cols)])  1.76 us
  transfers between devices with their start and end apart: 15, of which 9 were waited for; matrix products, arithmetic and copies ran while one was open for 4% of the time, Pallas kernels for 5%

profile of v1, /device:TPU:0, one launch (start us, length us, event | category | flops | bytes accessed | tf_op | source)
XLA Modules:
  0.0 36.8 jit_solution(5502764722173656004)
XLA Ops:
  0.6 1.6 %shard_map.95 = (bf16[128,128]{1,0:T(8,128)(2,1)}, bf16[128,128]{1,0:T(8,128)(2,1)}) custom-call(bf16[128,128]{1,0:T(8,128)(2,1)} %grad_ref.1, bf16[128,128]{1,0:T(8,128)(2,1)} %pre_ref.1, bf16[128,128]{1,0:T(8,128)(2,1)} %feat_ref.1, s32[1,128]{1,0:T(1,128)} %bitcast.1), custom_call_target="tpu_custom_call" | custom-call | tf_op jit(solution)/shard_map/pallas_call | solution.py:36
  2.3 0.5 %collective-permute-start = (bf16[128,128]{1,0:T(8,128)(2,1)}, bf16[128,128]{1,0:T(8,128)(2,1)S(1)}, u32[]{:S(2)}, u32[]{:S(2)}) collective-permute-start(bf16[128,128]{1,0:T(8,128)(2,1)} %get-tuple-element.9), channel_id=1, source_target_pairs={{0,1},{1,0},{2,3},{3,2},{4,5},{5,4},{6,7},{7,6},{8,9},{9,8},{10,11... | collective-permute-start | bytes 98312 | tf_op jit(solution)/shard_map/ppermute | solution.py:128
  2.7 0.8 %constant_dynamic-update-slice_fusion.1 = bf16[256,128]{1,0:T(8,128)(2,1)S(1)} fusion(bf16[128,128]{1,0:T(8,128)(2,1)} %get-tuple-element.8), kind=kLoop, calls=%fused_computation.4 | loop fusion | bytes 65536
  3.8 5.0 %collective-permute-start.3 = (bf16[256,128]{1,0:T(8,128)(2,1)S(1)}, bf16[256,128]{1,0:T(8,128)(2,1)S(1)}, u32[]{:S(2)}, u32[]{:S(2)}) collective-permute-start(bf16[256,128]{1,0:T(8,128)(2,1)S(1)} %constant_dynamic-update-slice_fusion.refs_3_), channel_id=1, source_target_pairs={{0,6},{1,25},{2,4},{3,27},{4,2},{5,29},{6,0},{7,31},{8,14},{9,17},... | collective-permute-start | bytes 196616 | tf_op jit(solution)/shard_map/ppermute | solution.py:145
  8.8 0.6 %collective-permute-start.1 = (bf16[256,128]{1,0:T(8,128)(2,1)S(1)}, bf16[256,128]{1,0:T(8,128)(2,1)S(1)}, u32[]{:S(2)}, u32[]{:S(2)}) collective-permute-start(bf16[256,128]{1,0:T(8,128)(2,1)S(1)} %constant_dynamic-update-slice_fusion.refs_3_), channel_id=1, source_target_pairs={{0,2},{1,9},{2,0},{3,11},{4,6},{5,13},{6,4},{7,15},{8,10},{9,1},{1... | collective-permute-start | bytes 196616 | tf_op jit(solution)/shard_map/ppermute | solution.py:145
  9.4 1.7 %collective-permute-done.3.refs_6_ = bf16[256,128]{1,0:T(8,128)(2,1)S(1)} collective-permute-done((bf16[256,128]{1,0:T(8,128)(2,1)S(1)}, bf16[256,128]{1,0:T(8,128)(2,1)S(1)}, u32[]{:S(2)}, u32[]{:S(2)}) %collective-permute-start.3) | collective-permute-done | bytes 65568 | tf_op jit(solution)/shard_map/ppermute | solution.py:145
  11.2 2.8 %collective-permute-done.2.refs_5_ = bf16[256,128]{1,0:T(8,128)(2,1)S(1)} collective-permute-done((bf16[256,128]{1,0:T(8,128)(2,1)S(1)}, bf16[256,128]{1,0:T(8,128)(2,1)S(1)}, u32[]{:S(2)}, u32[]{:S(2)}) %collective-permute-start.2) | collective-permute-done | bytes 65568 | tf_op jit(solution)/shard_map/ppermute | solution.py:145
  14.0 0.5 %collective-permute-start.5 = (bf16[256,128]{1,0:T(8,128)(2,1)S(1)}, bf16[256,128]{1,0:T(8,128)(2,1)S(1)}, u32[]{:S(2)}, u32[]{:S(2)}) collective-permute-start(bf16[256,128]{1,0:T(8,128)(2,1)S(1)} %collective-permute-done.1.refs_4_), channel_id=1, source_target_pairs={{0,1},{1,0},{2,3},{3,2},{4,5},{5,4},{6,7},{7,6},{8,9},{9,8},{10,11... | collective-permute-start | bytes 196616 | tf_op jit(solution)/shard_map/ppermute | solution.py:128
  14.5 0.7 %copy.10.refs_0_ = s32[1,1,8,2]{3,2,1,0:T(8,128)} copy(s32[1,1,8,2]{2,3,1,0:T(2,128)S(1)} %copy-done.11) | data formatting | bytes 128 | tf_op args[5]
  15.9 0.6 %copy-done.10 = bf16[256,128]{1,0:T(8,128)(2,1)} copy-done((bf16[256,128]{1,0:T(8,128)(2,1)}, bf16[256,128]{1,0:T(8,128)(2,1)S(1)}, u32[]{:S(2)}) %copy-start.10) | copy-done | bytes 65560
  16.5 2.5 %shard_map.96 = (bf16[256,128]{1,0:T(8,128)(2,1)}, bf16[256,128]{1,0:T(8,128)(2,1)}, bf16[256,128]{1,0:T(8,128)(2,1)}, bf16[256,128]{1,0:T(8,128)(2,1)}) custom-call(s32[1,1,8,2]{3,2,1,0:T(8,128)} %copy.10.refs_0_, s32[1,1,8]{2,1,0:T(1,128)} %refs_1_.1, bf16[1,1,8,2,128,128]{5,4,3,2,1,0:T(8,128)(2,1)} %refs_2_.1, bf16[256,128]{1,0:T(8,128)(2,1)} %copy-done.3, ...), custom_call_target="tpu_custom_call" | custom-call | tf_op jit(solution)/shard_map/pallas_call | solution.py:36
  19.0 1.5 %collective-permute-start.8 = (bf16[256,128]{1,0:T(8,128)(2,1)}, bf16[256,128]{1,0:T(8,128)(2,1)S(1)}, u32[]{:S(2)}, u32[]{:S(2)}) collective-permute-start(bf16[256,128]{1,0:T(8,128)(2,1)} %get-tuple-element.11), channel_id=1, source_target_pairs={{0,8},{8,0},{16,24},{24,16},{1,9},{9,1},{17,25},{25,17},{2,10},{10... | collective-permute-start | bytes 196616 | tf_op jit(solution)/shard_map/ppermute | solution.py:131
  20.4 1.5 %collective-permute-start.9 = (bf16[256,128]{1,0:T(8,128)(2,1)}, bf16[256,128]{1,0:T(8,128)(2,1)S(1)}, u32[]{:S(2)}, u32[]{:S(2)}) collective-permute-start(bf16[256,128]{1,0:T(8,128)(2,1)} %get-tuple-element.12), channel_id=1, source_target_pairs={{0,16},{8,24},{16,0},{24,8},{1,17},{9,25},{17,1},{25,9},{2,18},{10... | collective-permute-start | bytes 196616 | tf_op jit(solution)/shard_map/ppermute | solution.py:131
  22.0 0.5 %collective-permute-start.10 = (bf16[256,128]{1,0:T(8,128)(2,1)}, bf16[256,128]{1,0:T(8,128)(2,1)S(1)}, u32[]{:S(2)}, u32[]{:S(2)}) collective-permute-start(bf16[256,128]{1,0:T(8,128)(2,1)} %get-tuple-element.13), channel_id=1, source_target_pairs={{0,24},{8,16},{16,8},{24,0},{1,25},{9,17},{17,9},{25,1},{2,26},{10... | collective-permute-start | bytes 196616 | tf_op jit(solution)/shard_map/ppermute | solution.py:131
  22.4 1.0 %collective-permute-done.8.refs_1_ = bf16[256,128]{1,0:T(8,128)(2,1)S(1)} collective-permute-done((bf16[256,128]{1,0:T(8,128)(2,1)}, bf16[256,128]{1,0:T(8,128)(2,1)S(1)}, u32[]{:S(2)}, u32[]{:S(2)}) %collective-permute-start.8) | collective-permute-done | bytes 65568 | tf_op jit(solution)/shard_map/ppermute | solution.py:131
  23.4 1.5 %collective-permute-done.9.refs_2_ = bf16[256,128]{1,0:T(8,128)(2,1)S(1)} collective-permute-done((bf16[256,128]{1,0:T(8,128)(2,1)}, bf16[256,128]{1,0:T(8,128)(2,1)S(1)}, u32[]{:S(2)}, u32[]{:S(2)}) %collective-permute-start.9) | collective-permute-done | bytes 65568 | tf_op jit(solution)/shard_map/ppermute | solution.py:131
  24.9 2.4 %collective-permute-done.10.refs_3_ = bf16[256,128]{1,0:T(8,128)(2,1)S(1)} collective-permute-done((bf16[256,128]{1,0:T(8,128)(2,1)}, bf16[256,128]{1,0:T(8,128)(2,1)S(1)}, u32[]{:S(2)}, u32[]{:S(2)}) %collective-permute-start.10) | collective-permute-done | bytes 65568 | tf_op jit(solution)/shard_map/ppermute | solution.py:131
  27.3 0.8 %add_add_fusion = f32[128,128]{1,0:T(8,128)S(1)} fusion(bf16[256,128]{1,0:T(8,128)(2,1)S(1)} %collective-permute-done.10.refs_3_, bf16[256,128]{1,0:T(8,128)(2,1)S(1)} %collective-permute-done.9.refs_2_, bf16[256,128]{1,0:T(8,128)(2,1)S(1)} %collective-permute-done.8.refs_1_, bf16[256,128]{1,0:T(8,128)(2,1)} %get-tuple-element.10.refs_0_), kind=kLoop, calls=%fused_computation.2 | loop fusion | flops 114688 | bytes 196608 | tf_op jit(solution)/shard_map/add | solution.py:100
  28.2 1.2 %collective-permute-done.11 = f32[128,128]{1,0:T(8,128)S(1)} collective-permute-done((f32[128,128]{1,0:T(8,128)S(1)}, f32[128,128]{1,0:T(8,128)S(1)}, u32[]{:S(2)}, u32[]{:S(2)}) %collective-permute-start.11) | collective-permute-done | bytes 65568 | tf_op jit(solution)/shard_map/ppermute | solution.py:128
  29.5 1.2 %collective-permute-start.14 = (bf16[128,128]{1,0:T(8,128)(2,1)S(1)}, bf16[128,128]{1,0:T(8,128)(2,1)S(1)}, u32[]{:S(2)}, u32[]{:S(2)}) collective-permute-start(bf16[128,128]{1,0:T(8,128)(2,1)S(1)} %add_convert_fusion), channel_id=1, source_target_pairs={{0,6},{1,7},{2,4},{3,5},{4,2},{5,3},{6,0},{7,1},{8,14},{9,15},{10,... | collective-permute-start | bytes 98312 | tf_op jit(solution)/shard_map/ppermute | solution.py:135
  30.7 0.5 %collective-permute-start.13 = (bf16[128,128]{1,0:T(8,128)(2,1)S(1)}, bf16[128,128]{1,0:T(8,128)(2,1)S(1)}, u32[]{:S(2)}, u32[]{:S(2)}) collective-permute-start(bf16[128,128]{1,0:T(8,128)(2,1)S(1)} %add_convert_fusion), channel_id=1, source_target_pairs={{0,4},{1,5},{2,6},{3,7},{4,0},{5,1},{6,2},{7,3},{8,12},{9,13},{10,... | collective-permute-start | bytes 98312 | tf_op jit(solution)/shard_map/ppermute | solution.py:135
  31.1 2.8 %collective-permute-start.12 = (bf16[128,128]{1,0:T(8,128)(2,1)S(1)}, bf16[128,128]{1,0:T(8,128)(2,1)S(1)}, u32[]{:S(2)}, u32[]{:S(2)}) collective-permute-start(bf16[128,128]{1,0:T(8,128)(2,1)S(1)} %add_convert_fusion), channel_id=1, source_target_pairs={{0,2},{1,3},{2,0},{3,1},{4,6},{5,7},{6,4},{7,5},{8,10},{9,11},{10,... | collective-permute-start | bytes 98312 | tf_op jit(solution)/shard_map/ppermute | solution.py:135
  33.9 1.9 %shard_map.97 = bf16[128,128]{1,0:T(8,128)(2,1)} custom-call(s32[1,128]{1,0:T(1,128)} %bitcast.2, bf16[128,128]{1,0:T(8,128)(2,1)} %weight_ref.1, bf16[256,128]{1,0:T(8,128)(2,1)} %get-tuple-element.10.refs_0_, bf16[256,128]{1,0:T(8,128)(2,1)} %copy-done, bf16[256,128]{1,0:T(8,128)(2,1)} %copy-done.1, bf16[256,128]{1,0:T(8,128)(2,1)} %copy-done.2), custom_call_target="tpu_custom_call" | custom-call | tf_op jit(solution)/shard_map/pallas_call | solution.py:36
  36.1 0.7 %add_multiply_fusion = f32[128,128]{1,0:T(8,128)} fusion(bf16[128,128]{1,0:T(8,128)(2,1)S(1)} %collective-permute-done.14, bf16[128,128]{1,0:T(8,128)(2,1)S(1)} %collective-permute-done.13, bf16[128,128]{1,0:T(8,128)(2,1)S(1)} %collective-permute-done.12, bf16[128,128]{1,0:T(8,128)(2,1)S(1)} %add_convert_fusion), kind=kLoop, calls=%fused_computation | loop fusion | flops 131072 | bytes 196608 | tf_op jit(solution)/shard_map/mul | solution.py:165
  (39 shorter events, 1.4 us)
Async XLA Ops:
  2.3 1.5 %collective-permute-start = (bf16[128,128]{1,0:T(8,128)(2,1)}, bf16[128,128]{1,0:T(8,128)(2,1)S(1)}, u32[]{:S(2)}, u32[]{:S(2)}) collective-permute-start(bf16[128,128]{1,0:T(8,128)(2,1)} %get-tuple-element.9), channel_id=1, source_target_pairs={{0,1},{1,0},{2,3},{3,2},{4,5},{5,4},{6,7},{7,6},{8,9},{9,8},{10,11... | collective-permute-start | bytes 98312 | tf_op jit(solution)/shard_map/ppermute | solution.py:128
  3.5 11.0 %copy-start.11 = (s32[1,1,8,2]{2,3,1,0:T(2,128)S(1)}, s32[1,1,8,2]{2,3,1,0:T(2,128)}, u32[]{:S(2)}) copy-start(s32[1,1,8,2]{2,3,1,0:T(2,128)} %param.13) | copy-start | bytes 196
  3.8 11.6 %copy-start.3 = (bf16[256,128]{1,0:T(8,128)(2,1)}, bf16[256,128]{1,0:T(8,128)(2,1)S(1)}, u32[]{:S(2)}) copy-start(bf16[256,128]{1,0:T(8,128)(2,1)S(1)} %constant_dynamic-update-slice_fusion.refs_3_) | copy-start | bytes 196612
  3.8 7.4 %collective-permute-start.3 = (bf16[256,128]{1,0:T(8,128)(2,1)S(1)}, bf16[256,128]{1,0:T(8,128)(2,1)S(1)}, u32[]{:S(2)}, u32[]{:S(2)}) collective-permute-start(bf16[256,128]{1,0:T(8,128)(2,1)S(1)} %constant_dynamic-update-slice_fusion.refs_3_), channel_id=1, source_target_pairs={{0,6},{1,25},{2,4},{3,27},{4,2},{5,29},{6,0},{7,31},{8,14},{9,17},... | collective-permute-start | bytes 196616 | tf_op jit(solution)/shard_map/ppermute | solution.py:145
  8.8 5.2 %collective-permute-start.2 = (bf16[256,128]{1,0:T(8,128)(2,1)S(1)}, bf16[256,128]{1,0:T(8,128)(2,1)S(1)}, u32[]{:S(2)}, u32[]{:S(2)}) collective-permute-start(bf16[256,128]{1,0:T(8,128)(2,1)S(1)} %constant_dynamic-update-slice_fusion.refs_3_), channel_id=1, source_target_pairs={{0,4},{1,17},{2,6},{3,19},{4,0},{5,21},{6,2},{7,23},{8,12},{9,25},... | collective-permute-start | bytes 196616 | tf_op jit(solution)/shard_map/ppermute | solution.py:145
  8.8 5.2 %collective-permute-start.1 = (bf16[256,128]{1,0:T(8,128)(2,1)S(1)}, bf16[256,128]{1,0:T(8,128)(2,1)S(1)}, u32[]{:S(2)}, u32[]{:S(2)}) collective-permute-start(bf16[256,128]{1,0:T(8,128)(2,1)S(1)} %constant_dynamic-update-slice_fusion.refs_3_), channel_id=1, source_target_pairs={{0,2},{1,9},{2,0},{3,11},{4,6},{5,13},{6,4},{7,15},{8,10},{9,1},{1... | collective-permute-start | bytes 196616 | tf_op jit(solution)/shard_map/ppermute | solution.py:145
  9.4 5.7 %collective-permute-start.4 = (bf16[256,128]{1,0:T(8,128)(2,1)S(1)}, bf16[256,128]{1,0:T(8,128)(2,1)S(1)}, u32[]{:S(2)}, u32[]{:S(2)}) collective-permute-start(bf16[256,128]{1,0:T(8,128)(2,1)S(1)} %constant_dynamic-update-slice_fusion.refs_3_), channel_id=1, source_target_pairs={{0,1},{1,0},{2,3},{3,2},{4,5},{5,4},{6,7},{7,6},{8,9},{9,8},{10,11... | collective-permute-start | bytes 196616 | tf_op jit(solution)/shard_map/ppermute | solution.py:128
  11.1 4.2 %copy-start.4 = (bf16[256,128]{1,0:T(8,128)(2,1)}, bf16[256,128]{1,0:T(8,128)(2,1)S(1)}, u32[]{:S(2)}) copy-start(bf16[256,128]{1,0:T(8,128)(2,1)S(1)} %collective-permute-done.3.refs_6_) | copy-start | bytes 196612
  11.2 4.0 %collective-permute-start.7 = (bf16[256,128]{1,0:T(8,128)(2,1)S(1)}, bf16[256,128]{1,0:T(8,128)(2,1)S(1)}, u32[]{:S(2)}, u32[]{:S(2)}) collective-permute-start(bf16[256,128]{1,0:T(8,128)(2,1)S(1)} %collective-permute-done.3.refs_6_), channel_id=1, source_target_pairs={{0,1},{1,0},{2,3},{3,2},{4,5},{5,4},{6,7},{7,6},{8,9},{9,8},{10,11... | collective-permute-start | bytes 196616 | tf_op jit(solution)/shard_map/ppermute | solution.py:128
  14.0 1.4 %copy-start.5 = (bf16[256,128]{1,0:T(8,128)(2,1)}, bf16[256,128]{1,0:T(8,128)(2,1)S(1)}, u32[]{:S(2)}) copy-start(bf16[256,128]{1,0:T(8,128)(2,1)S(1)} %collective-permute-done.2.refs_5_) | copy-start | bytes 196612
  14.0 1.3 %collective-permute-start.6 = (bf16[256,128]{1,0:T(8,128)(2,1)S(1)}, bf16[256,128]{1,0:T(8,128)(2,1)S(1)}, u32[]{:S(2)}, u32[]{:S(2)}) collective-permute-start(bf16[256,128]{1,0:T(8,128)(2,1)S(1)} %collective-permute-done.2.refs_5_), channel_id=1, source_target_pairs={{0,1},{1,0},{2,3},{3,2},{4,5},{5,4},{6,7},{7,6},{8,9},{9,8},{10,11... | collective-permute-start | bytes 196616 | tf_op jit(solution)/shard_map/ppermute | solution.py:128
  14.0 1.4 %copy-start.6 = (bf16[256,128]{1,0:T(8,128)(2,1)}, bf16[256,128]{1,0:T(8,128)(2,1)S(1)}, u32[]{:S(2)}) copy-start(bf16[256,128]{1,0:T(8,128)(2,1)S(1)} %collective-permute-done.1.refs_4_) | copy-start | bytes 196612
  14.0 1.4 %collective-permute-start.5 = (bf16[256,128]{1,0:T(8,128)(2,1)S(1)}, bf16[256,128]{1,0:T(8,128)(2,1)S(1)}, u32[]{:S(2)}, u32[]{:S(2)}) collective-permute-start(bf16[256,128]{1,0:T(8,128)(2,1)S(1)} %collective-permute-done.1.refs_4_), channel_id=1, source_target_pairs={{0,1},{1,0},{2,3},{3,2},{4,5},{5,4},{6,7},{7,6},{8,9},{9,8},{10,11... | collective-permute-start | bytes 196616 | tf_op jit(solution)/shard_map/ppermute | solution.py:128
  15.2 0.7 %copy-start.8 = (bf16[256,128]{1,0:T(8,128)(2,1)}, bf16[256,128]{1,0:T(8,128)(2,1)S(1)}, u32[]{:S(2)}) copy-start(bf16[256,128]{1,0:T(8,128)(2,1)S(1)} %collective-permute-done.7.refs_10_) | copy-start | bytes 196612
  19.0 4.5 %collective-permute-start.8 = (bf16[256,128]{1,0:T(8,128)(2,1)}, bf16[256,128]{1,0:T(8,128)(2,1)S(1)}, u32[]{:S(2)}, u32[]{:S(2)}) collective-permute-start(bf16[256,128]{1,0:T(8,128)(2,1)} %get-tuple-element.11), channel_id=1, source_target_pairs={{0,8},{8,0},{16,24},{24,16},{1,9},{9,1},{17,25},{25,17},{2,10},{10... | collective-permute-start | bytes 196616 | tf_op jit(solution)/shard_map/ppermute | solution.py:131
  20.4 4.5 %collective-permute-start.9 = (bf16[256,128]{1,0:T(8,128)(2,1)}, bf16[256,128]{1,0:T(8,128)(2,1)S(1)}, u32[]{:S(2)}, u32[]{:S(2)}) collective-permute-start(bf16[256,128]{1,0:T(8,128)(2,1)} %get-tuple-element.12), channel_id=1, source_target_pairs={{0,16},{8,24},{16,0},{24,8},{1,17},{9,25},{17,1},{25,9},{2,18},{10... | collective-permute-start | bytes 196616 | tf_op jit(solution)/shard_map/ppermute | solution.py:131
  22.0 5.4 %collective-permute-start.10 = (bf16[256,128]{1,0:T(8,128)(2,1)}, bf16[256,128]{1,0:T(8,128)(2,1)S(1)}, u32[]{:S(2)}, u32[]{:S(2)}) collective-permute-start(bf16[256,128]{1,0:T(8,128)(2,1)} %get-tuple-element.13), channel_id=1, source_target_pairs={{0,24},{8,16},{16,8},{24,0},{1,25},{9,17},{17,9},{25,1},{2,26},{10... | collective-permute-start | bytes 196616 | tf_op jit(solution)/shard_map/ppermute | solution.py:131
  23.4 4.7 %copy-start = (bf16[256,128]{1,0:T(8,128)(2,1)}, bf16[256,128]{1,0:T(8,128)(2,1)S(1)}, u32[]{:S(2)}) copy-start(bf16[256,128]{1,0:T(8,128)(2,1)S(1)} %collective-permute-done.8.refs_1_) | copy-start | bytes 196612
  24.9 3.2 %copy-start.1 = (bf16[256,128]{1,0:T(8,128)(2,1)}, bf16[256,128]{1,0:T(8,128)(2,1)S(1)}, u32[]{:S(2)}) copy-start(bf16[256,128]{1,0:T(8,128)(2,1)S(1)} %collective-permute-done.9.refs_2_) | copy-start | bytes 196612
  27.3 0.8 %copy-start.2 = (bf16[256,128]{1,0:T(8,128)(2,1)}, bf16[256,128]{1,0:T(8,128)(2,1)S(1)}, u32[]{:S(2)}) copy-start(bf16[256,128]{1,0:T(8,128)(2,1)S(1)} %collective-permute-done.10.refs_3_) | copy-start | bytes 196612
  28.2 1.3 %collective-permute-start.11 = (f32[128,128]{1,0:T(8,128)S(1)}, f32[128,128]{1,0:T(8,128)S(1)}, u32[]{:S(2)}, u32[]{:S(2)}) collective-permute-start(f32[128,128]{1,0:T(8,128)S(1)} %add_add_fusion), channel_id=1, source_target_pairs={{0,1},{1,0},{2,3},{3,2},{4,5},{5,4},{6,7},{7,6},{8,9},{9,8},{10,11... | collective-permute-start | bytes 196616 | tf_op jit(solution)/shard_map/ppermute | solution.py:128
  29.5 6.3 %collective-permute-start.14 = (bf16[128,128]{1,0:T(8,128)(2,1)S(1)}, bf16[128,128]{1,0:T(8,128)(2,1)S(1)}, u32[]{:S(2)}, u32[]{:S(2)}) collective-permute-start(bf16[128,128]{1,0:T(8,128)(2,1)S(1)} %add_convert_fusion), channel_id=1, source_target_pairs={{0,6},{1,7},{2,4},{3,5},{4,2},{5,3},{6,0},{7,1},{8,14},{9,15},{10,... | collective-permute-start | bytes 98312 | tf_op jit(solution)/shard_map/ppermute | solution.py:135
  30.7 5.5 %collective-permute-start.13 = (bf16[128,128]{1,0:T(8,128)(2,1)S(1)}, bf16[128,128]{1,0:T(8,128)(2,1)S(1)}, u32[]{:S(2)}, u32[]{:S(2)}) collective-permute-start(bf16[128,128]{1,0:T(8,128)(2,1)S(1)} %add_convert_fusion), channel_id=1, source_target_pairs={{0,4},{1,5},{2,6},{3,7},{4,0},{5,1},{6,2},{7,3},{8,12},{9,13},{10,... | collective-permute-start | bytes 98312 | tf_op jit(solution)/shard_map/ppermute | solution.py:135
  31.1 5.0 %collective-permute-start.12 = (bf16[128,128]{1,0:T(8,128)(2,1)S(1)}, bf16[128,128]{1,0:T(8,128)(2,1)S(1)}, u32[]{:S(2)}, u32[]{:S(2)}) collective-permute-start(bf16[128,128]{1,0:T(8,128)(2,1)S(1)} %add_convert_fusion), channel_id=1, source_target_pairs={{0,2},{1,3},{2,0},{3,1},{4,6},{5,7},{6,4},{7,5},{8,10},{9,11},{10,... | collective-permute-start | bytes 98312 | tf_op jit(solution)/shard_map/ppermute | solution.py:135
  (3 other events, 1.9 us)

commit v2 on v1

v2 whole, which is shorter than its diff:
```python
import functools

import jax
import jax.numpy as jnp
from jax import lax
from jax.experimental import pallas as pl
from jax.experimental.pallas import tpu as pltpu
from jax.sharding import PartitionSpec as P

F = 128
B = 128
K = 2
BF = jnp.bfloat16
F32 = jnp.float32


def swaps(size):
    return size & (size - 1) == 0


def target_of(index, step, size):
    return index ^ step if swaps(size) else (index + step) % size


def source_of(index, step, size):
    return index ^ step if swaps(size) else lax.rem(index + (size - step), size)


def dot(a, b, contract):
    return lax.dot_general(a, b, (contract, ((), ())), preferred_element_type=F32)


def call(body, outs, args, spaces, out_spaces=None, scratch=(), limit=4 << 20):
    return pl.pallas_call(
        body,
        out_shape=outs,
        in_specs=[pl.BlockSpec(memory_space=space) for space in spaces],
        out_specs=[pl.BlockSpec(memory_space=pltpu.VMEM)] * len(outs),
        scratch_shapes=list(scratch),
        compiler_params=pltpu.CompilerParams(vmem_limit_bytes=limit),
    )(*args)


def spread(order_row):
    n = order_row.shape[1]
    return (lax.broadcasted_iota(jnp.int32, (n, n), 0) == order_row).astype(BF)


def first_kernel(order_ref, keep_ref, give_ref, keep_out, give_out):
    place = spread(order_ref[...])
    keep_out[...] = dot(place, keep_ref[...], ((0,), (0,))).astype(BF)
    give_out[...] = dot(place, give_ref[...], ((0,), (0,))).astype(BF)


def row_steps(rows):
    return list(zip([1, 2, *range(3, rows)], [2, 1, *range(3, rows)]))


def product_kernel(rows, depth, *refs):
    steps = max(rows, depth)
    cols_ref, blocks_ref = refs[:2]
    own, other = refs[2 : 2 + steps], refs[2 + steps : 2 + 2 * steps]
    term_ref, weight_ref = refs[2 + 2 * steps : 4 + 2 * steps]
    outs = refs[4 + 2 * steps : -1]
    total = refs[-1]
    r = lax.axis_index("row")
    c = lax.axis_index("col")
    z, even = lax.div(c, 2), lax.rem(c, 2) == 0
    total[...] = jnp.zeros_like(total)
    for step in range(depth):
        pair = jnp.where(even, own[step][...], other[step][...])
        chip = source_of(z, step, depth)
        for core in range(2):
            i = 2 * chip + core
            panel = pair[core * B : (core + 1) * B]
            for k in range(K):
                total[cols_ref[k, i]] += dot(blocks_ref[i, k], panel, ((0,), (0,)))
    terms = [total[source_of(r, step, rows)].astype(BF) for step in range(rows)]
    weight = jnp.zeros((F, F), F32)
    for step in range(rows):
        feat = jnp.where(even, other[step][B : 2 * B], own[step][0:B])
        weight += dot(feat, terms[step], ((0,), (0,)))
    term_ref[...] = terms[0]
    weight_ref[...] = weight
    sent = terms if swaps(rows) else [terms[-step] for step in range(rows)]
    for out, (first, second) in zip(outs, row_steps(rows)):
        out[0:B] = jnp.where(even, sent[first], sent[second])


def sum_in_order(values, index, size):
    values = [v.astype(F32) for v in values]
    if swaps(size):
        while len(values) > 1:
            values = [a + b for a, b in zip(values[0::2], values[1::2])]
        return values[0]
    places = jnp.stack([source_of(index, step, size) for step in range(size)])
    held = jnp.zeros((size,) + values[0].shape, F32).at[places].set(jnp.stack(values))
    return functools.reduce(lambda a, b: a + b, [held[i] for i in range(size)])


def feature_kernel(count, order_ref, weight_ref, *refs):
    terms, out_ref = refs[:count], refs[count]
    total = terms[0][0:B].astype(F32)
    for term in terms[1:]:
        total += term[0:B].astype(F32)
    grad = dot(total.astype(BF), weight_ref[...], ((1,), (1,))).astype(BF)
    out_ref[...] = dot(spread(order_ref[...]), grad, ((1,), (0,))).astype(BF)


def shards(grad_out, pre_act, features, weight, blocks, block_cols, block_counts, order):
    slab_rows = grad_out.shape[0]
    rows = lax.axis_size("row")
    cols = lax.axis_size("col")
    depth = cols // 2
    axes = ("row", "col")
    r, c = lax.axis_index("row"), lax.axis_index("col")
    z, even = lax.div(c, 2), lax.rem(c, 2) == 0
    order_row = order.reshape(1, slab_rows)
    slab = jax.ShapeDtypeStruct((B, F), BF)
    pair = jax.ShapeDtypeStruct((2 * B, F), BF)
    limit = (4 << 20) + 8 * blocks.size

    def across(value):
        return lax.ppermute(value, "col", [(i, i ^ 1) for i in range(cols)])

    def move(value, row_of, depth_of):
        pairs = []
        for i in range(rows):
            for j in range(depth):
                for core in range(2):
                    a, b = row_of(i, core), depth_of(j, core)
                    if a is not None and b is not None:
                        pairs.append((i * cols + 2 * j + core, a * cols + 2 * b + core))
        return lax.ppermute(value, axes, pairs)

    def along_row(value, steps):
        return move(value, lambda i, core: target_of(i, steps[core], rows), lambda j, core: j)

    def along_depth(value, steps):
        return move(value, lambda i, core: i, lambda j, core: target_of(j, steps[core], depth))

    def both(value, step):
        return move(
            value,
            lambda i, core: i if core == 0 else target_of(i, step, rows) if step < rows else None,
            lambda j, core: j if core == 1 else target_of(j, step, depth) if step < depth else None,
        )

    masked = jnp.where(pre_act > 0, grad_out, jnp.zeros_like(grad_out))
    keep, give = jnp.where(even, masked, features), jnp.where(even, features, masked)
    keep, give = call(first_kernel, [slab, slab], (order_row, keep, give), [pltpu.VMEM] * 3)
    filled = jnp.arange(K, dtype=jnp.int32)[None, :] < block_counts[0, 0][:, None]
    blocks = jnp.where(filled[:, :, None, None], blocks[0, 0], jnp.zeros((), BF))
    message = jnp.concatenate([keep, across(give)], axis=0)
    steps = max(rows, depth)
    own = [message] + [both(message, step) for step in reversed(range(1, steps))][::-1]
    other = [across(value) for value in own]
    term, weight_term, *messages = call(
        functools.partial(product_kernel, rows, depth),
        [slab, jax.ShapeDtypeStruct((F, F), F32), slab] + [pair] * (rows - 2),
        (block_cols[0, 0].T, blocks, *own, *other),
        [pltpu.SMEM] + [pltpu.VMEM] * (1 + 2 * steps),
        scratch=[pltpu.VMEM((rows, B, F), F32)],
        limit=limit,
    )
    chip_weight = (weight_term + across(weight_term)).astype(BF)
    plan = row_steps(rows)
    terms = [along_row(messages[0], plan[0])]
    terms += [along_row(m.at[B:].set(chip_weight), plan[i + 1]) for i, m in enumerate(messages[1:])]
    (grad_feat,) = call(
        functools.partial(feature_kernel, rows), [slab], (order_row, weight, term, *terms), [pltpu.VMEM] * (2 + rows)
    )
    terms = list(lax.optimization_barrier(tuple(terms)))
    mine = terms[1][B:]
    swapped = across(mine)
    weights = [chip_weight, jnp.where(even, swapped, mine), jnp.where(even, mine, swapped)] + [t[B:] for t in terms[2:]]
    row_weight = sum_in_order(weights, r, rows).astype(BF)
    mine = along_depth(row_weight, (1, 2))
    rest = [along_depth(row_weight, (step, step)) for step in range(3, depth)]
    swapped = across(mine)
    weights = [row_weight, jnp.where(even, mine, swapped), jnp.where(even, swapped, mine)] + rest
    summed = sum_in_order(weights, z, depth)
    return grad_feat, summed * (slab_rows * rows * cols) ** (-0.5)


def solution(mesh):
    placed = (
        P(("row", "col"), None),
        P(("row", "col"), None),
        P(("row", "col"), None),
        P(),
        P("row", "col", None, None, None, None),
        P("row", "col", None, None),
        P("row", "col", None),
        P(("row", "col")),
    )
    return jax.shard_map(
        shards,
        mesh=mesh,
        in_specs=placed,
        out_specs=(P(("row", "col"), None), P()),
        check_vma=False,
    )
```

time: 37.2 us -> 33.8 us (0.909)
  Pallas kernels: 5.98 us -> 2.21 us
  waiting for transfers between devices: 11.5 us -> 12.9 us
  other arithmetic: 1.44 us -> 2.72 us
  local copies, waits for them, and re-layouts: 2.56 us -> 1.32 us
  starting transfers between devices: 14.6 us -> 13.6 us
    pallas_call x3, Pallas kernels: 5.98 us -> 2.21 us  [call(): pl.pallas_call(body, out_shape=outs, in_specs=[pl.BlockSpec(memory_space=...]
    select_n x0 -> x2, other arithmetic: none -> 1.94 us  [the longest x1 1.14 us: shards(): jnp.where(filled[:, :, None, None], blocks[0, 0], jnp.zeros((), BF))]
    ppermute x6 -> x8, waiting for transfers between devices: 1.76 us -> 3.3 us  [across(): return lax.ppermute(value, 'col', [(i, i ^ 1) for i in range(cols)])]
    unnamed x26 -> x9, local copies, waits for them, and re-layouts: 2.55 us -> 1.29 us
    ppermute x9 -> x8, starting transfers between devices: 13.6 us -> 12.4 us  [move(): return lax.ppermute(value, axes, pairs)]
    add x1 -> x0, other arithmetic: 0.78 us -> none  [sum_in_order(): values = [a + b for a, b in zip(values[0::2], values[1::2])]]
    ppermute x6 -> x8, starting transfers between devices: 1.03 us -> 1.18 us  [across(): return lax.ppermute(value, 'col', [(i, i ^ 1) for i in range(cols)])]
    ppermute x9 -> x8, waiting for transfers between devices: 9.72 us -> 9.63 us  [move(): return lax.ppermute(value, axes, pairs)]
  transfers between devices with their start and end apart: 15 -> 16, of which waited for: 9 -> 8; matrix products, arithmetic and copies ran while one was open for 4% -> 4% of each run, Pallas kernels for 5% -> 3%
where the time goes in v2:
time: 33.8 us; the launch traced here: 33.5 us
  starting transfers between devices  13.6 us (40%)
  waiting for transfers between devices  12.9 us (38%)
  other arithmetic  2.72 us (8%)
  Pallas kernels  2.21 us (7%)
  local copies, waits for them, and re-layouts  1.32 us (4%)
  between operations  0.76 us (2%)
    ppermute x8, starting transfers between devices, move(): return lax.ppermute(value, axes, pairs)  12.4 us
    ppermute x8, waiting for transfers between devices, move(): return lax.ppermute(value, axes, pairs)  9.63 us
    ppermute x8, waiting for transfers between devices, across(): return lax.ppermute(value, 'col', [(i, i ^ 1) for i in range(cols)])  3.3 us
    pallas_call x3, Pallas kernels, call(): pl.pallas_call(body, out_shape=outs, in_specs=[pl.BlockSpec(memory_space=...  2.21 us
    unnamed x9, local copies, waits for them, and re-layouts  1.29 us
    ppermute x8, starting transfers between devices, across(): return lax.ppermute(value, 'col', [(i, i ^ 1) for i in range(cols)])  1.18 us
    select_n x1, other arithmetic, shards(): jnp.where(filled[:, :, None, None], blocks[0, 0], jnp.zeros((), BF))  1.14 us
    select_n x1, other arithmetic, shards(): jnp.where(even, features, masked)  0.8 us
  transfers between devices with their start and end apart: 16, of which 8 were waited for; matrix products, arithmetic and copies ran while one was open for 4% of the time, Pallas kernels for 3%

profile of v2, /device:TPU:0, one launch (start us, length us, event | category | flops | bytes accessed | tf_op | source)
XLA Modules:
  0.0 33.5 jit_solution(12686663636761584043)
XLA Ops:
  0.6 0.8 %broadcast_select_fusion = (bf16[128,128]{1,0:T(8,128)(2,1)S(1)}, bf16[128,128]{1,0:T(8,128)(2,1)S(1)}) fusion(bf16[128,128]{1,0:T(8,128)(2,1)} %param.14, pred[]{:T(512)S(6)} %eq.3, bf16[128,128]{1,0:T(8,128)(2,1)} %param.12, bf16[128,128]{1,0:T(8,128)(2,1)} %param.13), kind=kLoop, calls=%fused_computation.5 | loop fusion | flops 65536 | bytes 163841 | tf_op jit(solution)/shard_map/jit(_where)/select_n | solution.py:150
  1.4 0.6 %copy-done.1 = s32[128]{0:T(128)S(1)} copy-done((s32[128]{0:T(128)S(1)}, s32[128]{0:T(128)}, u32[]{:S(2)}) %copy-start.1) | copy-done | bytes 536
  2.3 0.5 %collective-permute-start = (bf16[128,128]{1,0:T(8,128)(2,1)S(1)}, bf16[128,128]{1,0:T(8,128)(2,1)S(1)}, u32[]{:S(2)}, u32[]{:S(2)}) collective-permute-start(bf16[128,128]{1,0:T(8,128)(2,1)S(1)} %get-tuple-element.36), channel_id=1, source_target_pairs={{0,1},{1,0},{2,3},{3,2},{4,5},{5,4},{6,7},{7,6},{8,9},{9,8},{10,11... | collective-permute-start | bytes 98312 | tf_op jit(solution)/shard_map/ppermute | solution.py:124
  2.8 0.9 %collective-permute-done = bf16[128,128]{1,0:T(8,128)(2,1)S(1)} collective-permute-done((bf16[128,128]{1,0:T(8,128)(2,1)S(1)}, bf16[128,128]{1,0:T(8,128)(2,1)S(1)}, u32[]{:S(2)}, u32[]{:S(2)}) %collective-permute-start) | collective-permute-done | bytes 32800 | tf_op jit(solution)/shard_map/ppermute | solution.py:124
  3.7 5.0 %collective-permute-start.3 = (bf16[256,128]{1,0:T(8,128)(2,1)S(1)}, bf16[256,128]{1,0:T(8,128)(2,1)S(1)}, u32[]{:S(2)}, u32[]{:S(2)}) collective-permute-start(bf16[256,128]{1,0:T(8,128)(2,1)S(1)} %constant_dynamic-update-slice_fusion.refs_2_), channel_id=1, source_target_pairs={{0,6},{1,25},{2,4},{3,27},{4,2},{5,29},{6,0},{7,31},{8,14},{9,17},... | collective-permute-start | bytes 196616 | tf_op jit(solution)/shard_map/ppermute | solution.py:134
  8.7 0.6 %collective-permute-start.1 = (bf16[256,128]{1,0:T(8,128)(2,1)S(1)}, bf16[256,128]{1,0:T(8,128)(2,1)S(1)}, u32[]{:S(2)}, u32[]{:S(2)}) collective-permute-start(bf16[256,128]{1,0:T(8,128)(2,1)S(1)} %constant_dynamic-update-slice_fusion.refs_2_), channel_id=1, source_target_pairs={{0,2},{1,9},{2,0},{3,11},{4,6},{5,13},{6,4},{7,15},{8,10},{9,1},{1... | collective-permute-start | bytes 196616 | tf_op jit(solution)/shard_map/ppermute | solution.py:134
  9.4 1.6 %collective-permute-done.3.refs_5_ = bf16[256,128]{1,0:T(8,128)(2,1)S(1)} collective-permute-done((bf16[256,128]{1,0:T(8,128)(2,1)S(1)}, bf16[256,128]{1,0:T(8,128)(2,1)S(1)}, u32[]{:S(2)}, u32[]{:S(2)}) %collective-permute-start.3) | collective-permute-done | bytes 65568 | tf_op jit(solution)/shard_map/ppermute | solution.py:134
  11.0 2.8 %collective-permute-done.2.refs_4_ = bf16[256,128]{1,0:T(8,128)(2,1)S(1)} collective-permute-done((bf16[256,128]{1,0:T(8,128)(2,1)S(1)}, bf16[256,128]{1,0:T(8,128)(2,1)S(1)}, u32[]{:S(2)}, u32[]{:S(2)}) %collective-permute-start.2) | collective-permute-done | bytes 65568 | tf_op jit(solution)/shard_map/ppermute | solution.py:134
  13.9 0.5 %collective-permute-start.5 = (bf16[256,128]{1,0:T(8,128)(2,1)S(1)}, bf16[256,128]{1,0:T(8,128)(2,1)S(1)}, u32[]{:S(2)}, u32[]{:S(2)}) collective-permute-start(bf16[256,128]{1,0:T(8,128)(2,1)S(1)} %collective-permute-done.1.refs_3_), channel_id=1, source_target_pairs={{0,1},{1,0},{2,3},{3,2},{4,5},{5,4},{6,7},{7,6},{8,9},{9,8},{10,11... | collective-permute-start | bytes 196616 | tf_op jit(solution)/shard_map/ppermute | solution.py:124
  14.4 1.1 %bitcast_select_fusion.refs_1_ = bf16[8,2,128,128]{3,2,1,0:T(8,128)(2,1)S(1)} fusion(bf16[1,1,8,2,128,128]{5,4,3,2,1,0:T(8,128)(2,1)} %param.16, pred[8,2]{1,0:T(8,128)(4,1)S(1)} %iota_compare_fusion), kind=kLoop, calls=%fused_computation | loop fusion | flops 262144 | bytes 1048592 | tf_op jit(solution)/shard_map/jit(_where)/select_n | solution.py:153
  15.6 0.6 %copy-done.2 = s32[1,1,8,2]{2,3,1,0:T(2,128)S(1)} copy-done((s32[1,1,8,2]{2,3,1,0:T(2,128)S(1)}, s32[1,1,8,2]{2,3,1,0:T(2,128)}, u32[]{:S(2)}) %copy-start.2) | copy-done | bytes 88
  16.2 1.1 %shard_map.96 = (bf16[128,128]{1,0:T(8,128)(2,1)S(1)}, f32[128,128]{1,0:T(8,128)S(1)}, bf16[128,128]{1,0:T(8,128)(2,1)S(1)}, bf16[256,128]{1,0:T(8,128)(2,1)S(1)}, bf16[256,128]{1,0:T(8,128)(2,1)S(1)}) custom-call(s32[2,8]{1,0:T(2,128)S(1)} %bitcast.9, bf16[8,2,128,128]{3,2,1,0:T(8,128)(2,1)S(1)} %bitcast_select_fusion.refs_1_, ...), custom_call_target="tpu_custom_call" | custom-call | tf_op jit(solution)/shard_map/pallas_call | solution.py:34
  17.4 1.2 %collective-permute-done.9 = f32[128,128]{1,0:T(8,128)S(1)} collective-permute-done((f32[128,128]{1,0:T(8,128)S(1)}, f32[128,128]{1,0:T(8,128)S(1)}, u32[]{:S(2)}, u32[]{:S(2)}) %collective-permute-start.9) | collective-permute-done | bytes 65568 | tf_op jit(solution)/shard_map/ppermute | solution.py:124
  18.7 1.6 %collective-permute-start.10 = (bf16[256,128]{1,0:T(8,128)(2,1)S(1)}, bf16[256,128]{1,0:T(8,128)(2,1)S(1)}, u32[]{:S(2)}, u32[]{:S(2)}) collective-permute-start(bf16[256,128]{1,0:T(8,128)(2,1)S(1)} %constant_dynamic-update-slice_fusion.3), channel_id=1, source_target_pairs={{0,16},{1,9},{2,18},{3,11},{4,20},{5,13},{6,22},{7,15},{8,24},{9,1... | collective-permute-start | bytes 196616 | tf_op jit(solution)/shard_map/ppermute | solution.py:134
  20.3 1.4 %collective-permute-start.11 = (bf16[256,128]{1,0:T(8,128)(2,1)S(1)}, bf16[256,128]{1,0:T(8,128)(2,1)S(1)}, u32[]{:S(2)}, u32[]{:S(2)}) collective-permute-start(bf16[256,128]{1,0:T(8,128)(2,1)S(1)} %get-tuple-element.44), channel_id=1, source_target_pairs={{0,24},{1,25},{2,26},{3,27},{4,28},{5,29},{6,30},{7,31},{8,16},{9,... | collective-permute-start | bytes 196616 | tf_op jit(solution)/shard_map/ppermute | solution.py:134
  21.7 0.5 %collective-permute-start.8 = (bf16[128,128]{1,0:T(8,128)(2,1)S(1)}, bf16[128,128]{1,0:T(8,128)(2,1)S(1)}, u32[]{:S(2)}, u32[]{:S(2)}) collective-permute-start(bf16[128,128]{1,0:T(8,128)(2,1)S(1)} %get-tuple-element.38), channel_id=1, source_target_pairs={{0,8},{1,17},{2,10},{3,19},{4,12},{5,21},{6,14},{7,23},{8,0},{9,25... | collective-permute-start | bytes 98312 | tf_op jit(solution)/shard_map/ppermute | solution.py:134
  22.2 3.4 %collective-permute-done.8.refs_1_ = bf16[128,128]{1,0:T(8,128)(2,1)S(1)} collective-permute-done((bf16[128,128]{1,0:T(8,128)(2,1)S(1)}, bf16[128,128]{1,0:T(8,128)(2,1)S(1)}, u32[]{:S(2)}, u32[]{:S(2)}) %collective-permute-start.8) | collective-permute-done | bytes 32800 | tf_op jit(solution)/shard_map/ppermute | solution.py:134
  25.7 1.2 %collective-permute-done.12 = bf16[128,128]{1,0:T(8,128)(2,1)S(1)} collective-permute-done((bf16[128,128]{1,0:T(8,128)(2,1)S(1)}, bf16[128,128]{1,0:T(8,128)(2,1)S(1)}, u32[]{:S(2)}, u32[]{:S(2)}) %collective-permute-start.12) | collective-permute-done | bytes 32800 | tf_op jit(solution)/shard_map/ppermute | solution.py:124
  26.9 0.2 collective-permute-start.13
  27.1 3.0 %collective-permute-start.15 = (bf16[128,128]{1,0:T(8,128)(2,1)S(1)}, bf16[128,128]{1,0:T(8,128)(2,1)S(1)}, u32[]{:S(2)}, u32[]{:S(2)}) collective-permute-start(bf16[128,128]{1,0:T(8,128)(2,1)S(1)} %add_convert_fusion), channel_id=1, source_target_pairs={{0,6},{1,7},{2,4},{3,5},{4,2},{5,3},{6,0},{7,1},{8,14},{9,15},{10,... | collective-permute-start | bytes 98312 | tf_op jit(solution)/shard_map/ppermute | solution.py:134
  30.1 1.1 %collective-permute-done.13 = bf16[128,128]{1,0:T(8,128)(2,1)S(1)} collective-permute-done((bf16[128,128]{1,0:T(8,128)(2,1)S(1)}, bf16[128,128]{1,0:T(8,128)(2,1)S(1)}, u32[]{:S(2)}, u32[]{:S(2)}) %collective-permute-start.13) | collective-permute-done | bytes 32800 | tf_op jit(solution)/shard_map/ppermute | solution.py:134
  31.3 0.9 %shard_map.97 = bf16[128,128]{1,0:T(8,128)(2,1)} custom-call(s32[1,128]{1,0:T(1,128)S(1)} %bitcast.8, bf16[128,128]{1,0:T(8,128)(2,1)S(1)} %copy-done, bf16[128,128]{1,0:T(8,128)(2,1)S(1)} %get-tuple-element.37.refs_0_, bf16[128,128]{1,0:T(8,128)(2,1)S(1)} %collective-permute-done.8.refs_1_, bf16[256,128]{1,0:T(8,128)(2,1)S(1)} %collective-permute-done.10.refs_2_, ...), custom_call_target="tpu_custom_call" | custom-call | tf_op jit(solution)/shard_map/pallas_call | solution.py:34
  32.2 0.7 %collective-permute-done.15 = bf16[128,128]{1,0:T(8,128)(2,1)S(1)} collective-permute-done((bf16[128,128]{1,0:T(8,128)(2,1)S(1)}, bf16[128,128]{1,0:T(8,128)(2,1)S(1)}, u32[]{:S(2)}, u32[]{:S(2)}) %collective-permute-start.15) | collective-permute-done | bytes 32800 | tf_op jit(solution)/shard_map/ppermute | solution.py:134
  32.9 0.7 %add_multiply_fusion = f32[128,128]{1,0:T(8,128)} fusion(bf16[128,128]{1,0:T(8,128)(2,1)S(1)} %collective-permute-done.15, bf16[128,128]{1,0:T(8,128)(2,1)S(1)} %add_convert_fusion, bf16[128,128]{1,0:T(8,128)(2,1)S(1)} %collective-permute-done.14, bf16[128,128]{1,0:T(8,128)(2,1)S(1)} %collective-permute-done.13, pred[]{:T(512)S(6)} %eq.3), kind=kLoop, calls=%fused_computation.1 | loop fusion | flops 163840 | bytes 196609 | tf_op jit(solution)/shard_map/mul | solution.py:183
  (29 shorter events, 0.5 us)
Async XLA Ops:
  1.4 0.7 %copy-start.1 = (s32[128]{0:T(128)S(1)}, s32[128]{0:T(128)}, u32[]{:S(2)}) copy-start(s32[128]{0:T(128)} %param.19) | copy-start | bytes 1540
  2.3 1.4 %collective-permute-start = (bf16[128,128]{1,0:T(8,128)(2,1)S(1)}, bf16[128,128]{1,0:T(8,128)(2,1)S(1)}, u32[]{:S(2)}, u32[]{:S(2)}) collective-permute-start(bf16[128,128]{1,0:T(8,128)(2,1)S(1)} %get-tuple-element.36), channel_id=1, source_target_pairs={{0,1},{1,0},{2,3},{3,2},{4,5},{5,4},{6,7},{7,6},{8,9},{9,8},{10,11... | collective-permute-start | bytes 98312 | tf_op jit(solution)/shard_map/ppermute | solution.py:124
  3.7 5.7 %copy-start.3 = (s32[1,1,8]{2,1,0:T(1,128)S(1)}, s32[1,1,8]{2,1,0:T(1,128)}, u32[]{:S(2)}) copy-start(s32[1,1,8]{2,1,0:T(1,128)} %param.18) | copy-start | bytes 100
  3.7 7.4 %collective-permute-start.3 = (bf16[256,128]{1,0:T(8,128)(2,1)S(1)}, bf16[256,128]{1,0:T(8,128)(2,1)S(1)}, u32[]{:S(2)}, u32[]{:S(2)}) collective-permute-start(bf16[256,128]{1,0:T(8,128)(2,1)S(1)} %constant_dynamic-update-slice_fusion.refs_2_), channel_id=1, source_target_pairs={{0,6},{1,25},{2,4},{3,27},{4,2},{5,29},{6,0},{7,31},{8,14},{9,17},... | collective-permute-start | bytes 196616 | tf_op jit(solution)/shard_map/ppermute | solution.py:134
  8.7 5.2 %collective-permute-start.2 = (bf16[256,128]{1,0:T(8,128)(2,1)S(1)}, bf16[256,128]{1,0:T(8,128)(2,1)S(1)}, u32[]{:S(2)}, u32[]{:S(2)}) collective-permute-start(bf16[256,128]{1,0:T(8,128)(2,1)S(1)} %constant_dynamic-update-slice_fusion.refs_2_), channel_id=1, source_target_pairs={{0,4},{1,17},{2,6},{3,19},{4,0},{5,21},{6,2},{7,23},{8,12},{9,25},... | collective-permute-start | bytes 196616 | tf_op jit(solution)/shard_map/ppermute | solution.py:134
  8.7 5.2 %collective-permute-start.1 = (bf16[256,128]{1,0:T(8,128)(2,1)S(1)}, bf16[256,128]{1,0:T(8,128)(2,1)S(1)}, u32[]{:S(2)}, u32[]{:S(2)}) collective-permute-start(bf16[256,128]{1,0:T(8,128)(2,1)S(1)} %constant_dynamic-update-slice_fusion.refs_2_), channel_id=1, source_target_pairs={{0,2},{1,9},{2,0},{3,11},{4,6},{5,13},{6,4},{7,15},{8,10},{9,1},{1... | collective-permute-start | bytes 196616 | tf_op jit(solution)/shard_map/ppermute | solution.py:134
  9.4 6.1 %collective-permute-start.4 = (bf16[256,128]{1,0:T(8,128)(2,1)S(1)}, bf16[256,128]{1,0:T(8,128)(2,1)S(1)}, u32[]{:S(2)}, u32[]{:S(2)}) collective-permute-start(bf16[256,128]{1,0:T(8,128)(2,1)S(1)} %constant_dynamic-update-slice_fusion.refs_2_), channel_id=1, source_target_pairs={{0,1},{1,0},{2,3},{3,2},{4,5},{5,4},{6,7},{7,6},{8,9},{9,8},{10,11... | collective-permute-start | bytes 196616 | tf_op jit(solution)/shard_map/ppermute | solution.py:124
  11.0 4.5 %collective-permute-start.7 = (bf16[256,128]{1,0:T(8,128)(2,1)S(1)}, bf16[256,128]{1,0:T(8,128)(2,1)S(1)}, u32[]{:S(2)}, u32[]{:S(2)}) collective-permute-start(bf16[256,128]{1,0:T(8,128)(2,1)S(1)} %collective-permute-done.3.refs_5_), channel_id=1, source_target_pairs={{0,1},{1,0},{2,3},{3,2},{4,5},{5,4},{6,7},{7,6},{8,9},{9,8},{10,11... | collective-permute-start | bytes 196616 | tf_op jit(solution)/shard_map/ppermute | solution.py:124
  13.8 1.7 %collective-permute-start.6 = (bf16[256,128]{1,0:T(8,128)(2,1)S(1)}, bf16[256,128]{1,0:T(8,128)(2,1)S(1)}, u32[]{:S(2)}, u32[]{:S(2)}) collective-permute-start(bf16[256,128]{1,0:T(8,128)(2,1)S(1)} %collective-permute-done.2.refs_4_), channel_id=1, source_target_pairs={{0,1},{1,0},{2,3},{3,2},{4,5},{5,4},{6,7},{7,6},{8,9},{9,8},{10,11... | collective-permute-start | bytes 196616 | tf_op jit(solution)/shard_map/ppermute | solution.py:124
  13.9 1.7 %collective-permute-start.5 = (bf16[256,128]{1,0:T(8,128)(2,1)S(1)}, bf16[256,128]{1,0:T(8,128)(2,1)S(1)}, u32[]{:S(2)}, u32[]{:S(2)}) collective-permute-start(bf16[256,128]{1,0:T(8,128)(2,1)S(1)} %collective-permute-done.1.refs_3_), channel_id=1, source_target_pairs={{0,1},{1,0},{2,3},{3,2},{4,5},{5,4},{6,7},{7,6},{8,9},{9,8},{10,11... | collective-permute-start | bytes 196616 | tf_op jit(solution)/shard_map/ppermute | solution.py:124
  15.5 0.7 %copy-start.2 = (s32[1,1,8,2]{2,3,1,0:T(2,128)S(1)}, s32[1,1,8,2]{2,3,1,0:T(2,128)}, u32[]{:S(2)}) copy-start(s32[1,1,8,2]{2,3,1,0:T(2,128)} %param.17) | copy-start | bytes 196
  17.3 1.3 %collective-permute-start.9 = (f32[128,128]{1,0:T(8,128)S(1)}, f32[128,128]{1,0:T(8,128)S(1)}, u32[]{:S(2)}, u32[]{:S(2)}) collective-permute-start(f32[128,128]{1,0:T(8,128)S(1)} %get-tuple-element.40), channel_id=1, source_target_pairs={{0,1},{1,0},{2,3},{3,2},{4,5},{5,4},{6,7},{7,6},{8,9},{9,8},{10,11... | collective-permute-start | bytes 196616 | tf_op jit(solution)/shard_map/ppermute | solution.py:124
  18.7 6.9 %collective-permute-start.10 = (bf16[256,128]{1,0:T(8,128)(2,1)S(1)}, bf16[256,128]{1,0:T(8,128)(2,1)S(1)}, u32[]{:S(2)}, u32[]{:S(2)}) collective-permute-start(bf16[256,128]{1,0:T(8,128)(2,1)S(1)} %constant_dynamic-update-slice_fusion.3), channel_id=1, source_target_pairs={{0,16},{1,9},{2,18},{3,11},{4,20},{5,13},{6,22},{7,15},{8,24},{9,1... | collective-permute-start | bytes 196616 | tf_op jit(solution)/shard_map/ppermute | solution.py:134
  20.3 5.4 %collective-permute-start.11 = (bf16[256,128]{1,0:T(8,128)(2,1)S(1)}, bf16[256,128]{1,0:T(8,128)(2,1)S(1)}, u32[]{:S(2)}, u32[]{:S(2)}) collective-permute-start(bf16[256,128]{1,0:T(8,128)(2,1)S(1)} %get-tuple-element.44), channel_id=1, source_target_pairs={{0,24},{1,25},{2,26},{3,27},{4,28},{5,29},{6,30},{7,31},{8,16},{9,... | collective-permute-start | bytes 196616 | tf_op jit(solution)/shard_map/ppermute | solution.py:134
  21.7 3.9 %collective-permute-start.8 = (bf16[128,128]{1,0:T(8,128)(2,1)S(1)}, bf16[128,128]{1,0:T(8,128)(2,1)S(1)}, u32[]{:S(2)}, u32[]{:S(2)}) collective-permute-start(bf16[128,128]{1,0:T(8,128)(2,1)S(1)} %get-tuple-element.38), channel_id=1, source_target_pairs={{0,8},{1,17},{2,10},{3,19},{4,12},{5,21},{6,14},{7,23},{8,0},{9,25... | collective-permute-start | bytes 98312 | tf_op jit(solution)/shard_map/ppermute | solution.py:134
  25.6 5.7 %copy-start = (bf16[128,128]{1,0:T(8,128)(2,1)S(1)}, bf16[128,128]{1,0:T(8,128)(2,1)}, u32[]{:S(2)}) copy-start(bf16[128,128]{1,0:T(8,128)(2,1)} %weight_ref.1) | copy-start | bytes 98308
  25.6 1.3 %collective-permute-start.12 = (bf16[128,128]{1,0:T(8,128)(2,1)S(1)}, bf16[128,128]{1,0:T(8,128)(2,1)S(1)}, u32[]{:S(2)}, u32[]{:S(2)}) collective-permute-start(bf16[128,128]{1,0:T(8,128)(2,1)S(1)} %slice.40), channel_id=1, source_target_pairs={{0,1},{1,0},{2,3},{3,2},{4,5},{5,4},{6,7},{7,6},{8,9},{9,8},{10,11... | collective-permute-start | bytes 98312 | tf_op jit(solution)/shard_map/ppermute | solution.py:124
  26.9 4.3 %collective-permute-start.13 = (bf16[128,128]{1,0:T(8,128)(2,1)S(1)}, bf16[128,128]{1,0:T(8,128)(2,1)S(1)}, u32[]{:S(2)}, u32[]{:S(2)}) collective-permute-start(bf16[128,128]{1,0:T(8,128)(2,1)S(1)} %add_convert_fusion), channel_id=1, source_target_pairs={{0,2},{1,5},{2,0},{3,7},{4,6},{5,1},{6,4},{7,3},{8,10},{9,13},{10,... | collective-permute-start | bytes 98312 | tf_op jit(solution)/shard_map/ppermute | solution.py:134
  27.1 5.7 %collective-permute-start.15 = (bf16[128,128]{1,0:T(8,128)(2,1)S(1)}, bf16[128,128]{1,0:T(8,128)(2,1)S(1)}, u32[]{:S(2)}, u32[]{:S(2)}) collective-permute-start(bf16[128,128]{1,0:T(8,128)(2,1)S(1)} %add_convert_fusion), channel_id=1, source_target_pairs={{0,6},{1,7},{2,4},{3,5},{4,2},{5,3},{6,0},{7,1},{8,14},{9,15},{10,... | collective-permute-start | bytes 98312 | tf_op jit(solution)/shard_map/ppermute | solution.py:134
  31.3 1.6 %collective-permute-start.14 = (bf16[128,128]{1,0:T(8,128)(2,1)S(1)}, bf16[128,128]{1,0:T(8,128)(2,1)S(1)}, u32[]{:S(2)}, u32[]{:S(2)}) collective-permute-start(bf16[128,128]{1,0:T(8,128)(2,1)S(1)} %collective-permute-done.13), channel_id=1, source_target_pairs={{0,1},{1,0},{2,3},{3,2},{4,5},{5,4},{6,7},{7,6},{8,9},{9,8},{10,11... | collective-permute-start | bytes 98312 | tf_op jit(solution)/shard_map/ppermute | solution.py:124

commit v3 on v2

--- a/solution.py
+++ b/solution.py
@@ -24,6 +24,10 @@
 
 def source_of(index, step, size):
     return index ^ step if swaps(size) else lax.rem(index + (size - step), size)
+
+
+def far_steps(size):
+    return [0, 1, *range(size - 1, 1, -1)]
 
 
 def dot(a, b, contract):
@@ -50,10 +54,6 @@
     place = spread(order_ref[...])
     keep_out[...] = dot(place, keep_ref[...], ((0,), (0,))).astype(BF)
     give_out[...] = dot(place, give_ref[...], ((0,), (0,))).astype(BF)
-
-
-def row_steps(rows):
-    return list(zip([1, 2, *range(3, rows)], [2, 1, *range(3, rows)]))
 
 
 def product_kernel(rows, depth, *refs):
@@ -67,8 +67,8 @@
     c = lax.axis_index("col")
     z, even = lax.div(c, 2), lax.rem(c, 2) == 0
     total[...] = jnp.zeros_like(total)
-    for step in range(depth):
-        pair = jnp.where(even, own[step][...], other[step][...])
+    for slot, step in enumerate(far_steps(depth)):
+        pair = jnp.where(even, own[slot][...], other[slot][...])
         chip = source_of(z, step, depth)
         for core in range(2):
             i = 2 * chip + core
@@ -77,14 +77,13 @@
                 total[cols_ref[k, i]] += dot(blocks_ref[i, k], panel, ((0,), (0,)))
     terms = [total[source_of(r, step, rows)].astype(BF) for step in range(rows)]
     weight = jnp.zeros((F, F), F32)
-    for step in range(rows):
-        feat = jnp.where(even, other[step][B : 2 * B], own[step][0:B])
+    for slot, step in enumerate(far_steps(rows)):
+        feat = jnp.where(even, other[slot][B : 2 * B], own[slot][0:B])
         weight += dot(feat, terms[step], ((0,), (0,)))
     term_ref[...] = terms[0]
     weight_ref[...] = weight
-    sent = terms if swaps(rows) else [terms[-step] for step in range(rows)]
-    for out, (first, second) in zip(outs, row_steps(rows)):
-        out[0:B] = jnp.where(even, sent[first], sent[second])
+    for step, out in zip(far_steps(rows)[1:], outs):
+        out[0:B] = terms[step] if swaps(rows) else terms[rows - step]
 
 
 def sum_in_order(values, index, size):
@@ -139,41 +138,42 @@
     def along_depth(value, steps):
         return move(value, lambda i, core: i, lambda j, core: target_of(j, steps[core], depth))
 
-    def both(value, step):
-        return move(
-            value,
-            lambda i, core: i if core == 0 else target_of(i, step, rows) if step < rows else None,
-            lambda j, core: j if core == 1 else target_of(j, step, depth) if step < depth else None,
-        )
+    def both(value, slot):
+        def row_of(i, core):
+            return i if core == 0 else target_of(i, far_steps(rows)[slot], rows) if slot < rows else None
+
+        def depth_of(j, core):
+            return j if core == 1 else target_of(j, far_steps(depth)[slot], depth) if slot < depth else None
+
+        return move(value, row_of, depth_of)
 
     masked = jnp.where(pre_act > 0, grad_out, jnp.zeros_like(grad_out))
     keep, give = jnp.where(even, masked, features), jnp.where(even, features, masked)
     keep, give = call(first_kernel, [slab, slab], (order_row, keep, give), [pltpu.VMEM] * 3)
-    filled = jnp.arange(K, dtype=jnp.int32)[None, :] < block_counts[0, 0][:, None]
-    blocks = jnp.where(filled[:, :, None, None], blocks[0, 0], jnp.zeros((), BF))
     message = jnp.concatenate([keep, across(give)], axis=0)
+    message, counts = lax.optimization_barrier((message, block_counts))
+    filled = jnp.arange(K, dtype=jnp.int32)[:, None] < counts[0, 0][None, :]
+    targets = jnp.where(filled, block_cols[0, 0].T, 0)
+    blocks = jnp.where(filled.T[:, :, None, None], blocks[0, 0], jnp.zeros((), BF))
     steps = max(rows, depth)
-    own = [message] + [both(message, step) for step in reversed(range(1, steps))][::-1]
+    own = [message] + [both(message, slot) for slot in range(1, steps)]
     other = [across(value) for value in own]
     term, weight_term, *messages = call(
         functools.partial(product_kernel, rows, depth),
-        [slab, jax.ShapeDtypeStruct((F, F), F32), slab] + [pair] * (rows - 2),
-        (block_cols[0, 0].T, blocks, *own, *other),
+        [slab, jax.ShapeDtypeStruct((F, F), F32)] + [pair] * (rows - 1),
+        (targets, blocks, *own, *other),
         [pltpu.SMEM] + [pltpu.VMEM] * (1 + 2 * steps),
         scratch=[pltpu.VMEM((rows, B, F), F32)],
         limit=limit,
     )
     chip_weight = (weight_term + across(weight_term)).astype(BF)
-    plan = row_steps(rows)
-    terms = [along_row(messages[0], plan[0])]
-    terms += [along_row(m.at[B:].set(chip_weight), plan[i + 1]) for i, m in enumerate(messages[1:])]
+    row_plan = far_steps(rows)[1:]
+    terms = [along_row(m.at[B:].set(chip_weight), (step, step)) for step, m in zip(row_plan, messages)]
     (grad_feat,) = call(
         functools.partial(feature_kernel, rows), [slab], (order_row, weight, term, *terms), [pltpu.VMEM] * (2 + rows)
     )
-    terms = list(lax.optimization_barrier(tuple(terms)))
-    mine = terms[1][B:]
-    swapped = across(mine)
-    weights = [chip_weight, jnp.where(even, swapped, mine), jnp.where(even, mine, swapped)] + [t[B:] for t in terms[2:]]
+    by_step = dict(zip(row_plan, terms))
+    weights = [chip_weight] + [by_step[step][B:] for step in range(1, rows)]
     row_weight = sum_in_order(weights, r, rows).astype(BF)
     mine = along_depth(row_weight, (1, 2))
     rest = [along_depth(row_weight, (step, step)) for step in range(3, depth)]

time: 33.8 us -> 31.9 us (0.944)
  waiting for transfers between devices: 12.9 us -> 12.1 us
  local copies, waits for them, and re-layouts: 1.32 us -> 0.67 us
  starting transfers between devices: 13.6 us -> 13.2 us
    ppermute x8, starting transfers between devices: 12.4 us -> 11.5 us  [move(): return lax.ppermute(value, axes, pairs)]
    ppermute x8 -> x7, waiting for transfers between devices: 3.3 us -> 2.65 us  [across(): return lax.ppermute(value, 'col', [(i, i ^ 1) for i in range(cols)])]
    unnamed x9 -> x8, local copies, waits for them, and re-layouts: 1.29 us -> 0.66 us
    ppermute x8 -> x7, starting transfers between devices: 1.18 us -> 1.79 us  [across(): return lax.ppermute(value, 'col', [(i, i ^ 1) for i in range(cols)])]
    select_n x1 -> x2, other arithmetic: 1.14 us -> 1.16 us  [the longest x1 1.16 us: shards(): jnp.where(filled.T[:, :, None, None], blocks[0, 0], jnp.zeros((), BF))]
  transfers between devices with their start and end apart: 16 -> 15, of which waited for: 8 -> 11; matrix products, arithmetic and copies ran while one was open for 4% -> 4% of each run, Pallas kernels for 3% -> 3%
where the time goes in v3:
time: 31.9 us; the launch traced here: 31.7 us
  starting transfers between devices  13.2 us (41%)
  waiting for transfers between devices  12.1 us (38%)
  other arithmetic  2.74 us (9%)
  Pallas kernels  2.21 us (7%)
  between operations  0.72 us (2%)
  local copies, waits for them, and re-layouts  0.67 us (2%)
    ppermute x8, starting transfers between devices, move(): return lax.ppermute(value, axes, pairs)  11.5 us
    ppermute x8, waiting for transfers between devices, move(): return lax.ppermute(value, axes, pairs)  9.47 us
    ppermute x7, waiting for transfers between devices, across(): return lax.ppermute(value, 'col', [(i, i ^ 1) for i in range(cols)])  2.65 us
    pallas_call x3, Pallas kernels, call(): pl.pallas_call(body, out_shape=outs, in_specs=[pl.BlockSpec(memory_space=...  2.21 us
    ppermute x7, starting transfers between devices, across(): return lax.ppermute(value, 'col', [(i, i ^ 1) for i in range(cols)])  1.79 us
    select_n x1, other arithmetic, shards(): jnp.where(filled.T[:, :, None, None], blocks[0, 0], jnp.zeros((), BF))  1.16 us
    select_n x1, other arithmetic, shards(): jnp.where(even, features, masked)  0.8 us
    unnamed x8, local copies, waits for them, and re-layouts  0.66 us
  transfers between devices with their start and end apart: 15, of which 11 were waited for; matrix products, arithmetic and copies ran while one was open for 4% of the time, Pallas kernels for 3%

profile of v3, /device:TPU:0, one launch (start us, length us, event | category | flops | bytes accessed | tf_op | source)
XLA Modules:
  0.0 31.7 jit_solution(18206580899533756893)
XLA Ops:
  0.6 0.8 %broadcast_select_fusion = (bf16[128,128]{1,0:T(8,128)(2,1)S(1)}, bf16[128,128]{1,0:T(8,128)(2,1)S(1)}) fusion(bf16[128,128]{1,0:T(8,128)(2,1)} %param.16, pred[]{:T(512)S(6)} %eq.3, bf16[128,128]{1,0:T(8,128)(2,1)} %param.14, bf16[128,128]{1,0:T(8,128)(2,1)} %param.15), kind=kLoop, calls=%fused_computation.6 | loop fusion | flops 65536 | bytes 163841 | tf_op jit(solution)/shard_map/jit(_where)/select_n | solution.py:151
  1.4 0.6 %copy-done.1 = s32[128]{0:T(128)S(1)} copy-done((s32[128]{0:T(128)S(1)}, s32[128]{0:T(128)}, u32[]{:S(2)}) %copy-start.1) | copy-done | bytes 536
  2.3 0.5 %collective-permute-start = (bf16[128,128]{1,0:T(8,128)(2,1)S(1)}, bf16[128,128]{1,0:T(8,128)(2,1)S(1)}, u32[]{:S(2)}, u32[]{:S(2)}) collective-permute-start(bf16[128,128]{1,0:T(8,128)(2,1)S(1)} %get-tuple-element.48), channel_id=1, source_target_pairs={{0,1},{1,0},{2,3},{3,2},{4,5},{5,4},{6,7},{7,6},{8,9},{9,8},{10,11... | collective-permute-start | bytes 98312 | tf_op jit(solution)/shard_map/ppermute | solution.py:123
  2.8 0.9 %collective-permute-done = bf16[128,128]{1,0:T(8,128)(2,1)S(1)} collective-permute-done((bf16[128,128]{1,0:T(8,128)(2,1)S(1)}, bf16[128,128]{1,0:T(8,128)(2,1)S(1)}, u32[]{:S(2)}, u32[]{:S(2)}) %collective-permute-start) | collective-permute-done | bytes 32800 | tf_op jit(solution)/shard_map/ppermute | solution.py:123
  3.7 0.4 %collective-permute-start.4 = (bf16[256,128]{1,0:T(8,128)(2,1)S(1)}, bf16[256,128]{1,0:T(8,128)(2,1)S(1)}, u32[]{:S(2)}, u32[]{:S(2)}) collective-permute-start(bf16[256,128]{1,0:T(8,128)(2,1)S(1)} %pad_maximum_fusion.refs_2_), channel_id=1, source_target_pairs={{0,1},{1,0},{2,3},{3,2},{4,5},{5,4},{6,7},{7,6},{8,9},{9,8},{10,11... | collective-permute-start | bytes 196616 | tf_op jit(solution)/shard_map/ppermute | solution.py:123
  4.1 3.7 %collective-permute-start.3 = (bf16[256,128]{1,0:T(8,128)(2,1)S(1)}, bf16[256,128]{1,0:T(8,128)(2,1)S(1)}, u32[]{:S(2)}, u32[]{:S(2)}) collective-permute-start(bf16[256,128]{1,0:T(8,128)(2,1)S(1)} %pad_maximum_fusion.refs_2_), channel_id=1, source_target_pairs={{0,4},{1,17},{2,6},{3,19},{4,0},{5,21},{6,2},{7,23},{8,12},{9,25},... | collective-permute-start | bytes 196616 | tf_op jit(solution)/shard_map/ppermute | solution.py:133
  7.8 1.3 %collective-permute-start.2 = (bf16[256,128]{1,0:T(8,128)(2,1)S(1)}, bf16[256,128]{1,0:T(8,128)(2,1)S(1)}, u32[]{:S(2)}, u32[]{:S(2)}) collective-permute-start(bf16[256,128]{1,0:T(8,128)(2,1)S(1)} %pad_maximum_fusion.refs_2_), channel_id=1, source_target_pairs={{0,6},{1,25},{2,4},{3,27},{4,2},{5,29},{6,0},{7,31},{8,14},{9,17},... | collective-permute-start | bytes 196616 | tf_op jit(solution)/shard_map/ppermute | solution.py:133
  9.4 1.2 %bitcast_select_fusion.refs_1_ = bf16[8,2,128,128]{3,2,1,0:T(8,128)(2,1)S(1)} fusion(bf16[1,1,8,2,128,128]{5,4,3,2,1,0:T(8,128)(2,1)} %param.18, pred[8,2]{1,0:T(8,128)(4,1)S(1)} %iota_compare_fusion), kind=kLoop, calls=%fused_computation | loop fusion | flops 262144 | bytes 1048592 | tf_op jit(solution)/shard_map/jit(_where)/select_n | solution.py:157
  10.7 3.3 %collective-permute-done.2.refs_4_ = bf16[256,128]{1,0:T(8,128)(2,1)S(1)} collective-permute-done((bf16[256,128]{1,0:T(8,128)(2,1)S(1)}, bf16[256,128]{1,0:T(8,128)(2,1)S(1)}, u32[]{:S(2)}, u32[]{:S(2)}) %collective-permute-start.2) | collective-permute-done | bytes 65568 | tf_op jit(solution)/shard_map/ppermute | solution.py:133
  14.5 0.7 %collective-permute-done.6.refs_8_ = bf16[256,128]{1,0:T(8,128)(2,1)S(1)} collective-permute-done((bf16[256,128]{1,0:T(8,128)(2,1)S(1)}, bf16[256,128]{1,0:T(8,128)(2,1)S(1)}, u32[]{:S(2)}, u32[]{:S(2)}) %collective-permute-start.6) | collective-permute-done | bytes 65568 | tf_op jit(solution)/shard_map/ppermute | solution.py:123
  15.4 1.1 %shard_map.96 = (bf16[128,128]{1,0:T(8,128)(2,1)S(1)}, f32[128,128]{1,0:T(8,128)S(1)}, bf16[256,128]{1,0:T(8,128)(2,1)S(1)}, bf16[256,128]{1,0:T(8,128)(2,1)S(1)}, bf16[256,128]{1,0:T(8,128)(2,1)S(1)}) custom-call(s32[2,8]{1,0:T(2,128)S(1)} %compare_select_fusion.1.refs_0_, bf16[8,2,128,128]{3,2,1,0:T(8,128)(2,1)S(1)} %bitcast_select_fusion.refs_1_, ...), custom_call_target="tpu_custom_call" | custom-call | tf_op jit(solution)/shard_map/pallas_call | solution.py:38
  16.5 0.4 %collective-permute-start.8 = (f32[128,128]{1,0:T(8,128)S(1)}, f32[128,128]{1,0:T(8,128)S(1)}, u32[]{:S(2)}, u32[]{:S(2)}) collective-permute-start(f32[128,128]{1,0:T(8,128)S(1)} %get-tuple-element.53), channel_id=1, source_target_pairs={{0,1},{1,0},{2,3},{3,2},{4,5},{5,4},{6,7},{7,6},{8,9},{9,8},{10,11... | collective-permute-start | bytes 196616 | tf_op jit(solution)/shard_map/ppermute | solution.py:123
  16.9 0.9 %collective-permute-done.8 = f32[128,128]{1,0:T(8,128)S(1)} collective-permute-done((f32[128,128]{1,0:T(8,128)S(1)}, f32[128,128]{1,0:T(8,128)S(1)}, u32[]{:S(2)}, u32[]{:S(2)}) %collective-permute-start.8) | collective-permute-done | bytes 65568 | tf_op jit(solution)/shard_map/ppermute | solution.py:123
  17.9 2.5 %collective-permute-start.10 = (bf16[256,128]{1,0:T(8,128)(2,1)S(1)}, bf16[256,128]{1,0:T(8,128)(2,1)S(1)}, u32[]{:S(2)}, u32[]{:S(2)}) collective-permute-start(bf16[256,128]{1,0:T(8,128)(2,1)S(1)} %get-tuple-element.60), channel_id=1, source_target_pairs={{0,24},{1,25},{2,26},{3,27},{4,28},{5,29},{6,30},{7,31},{8,16},{9,... | collective-permute-start | bytes 196616 | tf_op jit(solution)/shard_map/ppermute | solution.py:133
  20.4 0.5 %collective-permute-start.9 = (bf16[256,128]{1,0:T(8,128)(2,1)S(1)}, bf16[256,128]{1,0:T(8,128)(2,1)S(1)}, u32[]{:S(2)}, u32[]{:S(2)}) collective-permute-start(bf16[256,128]{1,0:T(8,128)(2,1)S(1)} %get-tuple-element.61), channel_id=1, source_target_pairs={{0,8},{1,9},{2,10},{3,11},{4,12},{5,13},{6,14},{7,15},{8,0},{9,1},... | collective-permute-start | bytes 196616 | tf_op jit(solution)/shard_map/ppermute | solution.py:133
  20.9 0.5 %collective-permute-start.11 = (bf16[256,128]{1,0:T(8,128)(2,1)S(1)}, bf16[256,128]{1,0:T(8,128)(2,1)S(1)}, u32[]{:S(2)}, u32[]{:S(2)}) collective-permute-start(bf16[256,128]{1,0:T(8,128)(2,1)S(1)} %get-tuple-element.56), channel_id=1, source_target_pairs={{0,16},{1,17},{2,18},{3,19},{4,20},{5,21},{6,22},{7,23},{8,24},{9,... | collective-permute-start | bytes 196616 | tf_op jit(solution)/shard_map/ppermute | solution.py:133
  21.4 2.0 %collective-permute-done.10.refs_2_ = bf16[256,128]{1,0:T(8,128)(2,1)S(1)} collective-permute-done((bf16[256,128]{1,0:T(8,128)(2,1)S(1)}, bf16[256,128]{1,0:T(8,128)(2,1)S(1)}, u32[]{:S(2)}, u32[]{:S(2)}) %collective-permute-start.10) | collective-permute-done | bytes 65568 | tf_op jit(solution)/shard_map/ppermute | solution.py:133
  23.4 1.2 %collective-permute-done.9.refs_1_ = bf16[256,128]{1,0:T(8,128)(2,1)S(1)} collective-permute-done((bf16[256,128]{1,0:T(8,128)(2,1)S(1)}, bf16[256,128]{1,0:T(8,128)(2,1)S(1)}, u32[]{:S(2)}, u32[]{:S(2)}) %collective-permute-start.9) | collective-permute-done | bytes 65568 | tf_op jit(solution)/shard_map/ppermute | solution.py:133
  24.6 0.5 %collective-permute-done.11.refs_3_ = bf16[256,128]{1,0:T(8,128)(2,1)S(1)} collective-permute-done((bf16[256,128]{1,0:T(8,128)(2,1)S(1)}, bf16[256,128]{1,0:T(8,128)(2,1)S(1)}, u32[]{:S(2)}, u32[]{:S(2)}) %collective-permute-start.11) | collective-permute-done | bytes 65568 | tf_op jit(solution)/shard_map/ppermute | solution.py:133
  25.3 2.5 %collective-permute-start.14 = (bf16[128,128]{1,0:T(8,128)(2,1)S(1)}, bf16[128,128]{1,0:T(8,128)(2,1)S(1)}, u32[]{:S(2)}, u32[]{:S(2)}) collective-permute-start(bf16[128,128]{1,0:T(8,128)(2,1)S(1)} %add_convert_fusion), channel_id=1, source_target_pairs={{0,6},{1,7},{2,4},{3,5},{4,2},{5,3},{6,0},{7,1},{8,14},{9,15},{10,... | collective-permute-start | bytes 98312 | tf_op jit(solution)/shard_map/ppermute | solution.py:133
  27.8 1.4 %collective-permute-done.12 = bf16[128,128]{1,0:T(8,128)(2,1)S(1)} collective-permute-done((bf16[128,128]{1,0:T(8,128)(2,1)S(1)}, bf16[128,128]{1,0:T(8,128)(2,1)S(1)}, u32[]{:S(2)}, u32[]{:S(2)}) %collective-permute-start.12) | collective-permute-done | bytes 32800 | tf_op jit(solution)/shard_map/ppermute | solution.py:133
  29.2 0.9 %shard_map.97 = bf16[128,128]{1,0:T(8,128)(2,1)} custom-call(s32[1,128]{1,0:T(1,128)S(1)} %bitcast.9, bf16[128,128]{1,0:T(8,128)(2,1)S(1)} %copy-done, bf16[128,128]{1,0:T(8,128)(2,1)S(1)} %get-tuple-element.51.refs_0_, bf16[256,128]{1,0:T(8,128)(2,1)S(1)} %collective-permute-done.9.refs_1_, bf16[256,128]{1,0:T(8,128)(2,1)S(1)} %collective-permute-done.10.refs_2_, ...), custom_call_target="tpu_custom_call" | custom-call | tf_op jit(solution)/shard_map/pallas_call | solution.py:38
  30.1 1.0 %collective-permute-done.14 = bf16[128,128]{1,0:T(8,128)(2,1)S(1)} collective-permute-done((bf16[128,128]{1,0:T(8,128)(2,1)S(1)}, bf16[128,128]{1,0:T(8,128)(2,1)S(1)}, u32[]{:S(2)}, u32[]{:S(2)}) %collective-permute-start.14) | collective-permute-done | bytes 32800 | tf_op jit(solution)/shard_map/ppermute | solution.py:133
  31.1 0.7 %add_multiply_fusion = f32[128,128]{1,0:T(8,128)} fusion(bf16[128,128]{1,0:T(8,128)(2,1)S(1)} %collective-permute-done.14, bf16[128,128]{1,0:T(8,128)(2,1)S(1)} %add_convert_fusion, bf16[128,128]{1,0:T(8,128)(2,1)S(1)} %collective-permute-done.13, bf16[128,128]{1,0:T(8,128)(2,1)S(1)} %collective-permute-done.12, pred[]{:T(512)S(6)} %eq.3), kind=kLoop, calls=%fused_computation.2 | loop fusion | flops 163840 | bytes 196609 | tf_op jit(solution)/shard_map/mul | solution.py:183
  (26 shorter events, 1.4 us)
Async XLA Ops:
  1.4 0.7 %copy-start.1 = (s32[128]{0:T(128)S(1)}, s32[128]{0:T(128)}, u32[]{:S(2)}) copy-start(s32[128]{0:T(128)} %param.21) | copy-start | bytes 1540
  2.3 1.4 %collective-permute-start = (bf16[128,128]{1,0:T(8,128)(2,1)S(1)}, bf16[128,128]{1,0:T(8,128)(2,1)S(1)}, u32[]{:S(2)}, u32[]{:S(2)}) collective-permute-start(bf16[128,128]{1,0:T(8,128)(2,1)S(1)} %get-tuple-element.48), channel_id=1, source_target_pairs={{0,1},{1,0},{2,3},{3,2},{4,5},{5,4},{6,7},{7,6},{8,9},{9,8},{10,11... | collective-permute-start | bytes 98312 | tf_op jit(solution)/shard_map/ppermute | solution.py:123
  3.7 5.7 %copy-start.3 = (s32[1,1,8]{2,1,0:T(1,128)S(1)}, s32[1,1,8]{2,1,0:T(1,128)}, u32[]{:S(2)}) copy-start(s32[1,1,8]{2,1,0:T(1,128)} %param.20) | copy-start | bytes 100
  3.7 10.8 %collective-permute-start.4 = (bf16[256,128]{1,0:T(8,128)(2,1)S(1)}, bf16[256,128]{1,0:T(8,128)(2,1)S(1)}, u32[]{:S(2)}, u32[]{:S(2)}) collective-permute-start(bf16[256,128]{1,0:T(8,128)(2,1)S(1)} %pad_maximum_fusion.refs_2_), channel_id=1, source_target_pairs={{0,1},{1,0},{2,3},{3,2},{4,5},{5,4},{6,7},{7,6},{8,9},{9,8},{10,11... | collective-permute-start | bytes 196616 | tf_op jit(solution)/shard_map/ppermute | solution.py:123
  4.1 6.5 %collective-permute-start.3 = (bf16[256,128]{1,0:T(8,128)(2,1)S(1)}, bf16[256,128]{1,0:T(8,128)(2,1)S(1)}, u32[]{:S(2)}, u32[]{:S(2)}) collective-permute-start(bf16[256,128]{1,0:T(8,128)(2,1)S(1)} %pad_maximum_fusion.refs_2_), channel_id=1, source_target_pairs={{0,4},{1,17},{2,6},{3,19},{4,0},{5,21},{6,2},{7,23},{8,12},{9,25},... | collective-permute-start | bytes 196616 | tf_op jit(solution)/shard_map/ppermute | solution.py:133
  7.8 6.2 %collective-permute-start.2 = (bf16[256,128]{1,0:T(8,128)(2,1)S(1)}, bf16[256,128]{1,0:T(8,128)(2,1)S(1)}, u32[]{:S(2)}, u32[]{:S(2)}) collective-permute-start(bf16[256,128]{1,0:T(8,128)(2,1)S(1)} %pad_maximum_fusion.refs_2_), channel_id=1, source_target_pairs={{0,6},{1,25},{2,4},{3,27},{4,2},{5,29},{6,0},{7,31},{8,14},{9,17},... | collective-permute-start | bytes 196616 | tf_op jit(solution)/shard_map/ppermute | solution.py:133
  9.1 5.0 %collective-permute-start.1 = (bf16[256,128]{1,0:T(8,128)(2,1)S(1)}, bf16[256,128]{1,0:T(8,128)(2,1)S(1)}, u32[]{:S(2)}, u32[]{:S(2)}) collective-permute-start(bf16[256,128]{1,0:T(8,128)(2,1)S(1)} %pad_maximum_fusion.refs_2_), channel_id=1, source_target_pairs={{0,2},{1,9},{2,0},{3,11},{4,6},{5,13},{6,4},{7,15},{8,10},{9,1},{1... | collective-permute-start | bytes 196616 | tf_op jit(solution)/shard_map/ppermute | solution.py:133
  9.4 5.0 %copy-start.2 = (s32[1,1,8,2]{2,3,1,0:T(2,128)S(1)}, s32[1,1,8,2]{2,3,1,0:T(2,128)}, u32[]{:S(2)}) copy-start(s32[1,1,8,2]{2,3,1,0:T(2,128)} %param.19) | copy-start | bytes 196
  10.6 3.9 %collective-permute-start.7 = (bf16[256,128]{1,0:T(8,128)(2,1)S(1)}, bf16[256,128]{1,0:T(8,128)(2,1)S(1)}, u32[]{:S(2)}, u32[]{:S(2)}) collective-permute-start(bf16[256,128]{1,0:T(8,128)(2,1)S(1)} %collective-permute-done.3.refs_5_), channel_id=1, source_target_pairs={{0,1},{1,0},{2,3},{3,2},{4,5},{5,4},{6,7},{7,6},{8,9},{9,8},{10,11... | collective-permute-start | bytes 196616 | tf_op jit(solution)/shard_map/ppermute | solution.py:123
  14.0 1.3 %collective-permute-start.6 = (bf16[256,128]{1,0:T(8,128)(2,1)S(1)}, bf16[256,128]{1,0:T(8,128)(2,1)S(1)}, u32[]{:S(2)}, u32[]{:S(2)}) collective-permute-start(bf16[256,128]{1,0:T(8,128)(2,1)S(1)} %collective-permute-done.2.refs_4_), channel_id=1, source_target_pairs={{0,1},{1,0},{2,3},{3,2},{4,5},{5,4},{6,7},{7,6},{8,9},{9,8},{10,11... | collective-permute-start | bytes 196616 | tf_op jit(solution)/shard_map/ppermute | solution.py:123
  14.1 1.3 %collective-permute-start.5 = (bf16[256,128]{1,0:T(8,128)(2,1)S(1)}, bf16[256,128]{1,0:T(8,128)(2,1)S(1)}, u32[]{:S(2)}, u32[]{:S(2)}) collective-permute-start(bf16[256,128]{1,0:T(8,128)(2,1)S(1)} %collective-permute-done.1.refs_3_), channel_id=1, source_target_pairs={{0,1},{1,0},{2,3},{3,2},{4,5},{5,4},{6,7},{7,6},{8,9},{9,8},{10,11... | collective-permute-start | bytes 196616 | tf_op jit(solution)/shard_map/ppermute | solution.py:123
  16.5 1.3 %collective-permute-start.8 = (f32[128,128]{1,0:T(8,128)S(1)}, f32[128,128]{1,0:T(8,128)S(1)}, u32[]{:S(2)}, u32[]{:S(2)}) collective-permute-start(f32[128,128]{1,0:T(8,128)S(1)} %get-tuple-element.53), channel_id=1, source_target_pairs={{0,1},{1,0},{2,3},{3,2},{4,5},{5,4},{6,7},{7,6},{8,9},{9,8},{10,11... | collective-permute-start | bytes 196616 | tf_op jit(solution)/shard_map/ppermute | solution.py:123
  17.9 5.6 %collective-permute-start.10 = (bf16[256,128]{1,0:T(8,128)(2,1)S(1)}, bf16[256,128]{1,0:T(8,128)(2,1)S(1)}, u32[]{:S(2)}, u32[]{:S(2)}) collective-permute-start(bf16[256,128]{1,0:T(8,128)(2,1)S(1)} %get-tuple-element.60), channel_id=1, source_target_pairs={{0,24},{1,25},{2,26},{3,27},{4,28},{5,29},{6,30},{7,31},{8,16},{9,... | collective-permute-start | bytes 196616 | tf_op jit(solution)/shard_map/ppermute | solution.py:133
  20.4 4.3 %collective-permute-start.9 = (bf16[256,128]{1,0:T(8,128)(2,1)S(1)}, bf16[256,128]{1,0:T(8,128)(2,1)S(1)}, u32[]{:S(2)}, u32[]{:S(2)}) collective-permute-start(bf16[256,128]{1,0:T(8,128)(2,1)S(1)} %get-tuple-element.61), channel_id=1, source_target_pairs={{0,8},{1,9},{2,10},{3,11},{4,12},{5,13},{6,14},{7,15},{8,0},{9,1},... | collective-permute-start | bytes 196616 | tf_op jit(solution)/shard_map/ppermute | solution.py:133
  20.9 8.3 %copy-start = (bf16[128,128]{1,0:T(8,128)(2,1)S(1)}, bf16[128,128]{1,0:T(8,128)(2,1)}, u32[]{:S(2)}) copy-start(bf16[128,128]{1,0:T(8,128)(2,1)} %weight_ref.1) | copy-start | bytes 98308
  20.9 4.3 %collective-permute-start.11 = (bf16[256,128]{1,0:T(8,128)(2,1)S(1)}, bf16[256,128]{1,0:T(8,128)(2,1)S(1)}, u32[]{:S(2)}, u32[]{:S(2)}) collective-permute-start(bf16[256,128]{1,0:T(8,128)(2,1)S(1)} %get-tuple-element.56), channel_id=1, source_target_pairs={{0,16},{1,17},{2,18},{3,19},{4,20},{5,21},{6,22},{7,23},{8,24},{9,... | collective-permute-start | bytes 196616 | tf_op jit(solution)/shard_map/ppermute | solution.py:133
  25.2 4.0 %collective-permute-start.12 = (bf16[128,128]{1,0:T(8,128)(2,1)S(1)}, bf16[128,128]{1,0:T(8,128)(2,1)S(1)}, u32[]{:S(2)}, u32[]{:S(2)}) collective-permute-start(bf16[128,128]{1,0:T(8,128)(2,1)S(1)} %add_convert_fusion), channel_id=1, source_target_pairs={{0,2},{1,5},{2,0},{3,7},{4,6},{5,1},{6,4},{7,3},{8,10},{9,13},{10,... | collective-permute-start | bytes 98312 | tf_op jit(solution)/shard_map/ppermute | solution.py:133
  25.3 5.8 %collective-permute-start.14 = (bf16[128,128]{1,0:T(8,128)(2,1)S(1)}, bf16[128,128]{1,0:T(8,128)(2,1)S(1)}, u32[]{:S(2)}, u32[]{:S(2)}) collective-permute-start(bf16[128,128]{1,0:T(8,128)(2,1)S(1)} %add_convert_fusion), channel_id=1, source_target_pairs={{0,6},{1,7},{2,4},{3,5},{4,2},{5,3},{6,0},{7,1},{8,14},{9,15},{10,... | collective-permute-start | bytes 98312 | tf_op jit(solution)/shard_map/ppermute | solution.py:133
  29.2 1.9 %collective-permute-start.13 = (bf16[128,128]{1,0:T(8,128)(2,1)S(1)}, bf16[128,128]{1,0:T(8,128)(2,1)S(1)}, u32[]{:S(2)}, u32[]{:S(2)}) collective-permute-start(bf16[128,128]{1,0:T(8,128)(2,1)S(1)} %collective-permute-done.12), channel_id=1, source_target_pairs={{0,1},{1,0},{2,3},{3,2},{4,5},{5,4},{6,7},{7,6},{8,9},{9,8},{10,11... | collective-permute-start | bytes 98312 | tf_op jit(solution)/shard_map/ppermute | solution.py:123

commit v4 on v3

--- a/solution.py
+++ b/solution.py
@@ -34,7 +34,7 @@
     return lax.dot_general(a, b, (contract, ((), ())), preferred_element_type=F32)
 
 
-def call(body, outs, args, spaces, out_spaces=None, scratch=(), limit=4 << 20):
+def call(body, outs, args, spaces, scratch=(), limit=4 << 20):
     return pl.pallas_call(
         body,
         out_shape=outs,
@@ -56,25 +56,37 @@
     give_out[...] = dot(place, give_ref[...], ((0,), (0,))).astype(BF)
 
 
+def row_steps(rows):
+    return list(zip([1, 2, *range(3, rows)], [2, 1, *range(3, rows)]))
+
+
 def product_kernel(rows, depth, *refs):
     steps = max(rows, depth)
-    cols_ref, blocks_ref = refs[:2]
+    targets_vmem, blocks_ref = refs[:2]
     own, other = refs[2 : 2 + steps], refs[2 + steps : 2 + 2 * steps]
     term_ref, weight_ref = refs[2 + 2 * steps : 4 + 2 * steps]
-    outs = refs[4 + 2 * steps : -1]
-    total = refs[-1]
+    outs = refs[4 + 2 * steps : -4]
+    total, products, targets_ref, sem = refs[-4:]
+    fetch = pltpu.make_async_copy(targets_vmem, targets_ref, sem)
+    fetch.start()
     r = lax.axis_index("row")
     c = lax.axis_index("col")
     z, even = lax.div(c, 2), lax.rem(c, 2) == 0
-    total[...] = jnp.zeros_like(total)
     for slot, step in enumerate(far_steps(depth)):
         pair = jnp.where(even, own[slot][...], other[slot][...])
         chip = source_of(z, step, depth)
         for core in range(2):
-            i = 2 * chip + core
             panel = pair[core * B : (core + 1) * B]
             for k in range(K):
-                total[cols_ref[k, i]] += dot(blocks_ref[i, k], panel, ((0,), (0,)))
+                place = (2 * slot + core) * K + k
+                products[place] = dot(blocks_ref[2 * chip + core, k], panel, ((0,), (0,)))
+    total[...] = jnp.zeros_like(total)
+    fetch.wait()
+    for slot, step in enumerate(far_steps(depth)):
+        chip = source_of(z, step, depth)
+        for core in range(2):
+            for k in range(K):
+                total[targets_ref[k, 2 * chip + core]] += products[(2 * slot + core) * K + k]
     terms = [total[source_of(r, step, rows)].astype(BF) for step in range(rows)]
     weight = jnp.zeros((F, F), F32)
     for slot, step in enumerate(far_steps(rows)):
@@ -82,8 +94,10 @@
         weight += dot(feat, terms[step], ((0,), (0,)))
     term_ref[...] = terms[0]
     weight_ref[...] = weight
-    for step, out in zip(far_steps(rows)[1:], outs):
-        out[0:B] = terms[step] if swaps(rows) else terms[rows - step]
+    sent = terms if swaps(rows) else [terms[-step] for step in range(rows)]
+    for out, (first, second) in zip(outs, row_steps(rows)):
+        out[0:B] = jnp.where(even, sent[first], sent[second])
+    outs[0][B : 2 * B] = jnp.zeros((B, F), BF)
 
 
 def sum_in_order(values, index, size):
@@ -157,23 +171,31 @@
     blocks = jnp.where(filled.T[:, :, None, None], blocks[0, 0], jnp.zeros((), BF))
     steps = max(rows, depth)
     own = [message] + [both(message, slot) for slot in range(1, steps)]
-    other = [across(value) for value in own]
+    held, targets, blocks = lax.optimization_barrier((message, targets, blocks))
+    other = [across(value) for value in (held, *own[1:])]
     term, weight_term, *messages = call(
         functools.partial(product_kernel, rows, depth),
-        [slab, jax.ShapeDtypeStruct((F, F), F32)] + [pair] * (rows - 1),
+        [slab, jax.ShapeDtypeStruct((F, F), F32), pair] + [pair] * (rows - 2),
         (targets, blocks, *own, *other),
-        [pltpu.SMEM] + [pltpu.VMEM] * (1 + 2 * steps),
-        scratch=[pltpu.VMEM((rows, B, F), F32)],
+        [pltpu.VMEM] * (2 + 2 * steps),
+        scratch=[
+            pltpu.VMEM((rows, B, F), F32),
+            pltpu.VMEM((cols * K, B, F), F32),
+            pltpu.SMEM(targets.shape, jnp.int32),
+            pltpu.SemaphoreType.DMA,
+        ],
         limit=limit,
     )
     chip_weight = (weight_term + across(weight_term)).astype(BF)
-    row_plan = far_steps(rows)[1:]
-    terms = [along_row(m.at[B:].set(chip_weight), (step, step)) for step, m in zip(row_plan, messages)]
+    plan = row_steps(rows)
+    terms = [along_row(messages[0], plan[0])]
+    terms += [along_row(m.at[B:].set(chip_weight), plan[i]) for i, m in enumerate(messages) if i > 0]
     (grad_feat,) = call(
-        functools.partial(feature_kernel, rows), [slab], (order_row, weight, term, *terms), [pltpu.VMEM] * (2 + rows)
-    )
-    by_step = dict(zip(row_plan, terms))
-    weights = [chip_weight] + [by_step[step][B:] for step in range(1, rows)]
+        functools.partial(feature_kernel, rows), [slab], (order_row, weight, term, *terms), [pltpu.VMEM] * (rows + 2)
+    )
+    mine = terms[1][B:]
+    swapped = across(mine)
+    weights = [chip_weight, jnp.where(even, swapped, mine), jnp.where(even, mine, swapped)] + [t[B:] for t in terms[2:]]
     row_weight = sum_in_order(weights, r, rows).astype(BF)
     mine = along_depth(row_weight, (1, 2))
     rest = [along_depth(row_weight, (step, step)) for step in range(3, depth)]

time: 31.9 us -> 31.1 us (0.975)
  waiting for transfers between devices: 12.1 us -> 10 us
  starting transfers between devices: 13.2 us -> 14.6 us
    ppermute x8, waiting for transfers between devices: 9.47 us -> 7.35 us  [move(): return lax.ppermute(value, axes, pairs)]
    ppermute x8, starting transfers between devices: 11.5 us -> 12.8 us  [move(): return lax.ppermute(value, axes, pairs)]
    ppermute x7 -> x8, starting transfers between devices: 1.79 us -> 1.86 us  [across(): return lax.ppermute(value, 'col', [(i, i ^ 1) for i in range(cols)])]
    ppermute x7 -> x8, waiting for transfers between devices: 2.65 us -> 2.68 us  [across(): return lax.ppermute(value, 'col', [(i, i ^ 1) for i in range(cols)])]
  transfers between devices with their start and end apart: 15 -> 16, of which waited for: 11 -> 10; matrix products, arithmetic and copies ran while one was open for 4% -> 4% of each run, Pallas kernels for 3% -> 3%
where the time goes in v4:
time: 31.1 us; the launch traced here: 30.8 us
  starting transfers between devices  14.6 us (47%)
  waiting for transfers between devices  10 us (32%)
  other arithmetic  2.75 us (9%)
  Pallas kernels  2.04 us (7%)
  between operations  0.74 us (2%)
  local copies, waits for them, and re-layouts  0.67 us (2%)
    ppermute x8, starting transfers between devices, move(): return lax.ppermute(value, axes, pairs)  12.8 us
    ppermute x8, waiting for transfers between devices, move(): return lax.ppermute(value, axes, pairs)  7.35 us
    ppermute x8, waiting for transfers between devices, across(): return lax.ppermute(value, 'col', [(i, i ^ 1) for i in range(cols)])  2.68 us
    pallas_call x3, Pallas kernels, call(): pl.pallas_call(body, out_shape=outs, in_specs=[pl.BlockSpec(memory_space=...  2.04 us
    ppermute x8, starting transfers between devices, across(): return lax.ppermute(value, 'col', [(i, i ^ 1) for i in range(cols)])  1.86 us
    select_n x1, other arithmetic, shards(): jnp.where(filled.T[:, :, None, None], blocks[0, 0], jnp.zeros((), BF))  1.16 us
    select_n x1, other arithmetic, shards(): jnp.where(even, features, masked)  0.8 us
    unnamed x8, local copies, waits for them, and re-layouts  0.66 us
  transfers between devices with their start and end apart: 16, of which 10 were waited for; matrix products, arithmetic and copies ran while one was open for 4% of the time, Pallas kernels for 3%

profile of v4, /device:TPU:0, one launch (start us, length us, event | category | flops | bytes accessed | tf_op | source)
XLA Modules:
  0.0 30.8 jit_solution(555233437394280614)
XLA Ops:
  0.6 0.8 %broadcast_select_fusion = (bf16[128,128]{1,0:T(8,128)(2,1)S(1)}, bf16[128,128]{1,0:T(8,128)(2,1)S(1)}) fusion(bf16[128,128]{1,0:T(8,128)(2,1)} %param.14, pred[]{:T(512)S(6)} %eq.3, bf16[128,128]{1,0:T(8,128)(2,1)} %param.12, bf16[128,128]{1,0:T(8,128)(2,1)} %param.13), kind=kLoop, calls=%fused_computation.6 | loop fusion | flops 65536 | bytes 163841 | tf_op jit(solution)/shard_map/jit(_where)/select_n | solution.py:165
  1.4 0.6 %copy-done.1 = s32[128]{0:T(128)S(1)} copy-done((s32[128]{0:T(128)S(1)}, s32[128]{0:T(128)}, u32[]{:S(2)}) %copy-start.1) | copy-done | bytes 536
  2.3 0.5 %collective-permute-start = (bf16[128,128]{1,0:T(8,128)(2,1)S(1)}, bf16[128,128]{1,0:T(8,128)(2,1)S(1)}, u32[]{:S(2)}, u32[]{:S(2)}) collective-permute-start(bf16[128,128]{1,0:T(8,128)(2,1)S(1)} %get-tuple-element.39), channel_id=1, source_target_pairs={{0,1},{1,0},{2,3},{3,2},{4,5},{5,4},{6,7},{7,6},{8,9},{9,8},{10,11... | collective-permute-start | bytes 98312 | tf_op jit(solution)/shard_map/ppermute | solution.py:137
  2.8 0.9 %collective-permute-done = bf16[128,128]{1,0:T(8,128)(2,1)S(1)} collective-permute-done((bf16[128,128]{1,0:T(8,128)(2,1)S(1)}, bf16[128,128]{1,0:T(8,128)(2,1)S(1)}, u32[]{:S(2)}, u32[]{:S(2)}) %collective-permute-start) | collective-permute-done | bytes 32800 | tf_op jit(solution)/shard_map/ppermute | solution.py:137
  3.7 4.0 %collective-permute-start.3 = (bf16[256,128]{1,0:T(8,128)(2,1)S(1)}, bf16[256,128]{1,0:T(8,128)(2,1)S(1)}, u32[]{:S(2)}, u32[]{:S(2)}) collective-permute-start(bf16[256,128]{1,0:T(8,128)(2,1)S(1)} %pad_maximum_fusion.refs_2_), channel_id=1, source_target_pairs={{0,4},{1,17},{2,6},{3,19},{4,0},{5,21},{6,2},{7,23},{8,12},{9,25},... | collective-permute-start | bytes 196616 | tf_op jit(solution)/shard_map/ppermute | solution.py:147
  7.7 1.3 %collective-permute-start.2 = (bf16[256,128]{1,0:T(8,128)(2,1)S(1)}, bf16[256,128]{1,0:T(8,128)(2,1)S(1)}, u32[]{:S(2)}, u32[]{:S(2)}) collective-permute-start(bf16[256,128]{1,0:T(8,128)(2,1)S(1)} %pad_maximum_fusion.refs_2_), channel_id=1, source_target_pairs={{0,6},{1,25},{2,4},{3,27},{4,2},{5,29},{6,0},{7,31},{8,14},{9,17},... | collective-permute-start | bytes 196616 | tf_op jit(solution)/shard_map/ppermute | solution.py:147
  9.3 1.2 %bitcast_select_fusion.refs_1_ = bf16[8,2,128,128]{3,2,1,0:T(8,128)(2,1)S(1)} fusion(bf16[1,1,8,2,128,128]{5,4,3,2,1,0:T(8,128)(2,1)} %param.16, pred[8,2]{1,0:T(8,128)(4,1)S(1)} %iota_compare_fusion), kind=kLoop, calls=%fused_computation | loop fusion | flops 262144 | bytes 1048592 | tf_op jit(solution)/shard_map/jit(_where)/select_n | solution.py:171
  10.6 0.5 %collective-permute-start.7 = (bf16[256,128]{1,0:T(8,128)(2,1)S(1)}, bf16[256,128]{1,0:T(8,128)(2,1)S(1)}, u32[]{:S(2)}, u32[]{:S(2)}) collective-permute-start(bf16[256,128]{1,0:T(8,128)(2,1)S(1)} %collective-permute-done.3.refs_5_), channel_id=1, source_target_pairs={{0,1},{1,0},{2,3},{3,2},{4,5},{5,4},{6,7},{7,6},{8,9},{9,8},{10,11... | collective-permute-start | bytes 196616 | tf_op jit(solution)/shard_map/ppermute | solution.py:137
  11.1 2.7 %collective-permute-done.2.refs_4_ = bf16[256,128]{1,0:T(8,128)(2,1)S(1)} collective-permute-done((bf16[256,128]{1,0:T(8,128)(2,1)S(1)}, bf16[256,128]{1,0:T(8,128)(2,1)S(1)}, u32[]{:S(2)}, u32[]{:S(2)}) %collective-permute-start.2) | collective-permute-done | bytes 65568 | tf_op jit(solution)/shard_map/ppermute | solution.py:147
  14.0 0.4 %collective-permute-start.5 = (bf16[256,128]{1,0:T(8,128)(2,1)S(1)}, bf16[256,128]{1,0:T(8,128)(2,1)S(1)}, u32[]{:S(2)}, u32[]{:S(2)}) collective-permute-start(bf16[256,128]{1,0:T(8,128)(2,1)S(1)} %collective-permute-done.1.refs_3_), channel_id=1, source_target_pairs={{0,1},{1,0},{2,3},{3,2},{4,5},{5,4},{6,7},{7,6},{8,9},{9,8},{10,11... | collective-permute-start | bytes 196616 | tf_op jit(solution)/shard_map/ppermute | solution.py:137
  14.4 0.7 %collective-permute-done.6.refs_8_ = bf16[256,128]{1,0:T(8,128)(2,1)S(1)} collective-permute-done((bf16[256,128]{1,0:T(8,128)(2,1)S(1)}, bf16[256,128]{1,0:T(8,128)(2,1)S(1)}, u32[]{:S(2)}, u32[]{:S(2)}) %collective-permute-start.6) | collective-permute-done | bytes 65568 | tf_op jit(solution)/shard_map/ppermute | solution.py:137
  15.3 0.9 %shard_map.96 = (bf16[128,128]{1,0:T(8,128)(2,1)S(1)}, f32[128,128]{1,0:T(8,128)S(1)}, bf16[256,128]{1,0:T(8,128)(2,1)S(1)}, bf16[256,128]{1,0:T(8,128)(2,1)S(1)}, bf16[256,128]{1,0:T(8,128)(2,1)S(1)}) custom-call(s32[2,8]{1,0:T(2,128)S(1)} %compare_select_fusion.1.refs_0_, bf16[8,2,128,128]{3,2,1,0:T(8,128)(2,1)S(1)} %bitcast_select_fusion.refs_1_, ...), custom_call_target="tpu_custom_call" | custom-call | tf_op jit(solution)/shard_map/pallas_call | solution.py:38
  16.2 0.4 %collective-permute-start.9 = (f32[128,128]{1,0:T(8,128)S(1)}, f32[128,128]{1,0:T(8,128)S(1)}, u32[]{:S(2)}, u32[]{:S(2)}) collective-permute-start(f32[128,128]{1,0:T(8,128)S(1)} %get-tuple-element.48), channel_id=1, source_target_pairs={{0,1},{1,0},{2,3},{3,2},{4,5},{5,4},{6,7},{7,6},{8,9},{9,8},{10,11... | collective-permute-start | bytes 196616 | tf_op jit(solution)/shard_map/ppermute | solution.py:137
  16.6 0.9 %collective-permute-done.9 = f32[128,128]{1,0:T(8,128)S(1)} collective-permute-done((f32[128,128]{1,0:T(8,128)S(1)}, f32[128,128]{1,0:T(8,128)S(1)}, u32[]{:S(2)}, u32[]{:S(2)}) %collective-permute-start.9) | collective-permute-done | bytes 65568 | tf_op jit(solution)/shard_map/ppermute | solution.py:137
  17.6 1.6 %collective-permute-start.10 = (bf16[256,128]{1,0:T(8,128)(2,1)S(1)}, bf16[256,128]{1,0:T(8,128)(2,1)S(1)}, u32[]{:S(2)}, u32[]{:S(2)}) collective-permute-start(bf16[256,128]{1,0:T(8,128)(2,1)S(1)} %constant_dynamic-update-slice_fusion.1), channel_id=1, source_target_pairs={{0,16},{1,9},{2,18},{3,11},{4,20},{5,13},{6,22},{7,15},{8,24},{9,1... | collective-permute-start | bytes 196616 | tf_op jit(solution)/shard_map/ppermute | solution.py:147
  19.1 1.4 %collective-permute-start.11 = (bf16[256,128]{1,0:T(8,128)(2,1)S(1)}, bf16[256,128]{1,0:T(8,128)(2,1)S(1)}, u32[]{:S(2)}, u32[]{:S(2)}) collective-permute-start(bf16[256,128]{1,0:T(8,128)(2,1)S(1)} %get-tuple-element.50), channel_id=1, source_target_pairs={{0,24},{1,25},{2,26},{3,27},{4,28},{5,29},{6,30},{7,31},{8,16},{9,... | collective-permute-start | bytes 196616 | tf_op jit(solution)/shard_map/ppermute | solution.py:147
  20.6 1.3 %collective-permute-done.10.refs_2_ = bf16[256,128]{1,0:T(8,128)(2,1)S(1)} collective-permute-done((bf16[256,128]{1,0:T(8,128)(2,1)S(1)}, bf16[256,128]{1,0:T(8,128)(2,1)S(1)}, u32[]{:S(2)}, u32[]{:S(2)}) %collective-permute-start.10) | collective-permute-done | bytes 65568 | tf_op jit(solution)/shard_map/ppermute | solution.py:147
  21.9 1.6 %collective-permute-start.8 = (bf16[256,128]{1,0:T(8,128)(2,1)S(1)}, bf16[256,128]{1,0:T(8,128)(2,1)S(1)}, u32[]{:S(2)}, u32[]{:S(2)}) collective-permute-start(bf16[256,128]{1,0:T(8,128)(2,1)S(1)} %get-tuple-element.46), channel_id=1, source_target_pairs={{0,8},{1,17},{2,10},{3,19},{4,12},{5,21},{6,14},{7,23},{8,0},{9,25... | collective-permute-start | bytes 196616 | tf_op jit(solution)/shard_map/ppermute | solution.py:147
  23.5 0.8 %collective-permute-done.11.refs_3_ = bf16[256,128]{1,0:T(8,128)(2,1)S(1)} collective-permute-done((bf16[256,128]{1,0:T(8,128)(2,1)S(1)}, bf16[256,128]{1,0:T(8,128)(2,1)S(1)}, u32[]{:S(2)}, u32[]{:S(2)}) %collective-permute-start.11) | collective-permute-done | bytes 65568 | tf_op jit(solution)/shard_map/ppermute | solution.py:147
  24.4 2.6 %collective-permute-start.15 = (bf16[128,128]{1,0:T(8,128)(2,1)S(1)}, bf16[128,128]{1,0:T(8,128)(2,1)S(1)}, u32[]{:S(2)}, u32[]{:S(2)}) collective-permute-start(bf16[128,128]{1,0:T(8,128)(2,1)S(1)} %add_convert_fusion), channel_id=1, source_target_pairs={{0,6},{1,7},{2,4},{3,5},{4,2},{5,3},{6,0},{7,1},{8,14},{9,15},{10,... | collective-permute-start | bytes 98312 | tf_op jit(solution)/shard_map/ppermute | solution.py:147
  27.0 1.3 %collective-permute-done.13 = bf16[128,128]{1,0:T(8,128)(2,1)S(1)} collective-permute-done((bf16[128,128]{1,0:T(8,128)(2,1)S(1)}, bf16[128,128]{1,0:T(8,128)(2,1)S(1)}, u32[]{:S(2)}, u32[]{:S(2)}) %collective-permute-start.13) | collective-permute-done | bytes 32800 | tf_op jit(solution)/shard_map/ppermute | solution.py:147
  28.3 0.9 %shard_map.97 = bf16[128,128]{1,0:T(8,128)(2,1)} custom-call(s32[1,128]{1,0:T(1,128)S(1)} %bitcast.9, bf16[128,128]{1,0:T(8,128)(2,1)S(1)} %copy-done, bf16[128,128]{1,0:T(8,128)(2,1)S(1)} %get-tuple-element.45.refs_0_, bf16[256,128]{1,0:T(8,128)(2,1)S(1)} %collective-permute-done.8.refs_1_, bf16[256,128]{1,0:T(8,128)(2,1)S(1)} %collective-permute-done.10.refs_2_, ...), custom_call_target="tpu_custom_call" | custom-call | tf_op jit(solution)/shard_map/pallas_call | solution.py:38
  29.2 1.0 %collective-permute-done.15 = bf16[128,128]{1,0:T(8,128)(2,1)S(1)} collective-permute-done((bf16[128,128]{1,0:T(8,128)(2,1)S(1)}, bf16[128,128]{1,0:T(8,128)(2,1)S(1)}, u32[]{:S(2)}, u32[]{:S(2)}) %collective-permute-start.15) | collective-permute-done | bytes 32800 | tf_op jit(solution)/shard_map/ppermute | solution.py:147
  30.2 0.7 %add_multiply_fusion = f32[128,128]{1,0:T(8,128)} fusion(bf16[128,128]{1,0:T(8,128)(2,1)S(1)} %collective-permute-done.15, bf16[128,128]{1,0:T(8,128)(2,1)S(1)} %add_convert_fusion, bf16[128,128]{1,0:T(8,128)(2,1)S(1)} %collective-permute-done.14, bf16[128,128]{1,0:T(8,128)(2,1)S(1)} %collective-permute-done.13, pred[]{:T(512)S(6)} %eq.3), kind=kLoop, calls=%fused_computation.2 | loop fusion | flops 163840 | bytes 196609 | tf_op jit(solution)/shard_map/mul | solution.py:205
  (29 shorter events, 1.0 us)
Async XLA Ops:
  1.4 0.7 %copy-start.1 = (s32[128]{0:T(128)S(1)}, s32[128]{0:T(128)}, u32[]{:S(2)}) copy-start(s32[128]{0:T(128)} %param.19) | copy-start | bytes 1540
  2.3 1.4 %collective-permute-start = (bf16[128,128]{1,0:T(8,128)(2,1)S(1)}, bf16[128,128]{1,0:T(8,128)(2,1)S(1)}, u32[]{:S(2)}, u32[]{:S(2)}) collective-permute-start(bf16[128,128]{1,0:T(8,128)(2,1)S(1)} %get-tuple-element.39), channel_id=1, source_target_pairs={{0,1},{1,0},{2,3},{3,2},{4,5},{5,4},{6,7},{7,6},{8,9},{9,8},{10,11... | collective-permute-start | bytes 98312 | tf_op jit(solution)/shard_map/ppermute | solution.py:137
  3.7 5.6 %copy-start.3 = (s32[1,1,8]{2,1,0:T(1,128)S(1)}, s32[1,1,8]{2,1,0:T(1,128)}, u32[]{:S(2)}) copy-start(s32[1,1,8]{2,1,0:T(1,128)} %param.18) | copy-start | bytes 100
  3.7 6.9 %collective-permute-start.3 = (bf16[256,128]{1,0:T(8,128)(2,1)S(1)}, bf16[256,128]{1,0:T(8,128)(2,1)S(1)}, u32[]{:S(2)}, u32[]{:S(2)}) collective-permute-start(bf16[256,128]{1,0:T(8,128)(2,1)S(1)} %pad_maximum_fusion.refs_2_), channel_id=1, source_target_pairs={{0,4},{1,17},{2,6},{3,19},{4,0},{5,21},{6,2},{7,23},{8,12},{9,25},... | collective-permute-start | bytes 196616 | tf_op jit(solution)/shard_map/ppermute | solution.py:147
  7.7 6.2 %collective-permute-start.2 = (bf16[256,128]{1,0:T(8,128)(2,1)S(1)}, bf16[256,128]{1,0:T(8,128)(2,1)S(1)}, u32[]{:S(2)}, u32[]{:S(2)}) collective-permute-start(bf16[256,128]{1,0:T(8,128)(2,1)S(1)} %pad_maximum_fusion.refs_2_), channel_id=1, source_target_pairs={{0,6},{1,25},{2,4},{3,27},{4,2},{5,29},{6,0},{7,31},{8,14},{9,17},... | collective-permute-start | bytes 196616 | tf_op jit(solution)/shard_map/ppermute | solution.py:147
  9.0 5.0 %collective-permute-start.1 = (bf16[256,128]{1,0:T(8,128)(2,1)S(1)}, bf16[256,128]{1,0:T(8,128)(2,1)S(1)}, u32[]{:S(2)}, u32[]{:S(2)}) collective-permute-start(bf16[256,128]{1,0:T(8,128)(2,1)S(1)} %pad_maximum_fusion.refs_2_), channel_id=1, source_target_pairs={{0,2},{1,9},{2,0},{3,11},{4,6},{5,13},{6,4},{7,15},{8,10},{9,1},{1... | collective-permute-start | bytes 196616 | tf_op jit(solution)/shard_map/ppermute | solution.py:147
  9.3 1.2 %copy-start.2 = (s32[1,1,8,2]{2,3,1,0:T(2,128)S(1)}, s32[1,1,8,2]{2,3,1,0:T(2,128)}, u32[]{:S(2)}) copy-start(s32[1,1,8,2]{2,3,1,0:T(2,128)} %param.17) | copy-start | bytes 196
  10.5 3.8 %collective-permute-start.4 = (bf16[256,128]{1,0:T(8,128)(2,1)S(1)}, bf16[256,128]{1,0:T(8,128)(2,1)S(1)}, u32[]{:S(2)}, u32[]{:S(2)}) collective-permute-start(bf16[256,128]{1,0:T(8,128)(2,1)S(1)} %pad_maximum_fusion.refs_2_), channel_id=1, source_target_pairs={{0,1},{1,0},{2,3},{3,2},{4,5},{5,4},{6,7},{7,6},{8,9},{9,8},{10,11... | collective-permute-start | bytes 196616 | tf_op jit(solution)/shard_map/ppermute | solution.py:137
  10.6 3.8 %collective-permute-start.7 = (bf16[256,128]{1,0:T(8,128)(2,1)S(1)}, bf16[256,128]{1,0:T(8,128)(2,1)S(1)}, u32[]{:S(2)}, u32[]{:S(2)}) collective-permute-start(bf16[256,128]{1,0:T(8,128)(2,1)S(1)} %collective-permute-done.3.refs_5_), channel_id=1, source_target_pairs={{0,1},{1,0},{2,3},{3,2},{4,5},{5,4},{6,7},{7,6},{8,9},{9,8},{10,11... | collective-permute-start | bytes 196616 | tf_op jit(solution)/shard_map/ppermute | solution.py:137
  13.8 1.3 %collective-permute-start.6 = (bf16[256,128]{1,0:T(8,128)(2,1)S(1)}, bf16[256,128]{1,0:T(8,128)(2,1)S(1)}, u32[]{:S(2)}, u32[]{:S(2)}) collective-permute-start(bf16[256,128]{1,0:T(8,128)(2,1)S(1)} %collective-permute-done.2.refs_4_), channel_id=1, source_target_pairs={{0,1},{1,0},{2,3},{3,2},{4,5},{5,4},{6,7},{7,6},{8,9},{9,8},{10,11... | collective-permute-start | bytes 196616 | tf_op jit(solution)/shard_map/ppermute | solution.py:137
  14.0 1.3 %collective-permute-start.5 = (bf16[256,128]{1,0:T(8,128)(2,1)S(1)}, bf16[256,128]{1,0:T(8,128)(2,1)S(1)}, u32[]{:S(2)}, u32[]{:S(2)}) collective-permute-start(bf16[256,128]{1,0:T(8,128)(2,1)S(1)} %collective-permute-done.1.refs_3_), channel_id=1, source_target_pairs={{0,1},{1,0},{2,3},{3,2},{4,5},{5,4},{6,7},{7,6},{8,9},{9,8},{10,11... | collective-permute-start | bytes 196616 | tf_op jit(solution)/shard_map/ppermute | solution.py:137
  16.2 1.3 %collective-permute-start.9 = (f32[128,128]{1,0:T(8,128)S(1)}, f32[128,128]{1,0:T(8,128)S(1)}, u32[]{:S(2)}, u32[]{:S(2)}) collective-permute-start(f32[128,128]{1,0:T(8,128)S(1)} %get-tuple-element.48), channel_id=1, source_target_pairs={{0,1},{1,0},{2,3},{3,2},{4,5},{5,4},{6,7},{7,6},{8,9},{9,8},{10,11... | collective-permute-start | bytes 196616 | tf_op jit(solution)/shard_map/ppermute | solution.py:137
  17.6 4.3 %collective-permute-start.10 = (bf16[256,128]{1,0:T(8,128)(2,1)S(1)}, bf16[256,128]{1,0:T(8,128)(2,1)S(1)}, u32[]{:S(2)}, u32[]{:S(2)}) collective-permute-start(bf16[256,128]{1,0:T(8,128)(2,1)S(1)} %constant_dynamic-update-slice_fusion.1), channel_id=1, source_target_pairs={{0,16},{1,9},{2,18},{3,11},{4,20},{5,13},{6,22},{7,15},{8,24},{9,1... | collective-permute-start | bytes 196616 | tf_op jit(solution)/shard_map/ppermute | solution.py:147
  19.1 5.2 %collective-permute-start.11 = (bf16[256,128]{1,0:T(8,128)(2,1)S(1)}, bf16[256,128]{1,0:T(8,128)(2,1)S(1)}, u32[]{:S(2)}, u32[]{:S(2)}) collective-permute-start(bf16[256,128]{1,0:T(8,128)(2,1)S(1)} %get-tuple-element.50), channel_id=1, source_target_pairs={{0,24},{1,25},{2,26},{3,27},{4,28},{5,29},{6,30},{7,31},{8,16},{9,... | collective-permute-start | bytes 196616 | tf_op jit(solution)/shard_map/ppermute | solution.py:147
  21.9 2.4 %collective-permute-start.12 = (bf16[128,128]{1,0:T(8,128)(2,1)S(1)}, bf16[128,128]{1,0:T(8,128)(2,1)S(1)}, u32[]{:S(2)}, u32[]{:S(2)}) collective-permute-start(bf16[128,128]{1,0:T(8,128)(2,1)S(1)} %slice.42), channel_id=1, source_target_pairs={{0,1},{1,0},{2,3},{3,2},{4,5},{5,4},{6,7},{7,6},{8,9},{9,8},{10,11... | collective-permute-start | bytes 98312 | tf_op jit(solution)/shard_map/ppermute | solution.py:137
  21.9 6.4 %copy-start = (bf16[128,128]{1,0:T(8,128)(2,1)S(1)}, bf16[128,128]{1,0:T(8,128)(2,1)}, u32[]{:S(2)}) copy-start(bf16[128,128]{1,0:T(8,128)(2,1)} %weight_ref.1) | copy-start | bytes 98308
  21.9 6.4 %collective-permute-start.8 = (bf16[256,128]{1,0:T(8,128)(2,1)S(1)}, bf16[256,128]{1,0:T(8,128)(2,1)S(1)}, u32[]{:S(2)}, u32[]{:S(2)}) collective-permute-start(bf16[256,128]{1,0:T(8,128)(2,1)S(1)} %get-tuple-element.46), channel_id=1, source_target_pairs={{0,8},{1,17},{2,10},{3,19},{4,12},{5,21},{6,14},{7,23},{8,0},{9,25... | collective-permute-start | bytes 196616 | tf_op jit(solution)/shard_map/ppermute | solution.py:147
  24.3 4.0 %collective-permute-start.13 = (bf16[128,128]{1,0:T(8,128)(2,1)S(1)}, bf16[128,128]{1,0:T(8,128)(2,1)S(1)}, u32[]{:S(2)}, u32[]{:S(2)}) collective-permute-start(bf16[128,128]{1,0:T(8,128)(2,1)S(1)} %add_convert_fusion), channel_id=1, source_target_pairs={{0,2},{1,5},{2,0},{3,7},{4,6},{5,1},{6,4},{7,3},{8,10},{9,13},{10,... | collective-permute-start | bytes 98312 | tf_op jit(solution)/shard_map/ppermute | solution.py:147
  24.4 5.8 %collective-permute-start.15 = (bf16[128,128]{1,0:T(8,128)(2,1)S(1)}, bf16[128,128]{1,0:T(8,128)(2,1)S(1)}, u32[]{:S(2)}, u32[]{:S(2)}) collective-permute-start(bf16[128,128]{1,0:T(8,128)(2,1)S(1)} %add_convert_fusion), channel_id=1, source_target_pairs={{0,6},{1,7},{2,4},{3,5},{4,2},{5,3},{6,0},{7,1},{8,14},{9,15},{10,... | collective-permute-start | bytes 98312 | tf_op jit(solution)/shard_map/ppermute | solution.py:147
  28.3 1.9 %collective-permute-start.14 = (bf16[128,128]{1,0:T(8,128)(2,1)S(1)}, bf16[128,128]{1,0:T(8,128)(2,1)S(1)}, u32[]{:S(2)}, u32[]{:S(2)}) collective-permute-start(bf16[128,128]{1,0:T(8,128)(2,1)S(1)} %collective-permute-done.13), channel_id=1, source_target_pairs={{0,1},{1,0},{2,3},{3,2},{4,5},{5,4},{6,7},{7,6},{8,9},{9,8},{10,11... | collective-permute-start | bytes 98312 | tf_op jit(solution)/shard_map/ppermute | solution.py:137

commit v5 on v4

--- a/solution.py
+++ b/solution.py
@@ -2,6 +2,7 @@
 
 import jax
 import jax.numpy as jnp
+import numpy as np
 from jax import lax
 from jax.experimental import pallas as pl
 from jax.experimental.pallas import tpu as pltpu
@@ -43,17 +44,6 @@
         scratch_shapes=list(scratch),
         compiler_params=pltpu.CompilerParams(vmem_limit_bytes=limit),
     )(*args)
-
-
-def spread(order_row):
-    n = order_row.shape[1]
-    return (lax.broadcasted_iota(jnp.int32, (n, n), 0) == order_row).astype(BF)
-
-
-def first_kernel(order_ref, keep_ref, give_ref, keep_out, give_out):
-    place = spread(order_ref[...])
-    keep_out[...] = dot(place, keep_ref[...], ((0,), (0,))).astype(BF)
-    give_out[...] = dot(place, give_ref[...], ((0,), (0,))).astype(BF)
 
 
 def row_steps(rows):
@@ -111,13 +101,13 @@
     return functools.reduce(lambda a, b: a + b, [held[i] for i in range(size)])
 
 
-def feature_kernel(count, order_ref, weight_ref, *refs):
+def feature_kernel(count, place_ref, weight_ref, *refs):
     terms, out_ref = refs[:count], refs[count]
     total = terms[0][0:B].astype(F32)
     for term in terms[1:]:
         total += term[0:B].astype(F32)
     grad = dot(total.astype(BF), weight_ref[...], ((1,), (1,))).astype(BF)
-    out_ref[...] = dot(spread(order_ref[...]), grad, ((1,), (0,))).astype(BF)
+    out_ref[...] = dot(place_ref[...], grad, ((0,), (0,))).astype(BF)
 
 
 def shards(grad_out, pre_act, features, weight, blocks, block_cols, block_counts, order):
@@ -128,7 +118,6 @@
     axes = ("row", "col")
     r, c = lax.axis_index("row"), lax.axis_index("col")
     z, even = lax.div(c, 2), lax.rem(c, 2) == 0
-    order_row = order.reshape(1, slab_rows)
     slab = jax.ShapeDtypeStruct((B, F), BF)
     pair = jax.ShapeDtypeStruct((2 * B, F), BF)
     limit = (4 << 20) + 8 * blocks.size
@@ -161,10 +150,13 @@
 
         return move(value, row_of, depth_of)
 
-    masked = jnp.where(pre_act > 0, grad_out, jnp.zeros_like(grad_out))
-    keep, give = jnp.where(even, masked, features), jnp.where(even, features, masked)
-    keep, give = call(first_kernel, [slab, slab], (order_row, keep, give), [pltpu.VMEM] * 3)
-    message = jnp.concatenate([keep, across(give)], axis=0)
+    nodes = lax.broadcasted_iota(jnp.int32, (slab_rows, slab_rows), 0)
+    unit = jnp.asarray(np.eye(slab_rows), BF)
+    values = jnp.concatenate([grad_out, pre_act, features, unit], axis=1)
+    placed = dot((nodes == order[None, :]).astype(BF), values, ((0,), (0,))).astype(BF)
+    grad, pre, feat, place = [placed[:, i * F : (i + 1) * F] for i in range(4)]
+    masked = jnp.where(pre > 0, grad, jnp.zeros_like(grad))
+    message = jnp.concatenate([jnp.where(even, masked, feat), across(jnp.where(even, feat, masked))], axis=0)
     message, counts = lax.optimization_barrier((message, block_counts))
     filled = jnp.arange(K, dtype=jnp.int32)[:, None] < counts[0, 0][None, :]
     targets = jnp.where(filled, block_cols[0, 0].T, 0)
@@ -191,7 +183,7 @@
     terms = [along_row(messages[0], plan[0])]
     terms += [along_row(m.at[B:].set(chip_weight), plan[i]) for i, m in enumerate(messages) if i > 0]
     (grad_feat,) = call(
-        functools.partial(feature_kernel, rows), [slab], (order_row, weight, term, *terms), [pltpu.VMEM] * (rows + 2)
+        functools.partial(feature_kernel, rows), [slab], (place, weight, term, *terms), [pltpu.VMEM] * (rows + 2)
     )
     mine = terms[1][B:]
     swapped = across(mine)

time: 31.1 us -> 30.5 us (0.981)
  other arithmetic: 2.75 us -> 0.9 us
  matrix products: 0 us -> 1.11 us
  waiting for transfers between devices: 10 us -> 10.6 us
    dot_general x0 -> x1, matrix products: none -> 1.11 us  [dot(): lax.dot_general(a, b, (contract, ((), ())), preferred_element_type=F32)]
    select_n x1, other arithmetic: 1.16 us -> 0.1 us  [shards(): jnp.where(filled.T[:, :, None, None], blocks[0, 0], jnp.zeros((), BF))]
    select_n x1, other arithmetic: 0.8 us -> 0.01 us  [shards(): jnp.where(even, masked, feat)]
    ppermute x8, waiting for transfers between devices: 7.35 us -> 7.92 us  [move(): return lax.ppermute(value, axes, pairs)]
    pallas_call x3 -> x2, Pallas kernels: 2.04 us -> 1.84 us  [call(): pl.pallas_call(body, out_shape=outs, in_specs=[pl.BlockSpec(memory_space=...]
  transfers between devices with their start and end apart: 16 -> 16, of which waited for: 10 -> 10; matrix products, arithmetic and copies ran while one was open for 4% -> 1% of each run, Pallas kernels for 3% -> 3%
where the time goes in v5:
time: 30.5 us; the launch traced here: 30.4 us
  starting transfers between devices  14.6 us (48%)
  waiting for transfers between devices  10.6 us (35%)
  Pallas kernels  1.84 us (6%)
  matrix products  1.11 us (4%)
  other arithmetic  0.9 us (3%)
  between operations  0.73 us (2%)
  local copies, waits for them, and re-layouts  0.59 us (2%)
    ppermute x8, starting transfers between devices, move(): return lax.ppermute(value, axes, pairs)  12.8 us
    ppermute x8, waiting for transfers between devices, move(): return lax.ppermute(value, axes, pairs)  7.92 us
    ppermute x8, waiting for transfers between devices, across(): return lax.ppermute(value, 'col', [(i, i ^ 1) for i in range(cols)])  2.67 us
    pallas_call x2, Pallas kernels, call(): pl.pallas_call(body, out_shape=outs, in_specs=[pl.BlockSpec(memory_space=...  1.84 us
    ppermute x8, starting transfers between devices, across(): return lax.ppermute(value, 'col', [(i, i ^ 1) for i in range(cols)])  1.81 us
    dot_general x1, matrix products, dot(): lax.dot_general(a, b, (contract, ((), ())), preferred_element_type=F32)  1.11 us
    mul x1, other arithmetic, shards(): return (grad_feat, summed * (slab_rows * rows * cols) ** (-0.5))  0.66 us
  transfers between devices with their start and end apart: 16, of which 10 were waited for; matrix products, arithmetic and copies ran while one was open for 1% of the time, Pallas kernels for 3%

profile of v5, /device:TPU:0, one launch (start us, length us, event | category | flops | bytes accessed | tf_op | source)
XLA Modules:
  0.0 30.4 jit_solution(14724306860151502567)
XLA Ops:
  0.6 1.1 %convolution_convert_fusion = bf16[128,512]{1,0:T(8,128)(2,1)S(1)} fusion(bf16[128,128]{1,0:T(8,128)(2,1)} %constant.65.clone, bf16[128,128]{1,0:T(8,128)(2,1)} %param.15, bf16[128,128]{1,0:T(8,128)(2,1)} %param.14, bf16[128,128]{1,0:T(8,128)(2,1)} %param.13, s32[128]{0:T(128)} %param.20), kind=kOutput, calls=%fused_computation | convolution fusion | flops 17383424 | bytes 262656 | tf_op jit(solution)/shard_map/dot_general | solution.py:35
  1.8 0.5 %collective-permute-start = (bf16[128,128]{1,0:T(8,128)(2,1)S(1)}, bf16[128,128]{1,0:T(8,128)(2,1)S(1)}, u32[]{:S(2)}, u32[]{:S(2)}) collective-permute-start(bf16[128,128]{1,0:T(8,128)(2,1)S(1)} %get-tuple-element.50), channel_id=1, source_target_pairs={{0,1},{1,0},{2,3},{3,2},{4,5},{5,4},{6,7},{7,6},{8,9},{9,8},{10,11... | collective-permute-start | bytes 98312 | tf_op jit(solution)/shard_map/ppermute | solution.py:126
  2.3 0.9 %collective-permute-done = bf16[128,128]{1,0:T(8,128)(2,1)S(1)} collective-permute-done((bf16[128,128]{1,0:T(8,128)(2,1)S(1)}, bf16[128,128]{1,0:T(8,128)(2,1)S(1)}, u32[]{:S(2)}, u32[]{:S(2)}) %collective-permute-start) | collective-permute-done | bytes 32800 | tf_op jit(solution)/shard_map/ppermute | solution.py:126
  3.2 4.0 %collective-permute-start.3 = (bf16[256,128]{1,0:T(8,128)(2,1)S(1)}, bf16[256,128]{1,0:T(8,128)(2,1)S(1)}, u32[]{:S(2)}, u32[]{:S(2)}) collective-permute-start(bf16[256,128]{1,0:T(8,128)(2,1)S(1)} %pad_maximum_fusion.refs_2_), channel_id=1, source_target_pairs={{0,4},{1,17},{2,6},{3,19},{4,0},{5,21},{6,2},{7,23},{8,12},{9,25},... | collective-permute-start | bytes 196616 | tf_op jit(solution)/shard_map/ppermute | solution.py:136
  7.2 1.3 %collective-permute-start.2 = (bf16[256,128]{1,0:T(8,128)(2,1)S(1)}, bf16[256,128]{1,0:T(8,128)(2,1)S(1)}, u32[]{:S(2)}, u32[]{:S(2)}) collective-permute-start(bf16[256,128]{1,0:T(8,128)(2,1)S(1)} %pad_maximum_fusion.refs_2_), channel_id=1, source_target_pairs={{0,6},{1,25},{2,4},{3,27},{4,2},{5,29},{6,0},{7,31},{8,14},{9,17},... | collective-permute-start | bytes 196616 | tf_op jit(solution)/shard_map/ppermute | solution.py:136
  8.5 0.2 collective-permute-start.1
  8.9 0.6 %copy-done.2 = s32[1,1,8,2]{2,3,1,0:T(2,128)S(1)} copy-done((s32[1,1,8,2]{2,3,1,0:T(2,128)S(1)}, s32[1,1,8,2]{2,3,1,0:T(2,128)}, u32[]{:S(2)}) %copy-start.2) | copy-done | bytes 88
  9.5 0.5 %collective-permute-start.7 = (bf16[256,128]{1,0:T(8,128)(2,1)S(1)}, bf16[256,128]{1,0:T(8,128)(2,1)S(1)}, u32[]{:S(2)}, u32[]{:S(2)}) collective-permute-start(bf16[256,128]{1,0:T(8,128)(2,1)S(1)} %collective-permute-done.3.refs_5_), channel_id=1, source_target_pairs={{0,1},{1,0},{2,3},{3,2},{4,5},{5,4},{6,7},{7,6},{8,9},{9,8},{10,11... | collective-permute-start | bytes 196616 | tf_op jit(solution)/shard_map/ppermute | solution.py:126
  10.0 3.3 %collective-permute-done.2.refs_4_ = bf16[256,128]{1,0:T(8,128)(2,1)S(1)} collective-permute-done((bf16[256,128]{1,0:T(8,128)(2,1)S(1)}, bf16[256,128]{1,0:T(8,128)(2,1)S(1)}, u32[]{:S(2)}, u32[]{:S(2)}) %collective-permute-start.2) | collective-permute-done | bytes 65568 | tf_op jit(solution)/shard_map/ppermute | solution.py:136
  13.5 0.4 %collective-permute-start.5 = (bf16[256,128]{1,0:T(8,128)(2,1)S(1)}, bf16[256,128]{1,0:T(8,128)(2,1)S(1)}, u32[]{:S(2)}, u32[]{:S(2)}) collective-permute-start(bf16[256,128]{1,0:T(8,128)(2,1)S(1)} %collective-permute-done.1.refs_3_), channel_id=1, source_target_pairs={{0,1},{1,0},{2,3},{3,2},{4,5},{5,4},{6,7},{7,6},{8,9},{9,8},{10,11... | collective-permute-start | bytes 196616 | tf_op jit(solution)/shard_map/ppermute | solution.py:126
  13.9 0.7 %collective-permute-done.6.refs_8_ = bf16[256,128]{1,0:T(8,128)(2,1)S(1)} collective-permute-done((bf16[256,128]{1,0:T(8,128)(2,1)S(1)}, bf16[256,128]{1,0:T(8,128)(2,1)S(1)}, u32[]{:S(2)}, u32[]{:S(2)}) %collective-permute-start.6) | collective-permute-done | bytes 65568 | tf_op jit(solution)/shard_map/ppermute | solution.py:126
  14.8 0.9 %shard_map.104 = (bf16[128,128]{1,0:T(8,128)(2,1)S(1)}, f32[128,128]{1,0:T(8,128)S(1)}, bf16[256,128]{1,0:T(8,128)(2,1)S(1)}, bf16[256,128]{1,0:T(8,128)(2,1)S(1)}, bf16[256,128]{1,0:T(8,128)(2,1)S(1)}) custom-call(s32[2,8]{1,0:T(2,128)S(1)} %compare_select_fusion.1.refs_0_, bf16[8,2,128,128]{3,2,1,0:T(8,128)(2,1)S(1)} %bitcast_select_fusion.refs_1_, ...), custom_call_target="tpu_custom_call" | custom-call | tf_op jit(solution)/shard_map/pallas_call | solution.py:39
  15.7 0.4 %collective-permute-start.9 = (f32[128,128]{1,0:T(8,128)S(1)}, f32[128,128]{1,0:T(8,128)S(1)}, u32[]{:S(2)}, u32[]{:S(2)}) collective-permute-start(f32[128,128]{1,0:T(8,128)S(1)} %get-tuple-element.44), channel_id=1, source_target_pairs={{0,1},{1,0},{2,3},{3,2},{4,5},{5,4},{6,7},{7,6},{8,9},{9,8},{10,11... | collective-permute-start | bytes 196616 | tf_op jit(solution)/shard_map/ppermute | solution.py:126
  16.1 0.9 %collective-permute-done.9 = f32[128,128]{1,0:T(8,128)S(1)} collective-permute-done((f32[128,128]{1,0:T(8,128)S(1)}, f32[128,128]{1,0:T(8,128)S(1)}, u32[]{:S(2)}, u32[]{:S(2)}) %collective-permute-start.9) | collective-permute-done | bytes 65568 | tf_op jit(solution)/shard_map/ppermute | solution.py:126
  17.0 1.6 %collective-permute-start.10 = (bf16[256,128]{1,0:T(8,128)(2,1)S(1)}, bf16[256,128]{1,0:T(8,128)(2,1)S(1)}, u32[]{:S(2)}, u32[]{:S(2)}) collective-permute-start(bf16[256,128]{1,0:T(8,128)(2,1)S(1)} %constant_dynamic-update-slice_fusion.1), channel_id=1, source_target_pairs={{0,16},{1,9},{2,18},{3,11},{4,20},{5,13},{6,22},{7,15},{8,24},{9,1... | collective-permute-start | bytes 196616 | tf_op jit(solution)/shard_map/ppermute | solution.py:136
  18.6 1.4 %collective-permute-start.11 = (bf16[256,128]{1,0:T(8,128)(2,1)S(1)}, bf16[256,128]{1,0:T(8,128)(2,1)S(1)}, u32[]{:S(2)}, u32[]{:S(2)}) collective-permute-start(bf16[256,128]{1,0:T(8,128)(2,1)S(1)} %get-tuple-element.46), channel_id=1, source_target_pairs={{0,24},{1,25},{2,26},{3,27},{4,28},{5,29},{6,30},{7,31},{8,16},{9,... | collective-permute-start | bytes 196616 | tf_op jit(solution)/shard_map/ppermute | solution.py:136
  20.1 1.3 %collective-permute-done.10.refs_2_ = bf16[256,128]{1,0:T(8,128)(2,1)S(1)} collective-permute-done((bf16[256,128]{1,0:T(8,128)(2,1)S(1)}, bf16[256,128]{1,0:T(8,128)(2,1)S(1)}, u32[]{:S(2)}, u32[]{:S(2)}) %collective-permute-start.10) | collective-permute-done | bytes 65568 | tf_op jit(solution)/shard_map/ppermute | solution.py:136
  21.4 1.6 %collective-permute-start.8 = (bf16[256,128]{1,0:T(8,128)(2,1)S(1)}, bf16[256,128]{1,0:T(8,128)(2,1)S(1)}, u32[]{:S(2)}, u32[]{:S(2)}) collective-permute-start(bf16[256,128]{1,0:T(8,128)(2,1)S(1)} %get-tuple-element.42), channel_id=1, source_target_pairs={{0,8},{1,17},{2,10},{3,19},{4,12},{5,21},{6,14},{7,23},{8,0},{9,25... | collective-permute-start | bytes 196616 | tf_op jit(solution)/shard_map/ppermute | solution.py:136
  23.0 0.8 %collective-permute-done.11.refs_3_ = bf16[256,128]{1,0:T(8,128)(2,1)S(1)} collective-permute-done((bf16[256,128]{1,0:T(8,128)(2,1)S(1)}, bf16[256,128]{1,0:T(8,128)(2,1)S(1)}, u32[]{:S(2)}, u32[]{:S(2)}) %collective-permute-start.11) | collective-permute-done | bytes 65568 | tf_op jit(solution)/shard_map/ppermute | solution.py:136
  23.9 2.5 %collective-permute-start.15 = (bf16[128,128]{1,0:T(8,128)(2,1)S(1)}, bf16[128,128]{1,0:T(8,128)(2,1)S(1)}, u32[]{:S(2)}, u32[]{:S(2)}) collective-permute-start(bf16[128,128]{1,0:T(8,128)(2,1)S(1)} %add_convert_fusion), channel_id=1, source_target_pairs={{0,6},{1,7},{2,4},{3,5},{4,2},{5,3},{6,0},{7,1},{8,14},{9,15},{10,... | collective-permute-start | bytes 98312 | tf_op jit(solution)/shard_map/ppermute | solution.py:136
  26.5 1.4 %collective-permute-done.13 = bf16[128,128]{1,0:T(8,128)(2,1)S(1)} collective-permute-done((bf16[128,128]{1,0:T(8,128)(2,1)S(1)}, bf16[128,128]{1,0:T(8,128)(2,1)S(1)}, u32[]{:S(2)}, u32[]{:S(2)}) %collective-permute-start.13) | collective-permute-done | bytes 32800 | tf_op jit(solution)/shard_map/ppermute | solution.py:136
  27.8 0.9 %shard_map.105 = bf16[128,128]{1,0:T(8,128)(2,1)} custom-call(bf16[128,128]{1,0:T(8,128)(2,1)S(1)} %get-tuple-element.49.place_ref, bf16[128,128]{1,0:T(8,128)(2,1)S(1)} %copy-done, bf16[128,128]{1,0:T(8,128)(2,1)S(1)} %get-tuple-element.41.refs_0_, bf16[256,128]{1,0:T(8,128)(2,1)S(1)} %collective-permute-done.8.refs_1_, ...), custom_call_target="tpu_custom_call" | custom-call | tf_op jit(solution)/shard_map/pallas_call | solution.py:39
  28.7 0.9 %collective-permute-done.15 = bf16[128,128]{1,0:T(8,128)(2,1)S(1)} collective-permute-done((bf16[128,128]{1,0:T(8,128)(2,1)S(1)}, bf16[128,128]{1,0:T(8,128)(2,1)S(1)}, u32[]{:S(2)}, u32[]{:S(2)}) %collective-permute-start.15) | collective-permute-done | bytes 32800 | tf_op jit(solution)/shard_map/ppermute | solution.py:136
  29.7 0.7 %add_multiply_fusion = f32[128,128]{1,0:T(8,128)} fusion(bf16[128,128]{1,0:T(8,128)(2,1)S(1)} %collective-permute-done.15, bf16[128,128]{1,0:T(8,128)(2,1)S(1)} %add_convert_fusion, bf16[128,128]{1,0:T(8,128)(2,1)S(1)} %collective-permute-done.14, bf16[128,128]{1,0:T(8,128)(2,1)S(1)} %collective-permute-done.13, pred[]{:T(512)S(6)} %eq.13), kind=kLoop, calls=%fused_computation.10 | loop fusion | flops 163840 | bytes 196609 | tf_op jit(solution)/shard_map/mul | solution.py:197
  (29 shorter events, 0.7 us)
Async XLA Ops:
  0.6 8.2 %copy-start.1 = (bf16[1,1,8,2,128,128]{5,4,3,2,1,0:T(8,128)(2,1)S(1)}, bf16[1,1,8,2,128,128]{5,4,3,2,1,0:T(8,128)(2,1)}, u32[]{:S(2)}) copy-start(bf16[1,1,8,2,128,128]{5,4,3,2,1,0:T(8,128)(2,1)} %param.17) | copy-start | bytes 1572868
  1.8 1.4 %collective-permute-start = (bf16[128,128]{1,0:T(8,128)(2,1)S(1)}, bf16[128,128]{1,0:T(8,128)(2,1)S(1)}, u32[]{:S(2)}, u32[]{:S(2)}) collective-permute-start(bf16[128,128]{1,0:T(8,128)(2,1)S(1)} %get-tuple-element.50), channel_id=1, source_target_pairs={{0,1},{1,0},{2,3},{3,2},{4,5},{5,4},{6,7},{7,6},{8,9},{9,8},{10,11... | collective-permute-start | bytes 98312 | tf_op jit(solution)/shard_map/ppermute | solution.py:126
  3.2 5.6 %copy-start.3 = (s32[1,1,8]{2,1,0:T(1,128)S(1)}, s32[1,1,8]{2,1,0:T(1,128)}, u32[]{:S(2)}) copy-start(s32[1,1,8]{2,1,0:T(1,128)} %param.19) | copy-start | bytes 100
  3.2 6.3 %collective-permute-start.3 = (bf16[256,128]{1,0:T(8,128)(2,1)S(1)}, bf16[256,128]{1,0:T(8,128)(2,1)S(1)}, u32[]{:S(2)}, u32[]{:S(2)}) collective-permute-start(bf16[256,128]{1,0:T(8,128)(2,1)S(1)} %pad_maximum_fusion.refs_2_), channel_id=1, source_target_pairs={{0,4},{1,17},{2,6},{3,19},{4,0},{5,21},{6,2},{7,23},{8,12},{9,25},... | collective-permute-start | bytes 196616 | tf_op jit(solution)/shard_map/ppermute | solution.py:136
  7.2 6.2 %collective-permute-start.2 = (bf16[256,128]{1,0:T(8,128)(2,1)S(1)}, bf16[256,128]{1,0:T(8,128)(2,1)S(1)}, u32[]{:S(2)}, u32[]{:S(2)}) collective-permute-start(bf16[256,128]{1,0:T(8,128)(2,1)S(1)} %pad_maximum_fusion.refs_2_), channel_id=1, source_target_pairs={{0,6},{1,25},{2,4},{3,27},{4,2},{5,29},{6,0},{7,31},{8,14},{9,17},... | collective-permute-start | bytes 196616 | tf_op jit(solution)/shard_map/ppermute | solution.py:136
  8.5 5.0 %collective-permute-start.1 = (bf16[256,128]{1,0:T(8,128)(2,1)S(1)}, bf16[256,128]{1,0:T(8,128)(2,1)S(1)}, u32[]{:S(2)}, u32[]{:S(2)}) collective-permute-start(bf16[256,128]{1,0:T(8,128)(2,1)S(1)} %pad_maximum_fusion.refs_2_), channel_id=1, source_target_pairs={{0,2},{1,9},{2,0},{3,11},{4,6},{5,13},{6,4},{7,15},{8,10},{9,1},{1... | collective-permute-start | bytes 196616 | tf_op jit(solution)/shard_map/ppermute | solution.py:136
  8.8 0.7 %copy-start.2 = (s32[1,1,8,2]{2,3,1,0:T(2,128)S(1)}, s32[1,1,8,2]{2,3,1,0:T(2,128)}, u32[]{:S(2)}) copy-start(s32[1,1,8,2]{2,3,1,0:T(2,128)} %param.18) | copy-start | bytes 196
  9.5 4.3 %collective-permute-start.4 = (bf16[256,128]{1,0:T(8,128)(2,1)S(1)}, bf16[256,128]{1,0:T(8,128)(2,1)S(1)}, u32[]{:S(2)}, u32[]{:S(2)}) collective-permute-start(bf16[256,128]{1,0:T(8,128)(2,1)S(1)} %pad_maximum_fusion.refs_2_), channel_id=1, source_target_pairs={{0,1},{1,0},{2,3},{3,2},{4,5},{5,4},{6,7},{7,6},{8,9},{9,8},{10,11... | collective-permute-start | bytes 196616 | tf_op jit(solution)/shard_map/ppermute | solution.py:126
  9.5 4.3 %collective-permute-start.7 = (bf16[256,128]{1,0:T(8,128)(2,1)S(1)}, bf16[256,128]{1,0:T(8,128)(2,1)S(1)}, u32[]{:S(2)}, u32[]{:S(2)}) collective-permute-start(bf16[256,128]{1,0:T(8,128)(2,1)S(1)} %collective-permute-done.3.refs_5_), channel_id=1, source_target_pairs={{0,1},{1,0},{2,3},{3,2},{4,5},{5,4},{6,7},{7,6},{8,9},{9,8},{10,11... | collective-permute-start | bytes 196616 | tf_op jit(solution)/shard_map/ppermute | solution.py:126
  13.3 1.3 %collective-permute-start.6 = (bf16[256,128]{1,0:T(8,128)(2,1)S(1)}, bf16[256,128]{1,0:T(8,128)(2,1)S(1)}, u32[]{:S(2)}, u32[]{:S(2)}) collective-permute-start(bf16[256,128]{1,0:T(8,128)(2,1)S(1)} %collective-permute-done.2.refs_4_), channel_id=1, source_target_pairs={{0,1},{1,0},{2,3},{3,2},{4,5},{5,4},{6,7},{7,6},{8,9},{9,8},{10,11... | collective-permute-start | bytes 196616 | tf_op jit(solution)/shard_map/ppermute | solution.py:126
  13.5 1.3 %collective-permute-start.5 = (bf16[256,128]{1,0:T(8,128)(2,1)S(1)}, bf16[256,128]{1,0:T(8,128)(2,1)S(1)}, u32[]{:S(2)}, u32[]{:S(2)}) collective-permute-start(bf16[256,128]{1,0:T(8,128)(2,1)S(1)} %collective-permute-done.1.refs_3_), channel_id=1, source_target_pairs={{0,1},{1,0},{2,3},{3,2},{4,5},{5,4},{6,7},{7,6},{8,9},{9,8},{10,11... | collective-permute-start | bytes 196616 | tf_op jit(solution)/shard_map/ppermute | solution.py:126
  15.7 1.3 %collective-permute-start.9 = (f32[128,128]{1,0:T(8,128)S(1)}, f32[128,128]{1,0:T(8,128)S(1)}, u32[]{:S(2)}, u32[]{:S(2)}) collective-permute-start(f32[128,128]{1,0:T(8,128)S(1)} %get-tuple-element.44), channel_id=1, source_target_pairs={{0,1},{1,0},{2,3},{3,2},{4,5},{5,4},{6,7},{7,6},{8,9},{9,8},{10,11... | collective-permute-start | bytes 196616 | tf_op jit(solution)/shard_map/ppermute | solution.py:126
  17.0 4.3 %collective-permute-start.10 = (bf16[256,128]{1,0:T(8,128)(2,1)S(1)}, bf16[256,128]{1,0:T(8,128)(2,1)S(1)}, u32[]{:S(2)}, u32[]{:S(2)}) collective-permute-start(bf16[256,128]{1,0:T(8,128)(2,1)S(1)} %constant_dynamic-update-slice_fusion.1), channel_id=1, source_target_pairs={{0,16},{1,9},{2,18},{3,11},{4,20},{5,13},{6,22},{7,15},{8,24},{9,1... | collective-permute-start | bytes 196616 | tf_op jit(solution)/shard_map/ppermute | solution.py:136
  18.6 5.2 %collective-permute-start.11 = (bf16[256,128]{1,0:T(8,128)(2,1)S(1)}, bf16[256,128]{1,0:T(8,128)(2,1)S(1)}, u32[]{:S(2)}, u32[]{:S(2)}) collective-permute-start(bf16[256,128]{1,0:T(8,128)(2,1)S(1)} %get-tuple-element.46), channel_id=1, source_target_pairs={{0,24},{1,25},{2,26},{3,27},{4,28},{5,29},{6,30},{7,31},{8,16},{9,... | collective-permute-start | bytes 196616 | tf_op jit(solution)/shard_map/ppermute | solution.py:136
  21.4 2.4 %collective-permute-start.12 = (bf16[128,128]{1,0:T(8,128)(2,1)S(1)}, bf16[128,128]{1,0:T(8,128)(2,1)S(1)}, u32[]{:S(2)}, u32[]{:S(2)}) collective-permute-start(bf16[128,128]{1,0:T(8,128)(2,1)S(1)} %slice.62), channel_id=1, source_target_pairs={{0,1},{1,0},{2,3},{3,2},{4,5},{5,4},{6,7},{7,6},{8,9},{9,8},{10,11... | collective-permute-start | bytes 98312 | tf_op jit(solution)/shard_map/ppermute | solution.py:126
  21.4 6.4 %copy-start = (bf16[128,128]{1,0:T(8,128)(2,1)S(1)}, bf16[128,128]{1,0:T(8,128)(2,1)}, u32[]{:S(2)}) copy-start(bf16[128,128]{1,0:T(8,128)(2,1)} %weight_ref.1) | copy-start | bytes 98308
  21.4 6.4 %collective-permute-start.8 = (bf16[256,128]{1,0:T(8,128)(2,1)S(1)}, bf16[256,128]{1,0:T(8,128)(2,1)S(1)}, u32[]{:S(2)}, u32[]{:S(2)}) collective-permute-start(bf16[256,128]{1,0:T(8,128)(2,1)S(1)} %get-tuple-element.42), channel_id=1, source_target_pairs={{0,8},{1,17},{2,10},{3,19},{4,12},{5,21},{6,14},{7,23},{8,0},{9,25... | collective-permute-start | bytes 196616 | tf_op jit(solution)/shard_map/ppermute | solution.py:136
  23.8 4.0 %collective-permute-start.13 = (bf16[128,128]{1,0:T(8,128)(2,1)S(1)}, bf16[128,128]{1,0:T(8,128)(2,1)S(1)}, u32[]{:S(2)}, u32[]{:S(2)}) collective-permute-start(bf16[128,128]{1,0:T(8,128)(2,1)S(1)} %add_convert_fusion), channel_id=1, source_target_pairs={{0,2},{1,5},{2,0},{3,7},{4,6},{5,1},{6,4},{7,3},{8,10},{9,13},{10,... | collective-permute-start | bytes 98312 | tf_op jit(solution)/shard_map/ppermute | solution.py:136
  23.9 5.8 %collective-permute-start.15 = (bf16[128,128]{1,0:T(8,128)(2,1)S(1)}, bf16[128,128]{1,0:T(8,128)(2,1)S(1)}, u32[]{:S(2)}, u32[]{:S(2)}) collective-permute-start(bf16[128,128]{1,0:T(8,128)(2,1)S(1)} %add_convert_fusion), channel_id=1, source_target_pairs={{0,6},{1,7},{2,4},{3,5},{4,2},{5,3},{6,0},{7,1},{8,14},{9,15},{10,... | collective-permute-start | bytes 98312 | tf_op jit(solution)/shard_map/ppermute | solution.py:136
  27.8 1.9 %collective-permute-start.14 = (bf16[128,128]{1,0:T(8,128)(2,1)S(1)}, bf16[128,128]{1,0:T(8,128)(2,1)S(1)}, u32[]{:S(2)}, u32[]{:S(2)}) collective-permute-start(bf16[128,128]{1,0:T(8,128)(2,1)S(1)} %collective-permute-done.13), channel_id=1, source_target_pairs={{0,1},{1,0},{2,3},{3,2},{4,5},{5,4},{6,7},{7,6},{8,9},{9,8},{10,11... | collective-permute-start | bytes 98312 | tf_op jit(solution)/shard_map/ppermute | solution.py:126

commit v6 on v5

--- a/solution.py
+++ b/solution.py
@@ -52,31 +52,29 @@
 
 def product_kernel(rows, depth, *refs):
     steps = max(rows, depth)
-    targets_vmem, blocks_ref = refs[:2]
+    targets_ref, blocks_ref = refs[:2]
     own, other = refs[2 : 2 + steps], refs[2 + steps : 2 + 2 * steps]
     term_ref, weight_ref = refs[2 + 2 * steps : 4 + 2 * steps]
-    outs = refs[4 + 2 * steps : -4]
-    total, products, targets_ref, sem = refs[-4:]
-    fetch = pltpu.make_async_copy(targets_vmem, targets_ref, sem)
-    fetch.start()
+    outs = refs[4 + 2 * steps : -1]
+    total = refs[-1]
     r = lax.axis_index("row")
     c = lax.axis_index("col")
     z, even = lax.div(c, 2), lax.rem(c, 2) == 0
+    pairs = []
     for slot, step in enumerate(far_steps(depth)):
         pair = jnp.where(even, own[slot][...], other[slot][...])
-        chip = source_of(z, step, depth)
-        for core in range(2):
-            panel = pair[core * B : (core + 1) * B]
-            for k in range(K):
-                place = (2 * slot + core) * K + k
-                products[place] = dot(blocks_ref[2 * chip + core, k], panel, ((0,), (0,)))
+        pairs.append(pair)
     total[...] = jnp.zeros_like(total)
-    fetch.wait()
+    targets = targets_ref[...].astype(F32)
+    row_at = lax.broadcasted_iota(jnp.int32, targets.shape, 0)
+    col_at = lax.broadcasted_iota(jnp.int32, targets.shape, 1)
     for slot, step in enumerate(far_steps(depth)):
         chip = source_of(z, step, depth)
         for core in range(2):
             for k in range(K):
-                total[targets_ref[k, 2 * chip + core]] += products[(2 * slot + core) * K + k]
+                product = dot(blocks_ref[2 * chip + core, k], pairs[slot][core * B : (core + 1) * B], ((0,), (0,)))
+                target = jnp.max(jnp.where((row_at == k) & (col_at == 2 * chip + core), targets, 0.0))
+                total[target.astype(jnp.int32)] += product
     terms = [total[source_of(r, step, rows)].astype(BF) for step in range(rows)]
     weight = jnp.zeros((F, F), F32)
     for slot, step in enumerate(far_steps(rows)):
@@ -172,9 +170,6 @@
         [pltpu.VMEM] * (2 + 2 * steps),
         scratch=[
             pltpu.VMEM((rows, B, F), F32),
-            pltpu.VMEM((cols * K, B, F), F32),
-            pltpu.SMEM(targets.shape, jnp.int32),
-            pltpu.SemaphoreType.DMA,
         ],
         limit=limit,
     )

time: 30.5 us -> 30.2 us (level)
  Pallas kernels: 1.84 us -> 1.52 us
    pallas_call x2, Pallas kernels: 1.84 us -> 1.52 us  [call(): pl.pallas_call(body, out_shape=outs, in_specs=[pl.BlockSpec(memory_space=...]
where the time goes in v6:
time: 30.2 us; the launch traced here: 30 us
  starting transfers between devices  14.6 us (48%)
  waiting for transfers between devices  10.6 us (35%)
  Pallas kernels  1.52 us (5%)
  matrix products  1.11 us (4%)
  other arithmetic  0.9 us (3%)
  between operations  0.73 us (2%)
  local copies, waits for them, and re-layouts  0.59 us (2%)
    ppermute x8, starting transfers between devices, move(): return lax.ppermute(value, axes, pairs)  12.8 us
    ppermute x8, waiting for transfers between devices, move(): return lax.ppermute(value, axes, pairs)  7.91 us
    ppermute x8, waiting for transfers between devices, across(): return lax.ppermute(value, 'col', [(i, i ^ 1) for i in range(cols)])  2.67 us
    ppermute x8, starting transfers between devices, across(): return lax.ppermute(value, 'col', [(i, i ^ 1) for i in range(cols)])  1.81 us
    pallas_call x2, Pallas kernels, call(): pl.pallas_call(body, out_shape=outs, in_specs=[pl.BlockSpec(memory_space=...  1.52 us
    dot_general x1, matrix products, dot(): lax.dot_general(a, b, (contract, ((), ())), preferred_element_type=F32)  1.11 us
    mul x1, other arithmetic, shards(): return (grad_feat, summed * (slab_rows * rows * cols) ** (-0.5))  0.66 us
  transfers between devices with their start and end apart: 16, of which 10 were waited for; matrix products, arithmetic and copies ran while one was open for 1% of the time, Pallas kernels for 3%

profile of v6, /device:TPU:0, one launch (start us, length us, event | category | flops | bytes accessed | tf_op | source)
XLA Modules:
  0.0 30.0 jit_solution(14710608396414312219)
XLA Ops:
  0.6 1.1 %convolution_convert_fusion = bf16[128,512]{1,0:T(8,128)(2,1)S(1)} fusion(bf16[128,128]{1,0:T(8,128)(2,1)} %constant.65.clone, bf16[128,128]{1,0:T(8,128)(2,1)} %param.15, bf16[128,128]{1,0:T(8,128)(2,1)} %param.14, bf16[128,128]{1,0:T(8,128)(2,1)} %param.13, s32[128]{0:T(128)} %param.20), kind=kOutput, calls=%fused_computation | convolution fusion | flops 17383424 | bytes 262656 | tf_op jit(solution)/shard_map/dot_general | solution.py:35
  1.8 0.5 %collective-permute-start = (bf16[128,128]{1,0:T(8,128)(2,1)S(1)}, bf16[128,128]{1,0:T(8,128)(2,1)S(1)}, u32[]{:S(2)}, u32[]{:S(2)}) collective-permute-start(bf16[128,128]{1,0:T(8,128)(2,1)S(1)} %get-tuple-element.50), channel_id=1, source_target_pairs={{0,1},{1,0},{2,3},{3,2},{4,5},{5,4},{6,7},{7,6},{8,9},{9,8},{10,11... | collective-permute-start | bytes 98312 | tf_op jit(solution)/shard_map/ppermute | solution.py:124
  2.3 0.9 %collective-permute-done = bf16[128,128]{1,0:T(8,128)(2,1)S(1)} collective-permute-done((bf16[128,128]{1,0:T(8,128)(2,1)S(1)}, bf16[128,128]{1,0:T(8,128)(2,1)S(1)}, u32[]{:S(2)}, u32[]{:S(2)}) %collective-permute-start) | collective-permute-done | bytes 32800 | tf_op jit(solution)/shard_map/ppermute | solution.py:124
  3.2 4.0 %collective-permute-start.3 = (bf16[256,128]{1,0:T(8,128)(2,1)S(1)}, bf16[256,128]{1,0:T(8,128)(2,1)S(1)}, u32[]{:S(2)}, u32[]{:S(2)}) collective-permute-start(bf16[256,128]{1,0:T(8,128)(2,1)S(1)} %pad_maximum_fusion.refs_2_), channel_id=1, source_target_pairs={{0,4},{1,17},{2,6},{3,19},{4,0},{5,21},{6,2},{7,23},{8,12},{9,25},... | collective-permute-start | bytes 196616 | tf_op jit(solution)/shard_map/ppermute | solution.py:134
  7.2 1.3 %collective-permute-start.2 = (bf16[256,128]{1,0:T(8,128)(2,1)S(1)}, bf16[256,128]{1,0:T(8,128)(2,1)S(1)}, u32[]{:S(2)}, u32[]{:S(2)}) collective-permute-start(bf16[256,128]{1,0:T(8,128)(2,1)S(1)} %pad_maximum_fusion.refs_2_), channel_id=1, source_target_pairs={{0,6},{1,25},{2,4},{3,27},{4,2},{5,29},{6,0},{7,31},{8,14},{9,17},... | collective-permute-start | bytes 196616 | tf_op jit(solution)/shard_map/ppermute | solution.py:134
  8.5 0.2 collective-permute-start.1
  8.9 0.6 %copy-done.2 = s32[1,1,8,2]{2,3,1,0:T(2,128)S(1)} copy-done((s32[1,1,8,2]{2,3,1,0:T(2,128)S(1)}, s32[1,1,8,2]{2,3,1,0:T(2,128)}, u32[]{:S(2)}) %copy-start.2) | copy-done | bytes 88
  9.5 0.5 %collective-permute-start.7 = (bf16[256,128]{1,0:T(8,128)(2,1)S(1)}, bf16[256,128]{1,0:T(8,128)(2,1)S(1)}, u32[]{:S(2)}, u32[]{:S(2)}) collective-permute-start(bf16[256,128]{1,0:T(8,128)(2,1)S(1)} %collective-permute-done.3.refs_5_), channel_id=1, source_target_pairs={{0,1},{1,0},{2,3},{3,2},{4,5},{5,4},{6,7},{7,6},{8,9},{9,8},{10,11... | collective-permute-start | bytes 196616 | tf_op jit(solution)/shard_map/ppermute | solution.py:124
  10.0 3.3 %collective-permute-done.2.refs_4_ = bf16[256,128]{1,0:T(8,128)(2,1)S(1)} collective-permute-done((bf16[256,128]{1,0:T(8,128)(2,1)S(1)}, bf16[256,128]{1,0:T(8,128)(2,1)S(1)}, u32[]{:S(2)}, u32[]{:S(2)}) %collective-permute-start.2) | collective-permute-done | bytes 65568 | tf_op jit(solution)/shard_map/ppermute | solution.py:134
  13.5 0.4 %collective-permute-start.5 = (bf16[256,128]{1,0:T(8,128)(2,1)S(1)}, bf16[256,128]{1,0:T(8,128)(2,1)S(1)}, u32[]{:S(2)}, u32[]{:S(2)}) collective-permute-start(bf16[256,128]{1,0:T(8,128)(2,1)S(1)} %collective-permute-done.1.refs_3_), channel_id=1, source_target_pairs={{0,1},{1,0},{2,3},{3,2},{4,5},{5,4},{6,7},{7,6},{8,9},{9,8},{10,11... | collective-permute-start | bytes 196616 | tf_op jit(solution)/shard_map/ppermute | solution.py:124
  13.9 0.7 %collective-permute-done.6.refs_8_ = bf16[256,128]{1,0:T(8,128)(2,1)S(1)} collective-permute-done((bf16[256,128]{1,0:T(8,128)(2,1)S(1)}, bf16[256,128]{1,0:T(8,128)(2,1)S(1)}, u32[]{:S(2)}, u32[]{:S(2)}) %collective-permute-start.6) | collective-permute-done | bytes 65568 | tf_op jit(solution)/shard_map/ppermute | solution.py:124
  14.8 0.6 %shard_map.104 = (bf16[128,128]{1,0:T(8,128)(2,1)S(1)}, f32[128,128]{1,0:T(8,128)S(1)}, bf16[256,128]{1,0:T(8,128)(2,1)S(1)}, bf16[256,128]{1,0:T(8,128)(2,1)S(1)}, bf16[256,128]{1,0:T(8,128)(2,1)S(1)}) custom-call(s32[2,8]{1,0:T(2,128)S(1)} %compare_select_fusion.1.refs_0_, bf16[8,2,128,128]{3,2,1,0:T(8,128)(2,1)S(1)} %bitcast_select_fusion.refs_1_, ...), custom_call_target="tpu_custom_call" | custom-call | tf_op jit(solution)/shard_map/pallas_call | solution.py:39
  15.4 0.4 %collective-permute-start.9 = (f32[128,128]{1,0:T(8,128)S(1)}, f32[128,128]{1,0:T(8,128)S(1)}, u32[]{:S(2)}, u32[]{:S(2)}) collective-permute-start(f32[128,128]{1,0:T(8,128)S(1)} %get-tuple-element.44), channel_id=1, source_target_pairs={{0,1},{1,0},{2,3},{3,2},{4,5},{5,4},{6,7},{7,6},{8,9},{9,8},{10,11... | collective-permute-start | bytes 196616 | tf_op jit(solution)/shard_map/ppermute | solution.py:124
  15.8 0.9 %collective-permute-done.9 = f32[128,128]{1,0:T(8,128)S(1)} collective-permute-done((f32[128,128]{1,0:T(8,128)S(1)}, f32[128,128]{1,0:T(8,128)S(1)}, u32[]{:S(2)}, u32[]{:S(2)}) %collective-permute-start.9) | collective-permute-done | bytes 65568 | tf_op jit(solution)/shard_map/ppermute | solution.py:124
  16.7 1.6 %collective-permute-start.10 = (bf16[256,128]{1,0:T(8,128)(2,1)S(1)}, bf16[256,128]{1,0:T(8,128)(2,1)S(1)}, u32[]{:S(2)}, u32[]{:S(2)}) collective-permute-start(bf16[256,128]{1,0:T(8,128)(2,1)S(1)} %constant_dynamic-update-slice_fusion.1), channel_id=1, source_target_pairs={{0,16},{1,9},{2,18},{3,11},{4,20},{5,13},{6,22},{7,15},{8,24},{9,1... | collective-permute-start | bytes 196616 | tf_op jit(solution)/shard_map/ppermute | solution.py:134
  18.3 1.4 %collective-permute-start.11 = (bf16[256,128]{1,0:T(8,128)(2,1)S(1)}, bf16[256,128]{1,0:T(8,128)(2,1)S(1)}, u32[]{:S(2)}, u32[]{:S(2)}) collective-permute-start(bf16[256,128]{1,0:T(8,128)(2,1)S(1)} %get-tuple-element.46), channel_id=1, source_target_pairs={{0,24},{1,25},{2,26},{3,27},{4,28},{5,29},{6,30},{7,31},{8,16},{9,... | collective-permute-start | bytes 196616 | tf_op jit(solution)/shard_map/ppermute | solution.py:134
  19.7 1.3 %collective-permute-done.10.refs_2_ = bf16[256,128]{1,0:T(8,128)(2,1)S(1)} collective-permute-done((bf16[256,128]{1,0:T(8,128)(2,1)S(1)}, bf16[256,128]{1,0:T(8,128)(2,1)S(1)}, u32[]{:S(2)}, u32[]{:S(2)}) %collective-permute-start.10) | collective-permute-done | bytes 65568 | tf_op jit(solution)/shard_map/ppermute | solution.py:134
  21.1 1.6 %collective-permute-start.8 = (bf16[256,128]{1,0:T(8,128)(2,1)S(1)}, bf16[256,128]{1,0:T(8,128)(2,1)S(1)}, u32[]{:S(2)}, u32[]{:S(2)}) collective-permute-start(bf16[256,128]{1,0:T(8,128)(2,1)S(1)} %get-tuple-element.42), channel_id=1, source_target_pairs={{0,8},{1,17},{2,10},{3,19},{4,12},{5,21},{6,14},{7,23},{8,0},{9,25... | collective-permute-start | bytes 196616 | tf_op jit(solution)/shard_map/ppermute | solution.py:134
  22.6 0.8 %collective-permute-done.11.refs_3_ = bf16[256,128]{1,0:T(8,128)(2,1)S(1)} collective-permute-done((bf16[256,128]{1,0:T(8,128)(2,1)S(1)}, bf16[256,128]{1,0:T(8,128)(2,1)S(1)}, u32[]{:S(2)}, u32[]{:S(2)}) %collective-permute-start.11) | collective-permute-done | bytes 65568 | tf_op jit(solution)/shard_map/ppermute | solution.py:134
  23.6 2.6 %collective-permute-start.15 = (bf16[128,128]{1,0:T(8,128)(2,1)S(1)}, bf16[128,128]{1,0:T(8,128)(2,1)S(1)}, u32[]{:S(2)}, u32[]{:S(2)}) collective-permute-start(bf16[128,128]{1,0:T(8,128)(2,1)S(1)} %add_convert_fusion), channel_id=1, source_target_pairs={{0,6},{1,7},{2,4},{3,5},{4,2},{5,3},{6,0},{7,1},{8,14},{9,15},{10,... | collective-permute-start | bytes 98312 | tf_op jit(solution)/shard_map/ppermute | solution.py:134
  26.1 1.4 %collective-permute-done.13 = bf16[128,128]{1,0:T(8,128)(2,1)S(1)} collective-permute-done((bf16[128,128]{1,0:T(8,128)(2,1)S(1)}, bf16[128,128]{1,0:T(8,128)(2,1)S(1)}, u32[]{:S(2)}, u32[]{:S(2)}) %collective-permute-start.13) | collective-permute-done | bytes 32800 | tf_op jit(solution)/shard_map/ppermute | solution.py:134
  27.5 0.9 %shard_map.105 = bf16[128,128]{1,0:T(8,128)(2,1)} custom-call(bf16[128,128]{1,0:T(8,128)(2,1)S(1)} %get-tuple-element.49.place_ref, bf16[128,128]{1,0:T(8,128)(2,1)S(1)} %copy-done, bf16[128,128]{1,0:T(8,128)(2,1)S(1)} %get-tuple-element.41.refs_0_, bf16[256,128]{1,0:T(8,128)(2,1)S(1)} %collective-permute-done.8.refs_1_, ...), custom_call_target="tpu_custom_call" | custom-call | tf_op jit(solution)/shard_map/pallas_call | solution.py:39
  28.4 0.9 %collective-permute-done.15 = bf16[128,128]{1,0:T(8,128)(2,1)S(1)} collective-permute-done((bf16[128,128]{1,0:T(8,128)(2,1)S(1)}, bf16[128,128]{1,0:T(8,128)(2,1)S(1)}, u32[]{:S(2)}, u32[]{:S(2)}) %collective-permute-start.15) | collective-permute-done | bytes 32800 | tf_op jit(solution)/shard_map/ppermute | solution.py:134
  29.4 0.7 %add_multiply_fusion = f32[128,128]{1,0:T(8,128)} fusion(bf16[128,128]{1,0:T(8,128)(2,1)S(1)} %collective-permute-done.15, bf16[128,128]{1,0:T(8,128)(2,1)S(1)} %add_convert_fusion, bf16[128,128]{1,0:T(8,128)(2,1)S(1)} %collective-permute-done.14, bf16[128,128]{1,0:T(8,128)(2,1)S(1)} %collective-permute-done.13, pred[]{:T(512)S(6)} %eq.13), kind=kLoop, calls=%fused_computation.10 | loop fusion | flops 163840 | bytes 196609 | tf_op jit(solution)/shard_map/mul | solution.py:192
  (29 shorter events, 0.7 us)
Async XLA Ops:
  0.6 8.2 %copy-start.1 = (bf16[1,1,8,2,128,128]{5,4,3,2,1,0:T(8,128)(2,1)S(1)}, bf16[1,1,8,2,128,128]{5,4,3,2,1,0:T(8,128)(2,1)}, u32[]{:S(2)}) copy-start(bf16[1,1,8,2,128,128]{5,4,3,2,1,0:T(8,128)(2,1)} %param.17) | copy-start | bytes 1572868
  1.8 1.4 %collective-permute-start = (bf16[128,128]{1,0:T(8,128)(2,1)S(1)}, bf16[128,128]{1,0:T(8,128)(2,1)S(1)}, u32[]{:S(2)}, u32[]{:S(2)}) collective-permute-start(bf16[128,128]{1,0:T(8,128)(2,1)S(1)} %get-tuple-element.50), channel_id=1, source_target_pairs={{0,1},{1,0},{2,3},{3,2},{4,5},{5,4},{6,7},{7,6},{8,9},{9,8},{10,11... | collective-permute-start | bytes 98312 | tf_op jit(solution)/shard_map/ppermute | solution.py:124
  3.2 5.6 %copy-start.3 = (s32[1,1,8]{2,1,0:T(1,128)S(1)}, s32[1,1,8]{2,1,0:T(1,128)}, u32[]{:S(2)}) copy-start(s32[1,1,8]{2,1,0:T(1,128)} %param.19) | copy-start | bytes 100
  3.2 6.3 %collective-permute-start.3 = (bf16[256,128]{1,0:T(8,128)(2,1)S(1)}, bf16[256,128]{1,0:T(8,128)(2,1)S(1)}, u32[]{:S(2)}, u32[]{:S(2)}) collective-permute-start(bf16[256,128]{1,0:T(8,128)(2,1)S(1)} %pad_maximum_fusion.refs_2_), channel_id=1, source_target_pairs={{0,4},{1,17},{2,6},{3,19},{4,0},{5,21},{6,2},{7,23},{8,12},{9,25},... | collective-permute-start | bytes 196616 | tf_op jit(solution)/shard_map/ppermute | solution.py:134
  7.2 6.2 %collective-permute-start.2 = (bf16[256,128]{1,0:T(8,128)(2,1)S(1)}, bf16[256,128]{1,0:T(8,128)(2,1)S(1)}, u32[]{:S(2)}, u32[]{:S(2)}) collective-permute-start(bf16[256,128]{1,0:T(8,128)(2,1)S(1)} %pad_maximum_fusion.refs_2_), channel_id=1, source_target_pairs={{0,6},{1,25},{2,4},{3,27},{4,2},{5,29},{6,0},{7,31},{8,14},{9,17},... | collective-permute-start | bytes 196616 | tf_op jit(solution)/shard_map/ppermute | solution.py:134
  8.5 5.0 %collective-permute-start.1 = (bf16[256,128]{1,0:T(8,128)(2,1)S(1)}, bf16[256,128]{1,0:T(8,128)(2,1)S(1)}, u32[]{:S(2)}, u32[]{:S(2)}) collective-permute-start(bf16[256,128]{1,0:T(8,128)(2,1)S(1)} %pad_maximum_fusion.refs_2_), channel_id=1, source_target_pairs={{0,2},{1,9},{2,0},{3,11},{4,6},{5,13},{6,4},{7,15},{8,10},{9,1},{1... | collective-permute-start | bytes 196616 | tf_op jit(solution)/shard_map/ppermute | solution.py:134
  8.8 0.7 %copy-start.2 = (s32[1,1,8,2]{2,3,1,0:T(2,128)S(1)}, s32[1,1,8,2]{2,3,1,0:T(2,128)}, u32[]{:S(2)}) copy-start(s32[1,1,8,2]{2,3,1,0:T(2,128)} %param.18) | copy-start | bytes 196
  9.5 4.3 %collective-permute-start.4 = (bf16[256,128]{1,0:T(8,128)(2,1)S(1)}, bf16[256,128]{1,0:T(8,128)(2,1)S(1)}, u32[]{:S(2)}, u32[]{:S(2)}) collective-permute-start(bf16[256,128]{1,0:T(8,128)(2,1)S(1)} %pad_maximum_fusion.refs_2_), channel_id=1, source_target_pairs={{0,1},{1,0},{2,3},{3,2},{4,5},{5,4},{6,7},{7,6},{8,9},{9,8},{10,11... | collective-permute-start | bytes 196616 | tf_op jit(solution)/shard_map/ppermute | solution.py:124
  9.5 4.3 %collective-permute-start.7 = (bf16[256,128]{1,0:T(8,128)(2,1)S(1)}, bf16[256,128]{1,0:T(8,128)(2,1)S(1)}, u32[]{:S(2)}, u32[]{:S(2)}) collective-permute-start(bf16[256,128]{1,0:T(8,128)(2,1)S(1)} %collective-permute-done.3.refs_5_), channel_id=1, source_target_pairs={{0,1},{1,0},{2,3},{3,2},{4,5},{5,4},{6,7},{7,6},{8,9},{9,8},{10,11... | collective-permute-start | bytes 196616 | tf_op jit(solution)/shard_map/ppermute | solution.py:124
  13.3 1.3 %collective-permute-start.6 = (bf16[256,128]{1,0:T(8,128)(2,1)S(1)}, bf16[256,128]{1,0:T(8,128)(2,1)S(1)}, u32[]{:S(2)}, u32[]{:S(2)}) collective-permute-start(bf16[256,128]{1,0:T(8,128)(2,1)S(1)} %collective-permute-done.2.refs_4_), channel_id=1, source_target_pairs={{0,1},{1,0},{2,3},{3,2},{4,5},{5,4},{6,7},{7,6},{8,9},{9,8},{10,11... | collective-permute-start | bytes 196616 | tf_op jit(solution)/shard_map/ppermute | solution.py:124
  13.5 1.3 %collective-permute-start.5 = (bf16[256,128]{1,0:T(8,128)(2,1)S(1)}, bf16[256,128]{1,0:T(8,128)(2,1)S(1)}, u32[]{:S(2)}, u32[]{:S(2)}) collective-permute-start(bf16[256,128]{1,0:T(8,128)(2,1)S(1)} %collective-permute-done.1.refs_3_), channel_id=1, source_target_pairs={{0,1},{1,0},{2,3},{3,2},{4,5},{5,4},{6,7},{7,6},{8,9},{9,8},{10,11... | collective-permute-start | bytes 196616 | tf_op jit(solution)/shard_map/ppermute | solution.py:124
  15.4 1.3 %collective-permute-start.9 = (f32[128,128]{1,0:T(8,128)S(1)}, f32[128,128]{1,0:T(8,128)S(1)}, u32[]{:S(2)}, u32[]{:S(2)}) collective-permute-start(f32[128,128]{1,0:T(8,128)S(1)} %get-tuple-element.44), channel_id=1, source_target_pairs={{0,1},{1,0},{2,3},{3,2},{4,5},{5,4},{6,7},{7,6},{8,9},{9,8},{10,11... | collective-permute-start | bytes 196616 | tf_op jit(solution)/shard_map/ppermute | solution.py:124
  16.7 4.3 %collective-permute-start.10 = (bf16[256,128]{1,0:T(8,128)(2,1)S(1)}, bf16[256,128]{1,0:T(8,128)(2,1)S(1)}, u32[]{:S(2)}, u32[]{:S(2)}) collective-permute-start(bf16[256,128]{1,0:T(8,128)(2,1)S(1)} %constant_dynamic-update-slice_fusion.1), channel_id=1, source_target_pairs={{0,16},{1,9},{2,18},{3,11},{4,20},{5,13},{6,22},{7,15},{8,24},{9,1... | collective-permute-start | bytes 196616 | tf_op jit(solution)/shard_map/ppermute | solution.py:134
  18.3 5.2 %collective-permute-start.11 = (bf16[256,128]{1,0:T(8,128)(2,1)S(1)}, bf16[256,128]{1,0:T(8,128)(2,1)S(1)}, u32[]{:S(2)}, u32[]{:S(2)}) collective-permute-start(bf16[256,128]{1,0:T(8,128)(2,1)S(1)} %get-tuple-element.46), channel_id=1, source_target_pairs={{0,24},{1,25},{2,26},{3,27},{4,28},{5,29},{6,30},{7,31},{8,16},{9,... | collective-permute-start | bytes 196616 | tf_op jit(solution)/shard_map/ppermute | solution.py:134
  21.1 2.4 %collective-permute-start.12 = (bf16[128,128]{1,0:T(8,128)(2,1)S(1)}, bf16[128,128]{1,0:T(8,128)(2,1)S(1)}, u32[]{:S(2)}, u32[]{:S(2)}) collective-permute-start(bf16[128,128]{1,0:T(8,128)(2,1)S(1)} %slice.62), channel_id=1, source_target_pairs={{0,1},{1,0},{2,3},{3,2},{4,5},{5,4},{6,7},{7,6},{8,9},{9,8},{10,11... | collective-permute-start | bytes 98312 | tf_op jit(solution)/shard_map/ppermute | solution.py:124
  21.1 6.4 %copy-start = (bf16[128,128]{1,0:T(8,128)(2,1)S(1)}, bf16[128,128]{1,0:T(8,128)(2,1)}, u32[]{:S(2)}) copy-start(bf16[128,128]{1,0:T(8,128)(2,1)} %weight_ref.1) | copy-start | bytes 98308
  21.1 6.4 %collective-permute-start.8 = (bf16[256,128]{1,0:T(8,128)(2,1)S(1)}, bf16[256,128]{1,0:T(8,128)(2,1)S(1)}, u32[]{:S(2)}, u32[]{:S(2)}) collective-permute-start(bf16[256,128]{1,0:T(8,128)(2,1)S(1)} %get-tuple-element.42), channel_id=1, source_target_pairs={{0,8},{1,17},{2,10},{3,19},{4,12},{5,21},{6,14},{7,23},{8,0},{9,25... | collective-permute-start | bytes 196616 | tf_op jit(solution)/shard_map/ppermute | solution.py:134
  23.5 4.0 %collective-permute-start.13 = (bf16[128,128]{1,0:T(8,128)(2,1)S(1)}, bf16[128,128]{1,0:T(8,128)(2,1)S(1)}, u32[]{:S(2)}, u32[]{:S(2)}) collective-permute-start(bf16[128,128]{1,0:T(8,128)(2,1)S(1)} %add_convert_fusion), channel_id=1, source_target_pairs={{0,2},{1,5},{2,0},{3,7},{4,6},{5,1},{6,4},{7,3},{8,10},{9,13},{10,... | collective-permute-start | bytes 98312 | tf_op jit(solution)/shard_map/ppermute | solution.py:134
  23.6 5.8 %collective-permute-start.15 = (bf16[128,128]{1,0:T(8,128)(2,1)S(1)}, bf16[128,128]{1,0:T(8,128)(2,1)S(1)}, u32[]{:S(2)}, u32[]{:S(2)}) collective-permute-start(bf16[128,128]{1,0:T(8,128)(2,1)S(1)} %add_convert_fusion), channel_id=1, source_target_pairs={{0,6},{1,7},{2,4},{3,5},{4,2},{5,3},{6,0},{7,1},{8,14},{9,15},{10,... | collective-permute-start | bytes 98312 | tf_op jit(solution)/shard_map/ppermute | solution.py:134
  27.5 1.9 %collective-permute-start.14 = (bf16[128,128]{1,0:T(8,128)(2,1)S(1)}, bf16[128,128]{1,0:T(8,128)(2,1)S(1)}, u32[]{:S(2)}, u32[]{:S(2)}) collective-permute-start(bf16[128,128]{1,0:T(8,128)(2,1)S(1)} %collective-permute-done.13), channel_id=1, source_target_pairs={{0,1},{1,0},{2,3},{3,2},{4,5},{5,4},{6,7},{7,6},{8,9},{9,8},{10,11... | collective-permute-start | bytes 98312 | tf_op jit(solution)/shard_map/ppermute | solution.py:124

commit v7 on v6

--- a/solution.py
+++ b/solution.py
@@ -47,7 +47,7 @@
 
 
 def row_steps(rows):
-    return list(zip([1, 2, *range(3, rows)], [2, 1, *range(3, rows)]))
+    return list(zip([2, 1, *range(3, rows)], [1, 2, *range(3, rows)]))
 
 
 def product_kernel(rows, depth, *refs):
@@ -182,13 +182,15 @@
     )
     mine = terms[1][B:]
     swapped = across(mine)
-    weights = [chip_weight, jnp.where(even, swapped, mine), jnp.where(even, mine, swapped)] + [t[B:] for t in terms[2:]]
-    row_weight = sum_in_order(weights, r, rows).astype(BF)
-    mine = along_depth(row_weight, (1, 2))
-    rest = [along_depth(row_weight, (step, step)) for step in range(3, depth)]
+    weights = {0: chip_weight, 1: jnp.where(even, mine, swapped), 2: jnp.where(even, swapped, mine)}
+    weights.update({plan[k][0]: term[B:] for k, term in enumerate(terms) if k > 1})
+    row_weight = sum_in_order([weights[step] for step in range(rows)], r, rows).astype(BF)
+    last = depth - 1
+    mine = along_depth(row_weight, (1, last))
+    weights = {step: along_depth(row_weight, (step, step)) for step in range(2, last)}
     swapped = across(mine)
-    weights = [row_weight, jnp.where(even, mine, swapped), jnp.where(even, swapped, mine)] + rest
-    summed = sum_in_order(weights, z, depth)
+    weights.update({0: row_weight, 1: jnp.where(even, mine, swapped), last: jnp.where(even, swapped, mine)})
+    summed = sum_in_order([weights[step] for step in range(depth)], z, depth)
     return grad_feat, summed * (slab_rows * rows * cols) ** (-0.5)
 
 

time: 30.2 us -> 29.8 us (0.987)
  waiting for transfers between devices: 10.6 us -> 9.85 us
    ppermute x8, waiting for transfers between devices: 7.91 us -> 7.17 us  [move(): return lax.ppermute(value, axes, pairs)]
    ppermute x8, starting transfers between devices: 1.81 us -> 2.18 us  [across(): return lax.ppermute(value, 'col', [(i, i ^ 1) for i in range(cols)])]
where the time goes in v7:
time: 29.8 us; the launch traced here: 29.6 us
  starting transfers between devices  14.9 us (50%)
  waiting for transfers between devices  9.85 us (33%)
  Pallas kernels  1.52 us (5%)
  matrix products  1.11 us (4%)
  other arithmetic  0.9 us (3%)
  between operations  0.72 us (2%)
  local copies, waits for them, and re-layouts  0.59 us (2%)
    ppermute x8, starting transfers between devices, move(): return lax.ppermute(value, axes, pairs)  12.7 us
    ppermute x8, waiting for transfers between devices, move(): return lax.ppermute(value, axes, pairs)  7.17 us
    ppermute x8, waiting for transfers between devices, across(): return lax.ppermute(value, 'col', [(i, i ^ 1) for i in range(cols)])  2.67 us
    ppermute x8, starting transfers between devices, across(): return lax.ppermute(value, 'col', [(i, i ^ 1) for i in range(cols)])  2.18 us
    pallas_call x2, Pallas kernels, call(): pl.pallas_call(body, out_shape=outs, in_specs=[pl.BlockSpec(memory_space=...  1.52 us
    dot_general x1, matrix products, dot(): lax.dot_general(a, b, (contract, ((), ())), preferred_element_type=F32)  1.11 us
    mul x1, other arithmetic, shards(): return (grad_feat, summed * (slab_rows * rows * cols) ** (-0.5))  0.66 us
  transfers between devices with their start and end apart: 16, of which 10 were waited for; matrix products, arithmetic and copies ran while one was open for 1% of the time, Pallas kernels for 3%

profile of v7, /device:TPU:0, one launch (start us, length us, event | category | flops | bytes accessed | tf_op | source)
XLA Modules:
  0.0 29.6 jit_solution(13798807345479572430)
XLA Ops:
  0.6 1.1 %convolution_convert_fusion = bf16[128,512]{1,0:T(8,128)(2,1)S(1)} fusion(bf16[128,128]{1,0:T(8,128)(2,1)} %constant.65.clone, bf16[128,128]{1,0:T(8,128)(2,1)} %param.15, bf16[128,128]{1,0:T(8,128)(2,1)} %param.14, bf16[128,128]{1,0:T(8,128)(2,1)} %param.13, s32[128]{0:T(128)} %param.20), kind=kOutput, calls=%fused_computation | convolution fusion | flops 17383424 | bytes 262656 | tf_op jit(solution)/shard_map/dot_general | solution.py:35
  1.8 0.5 %collective-permute-start = (bf16[128,128]{1,0:T(8,128)(2,1)S(1)}, bf16[128,128]{1,0:T(8,128)(2,1)S(1)}, u32[]{:S(2)}, u32[]{:S(2)}) collective-permute-start(bf16[128,128]{1,0:T(8,128)(2,1)S(1)} %get-tuple-element.50), channel_id=1, source_target_pairs={{0,1},{1,0},{2,3},{3,2},{4,5},{5,4},{6,7},{7,6},{8,9},{9,8},{10,11... | collective-permute-start | bytes 98312 | tf_op jit(solution)/shard_map/ppermute | solution.py:124
  2.3 0.9 %collective-permute-done = bf16[128,128]{1,0:T(8,128)(2,1)S(1)} collective-permute-done((bf16[128,128]{1,0:T(8,128)(2,1)S(1)}, bf16[128,128]{1,0:T(8,128)(2,1)S(1)}, u32[]{:S(2)}, u32[]{:S(2)}) %collective-permute-start) | collective-permute-done | bytes 32800 | tf_op jit(solution)/shard_map/ppermute | solution.py:124
  3.2 4.0 %collective-permute-start.3 = (bf16[256,128]{1,0:T(8,128)(2,1)S(1)}, bf16[256,128]{1,0:T(8,128)(2,1)S(1)}, u32[]{:S(2)}, u32[]{:S(2)}) collective-permute-start(bf16[256,128]{1,0:T(8,128)(2,1)S(1)} %pad_maximum_fusion.refs_2_), channel_id=1, source_target_pairs={{0,4},{1,17},{2,6},{3,19},{4,0},{5,21},{6,2},{7,23},{8,12},{9,25},... | collective-permute-start | bytes 196616 | tf_op jit(solution)/shard_map/ppermute | solution.py:134
  7.2 1.3 %collective-permute-start.2 = (bf16[256,128]{1,0:T(8,128)(2,1)S(1)}, bf16[256,128]{1,0:T(8,128)(2,1)S(1)}, u32[]{:S(2)}, u32[]{:S(2)}) collective-permute-start(bf16[256,128]{1,0:T(8,128)(2,1)S(1)} %pad_maximum_fusion.refs_2_), channel_id=1, source_target_pairs={{0,6},{1,25},{2,4},{3,27},{4,2},{5,29},{6,0},{7,31},{8,14},{9,17},... | collective-permute-start | bytes 196616 | tf_op jit(solution)/shard_map/ppermute | solution.py:134
  8.5 0.2 collective-permute-start.1
  8.9 0.6 %copy-done.2 = s32[1,1,8,2]{2,3,1,0:T(2,128)S(1)} copy-done((s32[1,1,8,2]{2,3,1,0:T(2,128)S(1)}, s32[1,1,8,2]{2,3,1,0:T(2,128)}, u32[]{:S(2)}) %copy-start.2) | copy-done | bytes 88
  9.5 0.5 %collective-permute-start.7 = (bf16[256,128]{1,0:T(8,128)(2,1)S(1)}, bf16[256,128]{1,0:T(8,128)(2,1)S(1)}, u32[]{:S(2)}, u32[]{:S(2)}) collective-permute-start(bf16[256,128]{1,0:T(8,128)(2,1)S(1)} %collective-permute-done.3.refs_5_), channel_id=1, source_target_pairs={{0,1},{1,0},{2,3},{3,2},{4,5},{5,4},{6,7},{7,6},{8,9},{9,8},{10,11... | collective-permute-start | bytes 196616 | tf_op jit(solution)/shard_map/ppermute | solution.py:124
  10.0 3.3 %collective-permute-done.2.refs_4_ = bf16[256,128]{1,0:T(8,128)(2,1)S(1)} collective-permute-done((bf16[256,128]{1,0:T(8,128)(2,1)S(1)}, bf16[256,128]{1,0:T(8,128)(2,1)S(1)}, u32[]{:S(2)}, u32[]{:S(2)}) %collective-permute-start.2) | collective-permute-done | bytes 65568 | tf_op jit(solution)/shard_map/ppermute | solution.py:134
  13.5 0.4 %collective-permute-start.5 = (bf16[256,128]{1,0:T(8,128)(2,1)S(1)}, bf16[256,128]{1,0:T(8,128)(2,1)S(1)}, u32[]{:S(2)}, u32[]{:S(2)}) collective-permute-start(bf16[256,128]{1,0:T(8,128)(2,1)S(1)} %collective-permute-done.1.refs_3_), channel_id=1, source_target_pairs={{0,1},{1,0},{2,3},{3,2},{4,5},{5,4},{6,7},{7,6},{8,9},{9,8},{10,11... | collective-permute-start | bytes 196616 | tf_op jit(solution)/shard_map/ppermute | solution.py:124
  13.9 0.7 %collective-permute-done.6.refs_8_ = bf16[256,128]{1,0:T(8,128)(2,1)S(1)} collective-permute-done((bf16[256,128]{1,0:T(8,128)(2,1)S(1)}, bf16[256,128]{1,0:T(8,128)(2,1)S(1)}, u32[]{:S(2)}, u32[]{:S(2)}) %collective-permute-start.6) | collective-permute-done | bytes 65568 | tf_op jit(solution)/shard_map/ppermute | solution.py:124
  14.8 0.6 %shard_map.104 = (bf16[128,128]{1,0:T(8,128)(2,1)S(1)}, f32[128,128]{1,0:T(8,128)S(1)}, bf16[256,128]{1,0:T(8,128)(2,1)S(1)}, bf16[256,128]{1,0:T(8,128)(2,1)S(1)}, bf16[256,128]{1,0:T(8,128)(2,1)S(1)}) custom-call(s32[2,8]{1,0:T(2,128)S(1)} %compare_select_fusion.1.refs_0_, bf16[8,2,128,128]{3,2,1,0:T(8,128)(2,1)S(1)} %bitcast_select_fusion.refs_1_, ...), custom_call_target="tpu_custom_call" | custom-call | tf_op jit(solution)/shard_map/pallas_call | solution.py:39
  15.4 0.4 %collective-permute-start.9 = (f32[128,128]{1,0:T(8,128)S(1)}, f32[128,128]{1,0:T(8,128)S(1)}, u32[]{:S(2)}, u32[]{:S(2)}) collective-permute-start(f32[128,128]{1,0:T(8,128)S(1)} %get-tuple-element.44), channel_id=1, source_target_pairs={{0,1},{1,0},{2,3},{3,2},{4,5},{5,4},{6,7},{7,6},{8,9},{9,8},{10,11... | collective-permute-start | bytes 196616 | tf_op jit(solution)/shard_map/ppermute | solution.py:124
  15.8 0.9 %collective-permute-done.9 = f32[128,128]{1,0:T(8,128)S(1)} collective-permute-done((f32[128,128]{1,0:T(8,128)S(1)}, f32[128,128]{1,0:T(8,128)S(1)}, u32[]{:S(2)}, u32[]{:S(2)}) %collective-permute-start.9) | collective-permute-done | bytes 65568 | tf_op jit(solution)/shard_map/ppermute | solution.py:124
  16.7 1.6 %collective-permute-start.10 = (bf16[256,128]{1,0:T(8,128)(2,1)S(1)}, bf16[256,128]{1,0:T(8,128)(2,1)S(1)}, u32[]{:S(2)}, u32[]{:S(2)}) collective-permute-start(bf16[256,128]{1,0:T(8,128)(2,1)S(1)} %constant_dynamic-update-slice_fusion.1), channel_id=1, source_target_pairs={{0,8},{1,17},{2,10},{3,19},{4,12},{5,21},{6,14},{7,23},{8,0},{9,25... | collective-permute-start | bytes 196616 | tf_op jit(solution)/shard_map/ppermute | solution.py:134
  18.3 1.5 %collective-permute-start.11 = (bf16[256,128]{1,0:T(8,128)(2,1)S(1)}, bf16[256,128]{1,0:T(8,128)(2,1)S(1)}, u32[]{:S(2)}, u32[]{:S(2)}) collective-permute-start(bf16[256,128]{1,0:T(8,128)(2,1)S(1)} %get-tuple-element.46), channel_id=1, source_target_pairs={{0,24},{1,25},{2,26},{3,27},{4,28},{5,29},{6,30},{7,31},{8,16},{9,... | collective-permute-start | bytes 196616 | tf_op jit(solution)/shard_map/ppermute | solution.py:134
  19.8 1.5 %collective-permute-done.10.refs_2_ = bf16[256,128]{1,0:T(8,128)(2,1)S(1)} collective-permute-done((bf16[256,128]{1,0:T(8,128)(2,1)S(1)}, bf16[256,128]{1,0:T(8,128)(2,1)S(1)}, u32[]{:S(2)}, u32[]{:S(2)}) %collective-permute-start.10) | collective-permute-done | bytes 65568 | tf_op jit(solution)/shard_map/ppermute | solution.py:134
  21.3 1.6 %collective-permute-start.8 = (bf16[256,128]{1,0:T(8,128)(2,1)S(1)}, bf16[256,128]{1,0:T(8,128)(2,1)S(1)}, u32[]{:S(2)}, u32[]{:S(2)}) collective-permute-start(bf16[256,128]{1,0:T(8,128)(2,1)S(1)} %get-tuple-element.42), channel_id=1, source_target_pairs={{0,16},{1,9},{2,18},{3,11},{4,20},{5,13},{6,22},{7,15},{8,24},{9,1... | collective-permute-start | bytes 196616 | tf_op jit(solution)/shard_map/ppermute | solution.py:134
  22.8 0.6 %collective-permute-done.11.refs_3_ = bf16[256,128]{1,0:T(8,128)(2,1)S(1)} collective-permute-done((bf16[256,128]{1,0:T(8,128)(2,1)S(1)}, bf16[256,128]{1,0:T(8,128)(2,1)S(1)}, u32[]{:S(2)}, u32[]{:S(2)}) %collective-permute-start.11) | collective-permute-done | bytes 65568 | tf_op jit(solution)/shard_map/ppermute | solution.py:134
  23.6 2.4 %collective-permute-start.15 = (bf16[128,128]{1,0:T(8,128)(2,1)S(1)}, bf16[128,128]{1,0:T(8,128)(2,1)S(1)}, u32[]{:S(2)}, u32[]{:S(2)}) collective-permute-start(bf16[128,128]{1,0:T(8,128)(2,1)S(1)} %add_convert_fusion), channel_id=1, source_target_pairs={{0,4},{1,5},{2,6},{3,7},{4,0},{5,1},{6,2},{7,3},{8,12},{9,13},{10,... | collective-permute-start | bytes 98312 | tf_op jit(solution)/shard_map/ppermute | solution.py:134
  26.0 1.5 %collective-permute-done.13 = bf16[128,128]{1,0:T(8,128)(2,1)S(1)} collective-permute-done((bf16[128,128]{1,0:T(8,128)(2,1)S(1)}, bf16[128,128]{1,0:T(8,128)(2,1)S(1)}, u32[]{:S(2)}, u32[]{:S(2)}) %collective-permute-start.13) | collective-permute-done | bytes 32800 | tf_op jit(solution)/shard_map/ppermute | solution.py:134
  27.5 0.4 %collective-permute-start.14 = (bf16[128,128]{1,0:T(8,128)(2,1)S(1)}, bf16[128,128]{1,0:T(8,128)(2,1)S(1)}, u32[]{:S(2)}, u32[]{:S(2)}) collective-permute-start(bf16[128,128]{1,0:T(8,128)(2,1)S(1)} %collective-permute-done.13), channel_id=1, source_target_pairs={{0,1},{1,0},{2,3},{3,2},{4,5},{5,4},{6,7},{7,6},{8,9},{9,8},{10,11... | collective-permute-start | bytes 98312 | tf_op jit(solution)/shard_map/ppermute | solution.py:124
  27.8 0.9 %shard_map.105 = bf16[128,128]{1,0:T(8,128)(2,1)} custom-call(bf16[128,128]{1,0:T(8,128)(2,1)S(1)} %get-tuple-element.49.place_ref, bf16[128,128]{1,0:T(8,128)(2,1)S(1)} %copy-done, bf16[128,128]{1,0:T(8,128)(2,1)S(1)} %get-tuple-element.41.refs_0_, bf16[256,128]{1,0:T(8,128)(2,1)S(1)} %collective-permute-done.8.refs_1_, ...), custom_call_target="tpu_custom_call" | custom-call | tf_op jit(solution)/shard_map/pallas_call | solution.py:39
  28.9 0.7 %add_multiply_fusion = f32[128,128]{1,0:T(8,128)} fusion(bf16[128,128]{1,0:T(8,128)(2,1)S(1)} %collective-permute-done.15, bf16[128,128]{1,0:T(8,128)(2,1)S(1)} %add_convert_fusion, bf16[128,128]{1,0:T(8,128)(2,1)S(1)} %collective-permute-done.14, bf16[128,128]{1,0:T(8,128)(2,1)S(1)} %collective-permute-done.13, pred[]{:T(512)S(6)} %eq.13), kind=kLoop, calls=%fused_computation.10 | loop fusion | flops 163840 | bytes 196609 | tf_op jit(solution)/shard_map/mul | solution.py:194
  (29 shorter events, 0.8 us)
Async XLA Ops:
  0.6 8.2 %copy-start.1 = (bf16[1,1,8,2,128,128]{5,4,3,2,1,0:T(8,128)(2,1)S(1)}, bf16[1,1,8,2,128,128]{5,4,3,2,1,0:T(8,128)(2,1)}, u32[]{:S(2)}) copy-start(bf16[1,1,8,2,128,128]{5,4,3,2,1,0:T(8,128)(2,1)} %param.17) | copy-start | bytes 1572868
  1.8 1.4 %collective-permute-start = (bf16[128,128]{1,0:T(8,128)(2,1)S(1)}, bf16[128,128]{1,0:T(8,128)(2,1)S(1)}, u32[]{:S(2)}, u32[]{:S(2)}) collective-permute-start(bf16[128,128]{1,0:T(8,128)(2,1)S(1)} %get-tuple-element.50), channel_id=1, source_target_pairs={{0,1},{1,0},{2,3},{3,2},{4,5},{5,4},{6,7},{7,6},{8,9},{9,8},{10,11... | collective-permute-start | bytes 98312 | tf_op jit(solution)/shard_map/ppermute | solution.py:124
  3.2 5.6 %copy-start.3 = (s32[1,1,8]{2,1,0:T(1,128)S(1)}, s32[1,1,8]{2,1,0:T(1,128)}, u32[]{:S(2)}) copy-start(s32[1,1,8]{2,1,0:T(1,128)} %param.19) | copy-start | bytes 100
  3.2 6.3 %collective-permute-start.3 = (bf16[256,128]{1,0:T(8,128)(2,1)S(1)}, bf16[256,128]{1,0:T(8,128)(2,1)S(1)}, u32[]{:S(2)}, u32[]{:S(2)}) collective-permute-start(bf16[256,128]{1,0:T(8,128)(2,1)S(1)} %pad_maximum_fusion.refs_2_), channel_id=1, source_target_pairs={{0,4},{1,17},{2,6},{3,19},{4,0},{5,21},{6,2},{7,23},{8,12},{9,25},... | collective-permute-start | bytes 196616 | tf_op jit(solution)/shard_map/ppermute | solution.py:134
  7.2 6.2 %collective-permute-start.2 = (bf16[256,128]{1,0:T(8,128)(2,1)S(1)}, bf16[256,128]{1,0:T(8,128)(2,1)S(1)}, u32[]{:S(2)}, u32[]{:S(2)}) collective-permute-start(bf16[256,128]{1,0:T(8,128)(2,1)S(1)} %pad_maximum_fusion.refs_2_), channel_id=1, source_target_pairs={{0,6},{1,25},{2,4},{3,27},{4,2},{5,29},{6,0},{7,31},{8,14},{9,17},... | collective-permute-start | bytes 196616 | tf_op jit(solution)/shard_map/ppermute | solution.py:134
  8.5 5.0 %collective-permute-start.1 = (bf16[256,128]{1,0:T(8,128)(2,1)S(1)}, bf16[256,128]{1,0:T(8,128)(2,1)S(1)}, u32[]{:S(2)}, u32[]{:S(2)}) collective-permute-start(bf16[256,128]{1,0:T(8,128)(2,1)S(1)} %pad_maximum_fusion.refs_2_), channel_id=1, source_target_pairs={{0,2},{1,9},{2,0},{3,11},{4,6},{5,13},{6,4},{7,15},{8,10},{9,1},{1... | collective-permute-start | bytes 196616 | tf_op jit(solution)/shard_map/ppermute | solution.py:134
  8.8 0.7 %copy-start.2 = (s32[1,1,8,2]{2,3,1,0:T(2,128)S(1)}, s32[1,1,8,2]{2,3,1,0:T(2,128)}, u32[]{:S(2)}) copy-start(s32[1,1,8,2]{2,3,1,0:T(2,128)} %param.18) | copy-start | bytes 196
  9.5 4.3 %collective-permute-start.4 = (bf16[256,128]{1,0:T(8,128)(2,1)S(1)}, bf16[256,128]{1,0:T(8,128)(2,1)S(1)}, u32[]{:S(2)}, u32[]{:S(2)}) collective-permute-start(bf16[256,128]{1,0:T(8,128)(2,1)S(1)} %pad_maximum_fusion.refs_2_), channel_id=1, source_target_pairs={{0,1},{1,0},{2,3},{3,2},{4,5},{5,4},{6,7},{7,6},{8,9},{9,8},{10,11... | collective-permute-start | bytes 196616 | tf_op jit(solution)/shard_map/ppermute | solution.py:124
  9.5 4.3 %collective-permute-start.7 = (bf16[256,128]{1,0:T(8,128)(2,1)S(1)}, bf16[256,128]{1,0:T(8,128)(2,1)S(1)}, u32[]{:S(2)}, u32[]{:S(2)}) collective-permute-start(bf16[256,128]{1,0:T(8,128)(2,1)S(1)} %collective-permute-done.3.refs_5_), channel_id=1, source_target_pairs={{0,1},{1,0},{2,3},{3,2},{4,5},{5,4},{6,7},{7,6},{8,9},{9,8},{10,11... | collective-permute-start | bytes 196616 | tf_op jit(solution)/shard_map/ppermute | solution.py:124
  13.3 1.3 %collective-permute-start.6 = (bf16[256,128]{1,0:T(8,128)(2,1)S(1)}, bf16[256,128]{1,0:T(8,128)(2,1)S(1)}, u32[]{:S(2)}, u32[]{:S(2)}) collective-permute-start(bf16[256,128]{1,0:T(8,128)(2,1)S(1)} %collective-permute-done.2.refs_4_), channel_id=1, source_target_pairs={{0,1},{1,0},{2,3},{3,2},{4,5},{5,4},{6,7},{7,6},{8,9},{9,8},{10,11... | collective-permute-start | bytes 196616 | tf_op jit(solution)/shard_map/ppermute | solution.py:124
  13.5 1.3 %collective-permute-start.5 = (bf16[256,128]{1,0:T(8,128)(2,1)S(1)}, bf16[256,128]{1,0:T(8,128)(2,1)S(1)}, u32[]{:S(2)}, u32[]{:S(2)}) collective-permute-start(bf16[256,128]{1,0:T(8,128)(2,1)S(1)} %collective-permute-done.1.refs_3_), channel_id=1, source_target_pairs={{0,1},{1,0},{2,3},{3,2},{4,5},{5,4},{6,7},{7,6},{8,9},{9,8},{10,11... | collective-permute-start | bytes 196616 | tf_op jit(solution)/shard_map/ppermute | solution.py:124
  15.4 1.3 %collective-permute-start.9 = (f32[128,128]{1,0:T(8,128)S(1)}, f32[128,128]{1,0:T(8,128)S(1)}, u32[]{:S(2)}, u32[]{:S(2)}) collective-permute-start(f32[128,128]{1,0:T(8,128)S(1)} %get-tuple-element.44), channel_id=1, source_target_pairs={{0,1},{1,0},{2,3},{3,2},{4,5},{5,4},{6,7},{7,6},{8,9},{9,8},{10,11... | collective-permute-start | bytes 196616 | tf_op jit(solution)/shard_map/ppermute | solution.py:124
  16.7 4.5 %collective-permute-start.10 = (bf16[256,128]{1,0:T(8,128)(2,1)S(1)}, bf16[256,128]{1,0:T(8,128)(2,1)S(1)}, u32[]{:S(2)}, u32[]{:S(2)}) collective-permute-start(bf16[256,128]{1,0:T(8,128)(2,1)S(1)} %constant_dynamic-update-slice_fusion.1), channel_id=1, source_target_pairs={{0,8},{1,17},{2,10},{3,19},{4,12},{5,21},{6,14},{7,23},{8,0},{9,25... | collective-permute-start | bytes 196616 | tf_op jit(solution)/shard_map/ppermute | solution.py:134
  18.3 5.2 %collective-permute-start.11 = (bf16[256,128]{1,0:T(8,128)(2,1)S(1)}, bf16[256,128]{1,0:T(8,128)(2,1)S(1)}, u32[]{:S(2)}, u32[]{:S(2)}) collective-permute-start(bf16[256,128]{1,0:T(8,128)(2,1)S(1)} %get-tuple-element.46), channel_id=1, source_target_pairs={{0,24},{1,25},{2,26},{3,27},{4,28},{5,29},{6,30},{7,31},{8,16},{9,... | collective-permute-start | bytes 196616 | tf_op jit(solution)/shard_map/ppermute | solution.py:134
  21.3 2.2 %collective-permute-start.12 = (bf16[128,128]{1,0:T(8,128)(2,1)S(1)}, bf16[128,128]{1,0:T(8,128)(2,1)S(1)}, u32[]{:S(2)}, u32[]{:S(2)}) collective-permute-start(bf16[128,128]{1,0:T(8,128)(2,1)S(1)} %slice.62), channel_id=1, source_target_pairs={{0,1},{1,0},{2,3},{3,2},{4,5},{5,4},{6,7},{7,6},{8,9},{9,8},{10,11... | collective-permute-start | bytes 98312 | tf_op jit(solution)/shard_map/ppermute | solution.py:124
  21.3 6.6 %copy-start = (bf16[128,128]{1,0:T(8,128)(2,1)S(1)}, bf16[128,128]{1,0:T(8,128)(2,1)}, u32[]{:S(2)}) copy-start(bf16[128,128]{1,0:T(8,128)(2,1)} %weight_ref.1) | copy-start | bytes 98308
  21.3 6.6 %collective-permute-start.8 = (bf16[256,128]{1,0:T(8,128)(2,1)S(1)}, bf16[256,128]{1,0:T(8,128)(2,1)S(1)}, u32[]{:S(2)}, u32[]{:S(2)}) collective-permute-start(bf16[256,128]{1,0:T(8,128)(2,1)S(1)} %get-tuple-element.42), channel_id=1, source_target_pairs={{0,16},{1,9},{2,18},{3,11},{4,20},{5,13},{6,22},{7,15},{8,24},{9,1... | collective-permute-start | bytes 196616 | tf_op jit(solution)/shard_map/ppermute | solution.py:134
  23.5 4.0 %collective-permute-start.13 = (bf16[128,128]{1,0:T(8,128)(2,1)S(1)}, bf16[128,128]{1,0:T(8,128)(2,1)S(1)}, u32[]{:S(2)}, u32[]{:S(2)}) collective-permute-start(bf16[128,128]{1,0:T(8,128)(2,1)S(1)} %add_convert_fusion), channel_id=1, source_target_pairs={{0,2},{1,7},{2,0},{3,5},{4,6},{5,3},{6,4},{7,1},{8,10},{9,15},{10,... | collective-permute-start | bytes 98312 | tf_op jit(solution)/shard_map/ppermute | solution.py:134
  23.6 5.4 %collective-permute-start.15 = (bf16[128,128]{1,0:T(8,128)(2,1)S(1)}, bf16[128,128]{1,0:T(8,128)(2,1)S(1)}, u32[]{:S(2)}, u32[]{:S(2)}) collective-permute-start(bf16[128,128]{1,0:T(8,128)(2,1)S(1)} %add_convert_fusion), channel_id=1, source_target_pairs={{0,4},{1,5},{2,6},{3,7},{4,0},{5,1},{6,2},{7,3},{8,12},{9,13},{10,... | collective-permute-start | bytes 98312 | tf_op jit(solution)/shard_map/ppermute | solution.py:134
  27.5 1.5 %collective-permute-start.14 = (bf16[128,128]{1,0:T(8,128)(2,1)S(1)}, bf16[128,128]{1,0:T(8,128)(2,1)S(1)}, u32[]{:S(2)}, u32[]{:S(2)}) collective-permute-start(bf16[128,128]{1,0:T(8,128)(2,1)S(1)} %collective-permute-done.13), channel_id=1, source_target_pairs={{0,1},{1,0},{2,3},{3,2},{4,5},{5,4},{6,7},{7,6},{8,9},{9,8},{10,11... | collective-permute-start | bytes 98312 | tf_op jit(solution)/shard_map/ppermute | solution.py:124

commit v8 on v7

--- a/solution.py
+++ b/solution.py
@@ -29,6 +29,10 @@
 
 def far_steps(size):
     return [0, 1, *range(size - 1, 1, -1)]
+
+
+def row_slots(rows):
+    return [0, 2, 1, *range(3, rows)]
 
 
 def dot(a, b, contract):
@@ -47,7 +51,7 @@
 
 
 def row_steps(rows):
-    return list(zip([2, 1, *range(3, rows)], [1, 2, *range(3, rows)]))
+    return list(zip([1, 2, *range(3, rows)], [2, 1, *range(3, rows)]))
 
 
 def product_kernel(rows, depth, *refs):
@@ -62,7 +66,7 @@
     z, even = lax.div(c, 2), lax.rem(c, 2) == 0
     pairs = []
     for slot, step in enumerate(far_steps(depth)):
-        pair = jnp.where(even, own[slot][...], other[slot][...])
+        pair = jnp.where(even, other[slot][...], own[slot][...])
         pairs.append(pair)
     total[...] = jnp.zeros_like(total)
     targets = targets_ref[...].astype(F32)
@@ -70,15 +74,16 @@
     col_at = lax.broadcasted_iota(jnp.int32, targets.shape, 1)
     for slot, step in enumerate(far_steps(depth)):
         chip = source_of(z, step, depth)
-        for core in range(2):
+        for part in range(2):
+            i = 2 * chip + 1 - part
             for k in range(K):
-                product = dot(blocks_ref[2 * chip + core, k], pairs[slot][core * B : (core + 1) * B], ((0,), (0,)))
-                target = jnp.max(jnp.where((row_at == k) & (col_at == 2 * chip + core), targets, 0.0))
+                product = dot(blocks_ref[i, k], pairs[slot][part * B : (part + 1) * B], ((0,), (0,)))
+                target = jnp.max(jnp.where((row_at == k) & (col_at == i), targets, 0.0))
                 total[target.astype(jnp.int32)] += product
     terms = [total[source_of(r, step, rows)].astype(BF) for step in range(rows)]
     weight = jnp.zeros((F, F), F32)
-    for slot, step in enumerate(far_steps(rows)):
-        feat = jnp.where(even, other[slot][B : 2 * B], own[slot][0:B])
+    for slot, step in enumerate(row_slots(rows)):
+        feat = jnp.where(even, own[slot][0:B], other[slot][B : 2 * B])
         weight += dot(feat, terms[step], ((0,), (0,)))
     term_ref[...] = terms[0]
     weight_ref[...] = weight
@@ -141,10 +146,14 @@
 
     def both(value, slot):
         def row_of(i, core):
-            return i if core == 0 else target_of(i, far_steps(rows)[slot], rows) if slot < rows else None
+            if core == 1:
+                return i
+            return target_of(i, row_slots(rows)[slot], rows) if slot < rows else None
 
         def depth_of(j, core):
-            return j if core == 1 else target_of(j, far_steps(depth)[slot], depth) if slot < depth else None
+            if core == 0:
+                return j
+            return target_of(j, far_steps(depth)[slot], depth) if slot < depth else None
 
         return move(value, row_of, depth_of)
 
@@ -154,7 +163,7 @@
     placed = dot((nodes == order[None, :]).astype(BF), values, ((0,), (0,))).astype(BF)
     grad, pre, feat, place = [placed[:, i * F : (i + 1) * F] for i in range(4)]
     masked = jnp.where(pre > 0, grad, jnp.zeros_like(grad))
-    message = jnp.concatenate([jnp.where(even, masked, feat), across(jnp.where(even, feat, masked))], axis=0)
+    message = jnp.concatenate([jnp.where(even, feat, masked), across(jnp.where(even, masked, feat))], axis=0)
     message, counts = lax.optimization_barrier((message, block_counts))
     filled = jnp.arange(K, dtype=jnp.int32)[:, None] < counts[0, 0][None, :]
     targets = jnp.where(filled, block_cols[0, 0].T, 0)
@@ -182,14 +191,14 @@
     )
     mine = terms[1][B:]
     swapped = across(mine)
-    weights = {0: chip_weight, 1: jnp.where(even, mine, swapped), 2: jnp.where(even, swapped, mine)}
+    weights = {0: chip_weight, 2: jnp.where(even, mine, swapped), 1: jnp.where(even, swapped, mine)}
     weights.update({plan[k][0]: term[B:] for k, term in enumerate(terms) if k > 1})
     row_weight = sum_in_order([weights[step] for step in range(rows)], r, rows).astype(BF)
-    last = depth - 1
-    mine = along_depth(row_weight, (1, last))
-    weights = {step: along_depth(row_weight, (step, step)) for step in range(2, last)}
+    first, second = depth - 2, depth - 1
+    mine = along_depth(row_weight, (first, second))
+    weights = {step: along_depth(row_weight, (step, step)) for step in range(1, first)}
     swapped = across(mine)
-    weights.update({0: row_weight, 1: jnp.where(even, mine, swapped), last: jnp.where(even, swapped, mine)})
+    weights.update({0: row_weight, first: jnp.where(even, mine, swapped), second: jnp.where(even, swapped, mine)})
     summed = sum_in_order([weights[step] for step in range(depth)], z, depth)
     return grad_feat, summed * (slab_rows * rows * cols) ** (-0.5)
 

time: 29.8 us -> 29.1 us (0.977)
  waiting for transfers between devices: 9.85 us -> 8.99 us
    ppermute x8, waiting for transfers between devices: 7.17 us -> 5.79 us  [move(): return lax.ppermute(value, axes, pairs)]
    ppermute x8, waiting for transfers between devices: 2.67 us -> 3.2 us  [across(): return lax.ppermute(value, 'col', [(i, i ^ 1) for i in range(cols)])]
    ppermute x8, starting transfers between devices: 12.7 us -> 13.1 us  [move(): return lax.ppermute(value, axes, pairs)]
where the time goes in v8:
time: 29.1 us; the launch traced here: 28.9 us
  starting transfers between devices  15.1 us (52%)
  waiting for transfers between devices  8.99 us (31%)
  Pallas kernels  1.51 us (5%)
  matrix products  1.11 us (4%)
  other arithmetic  0.9 us (3%)
  between operations  0.72 us (2%)
  local copies, waits for them, and re-layouts  0.59 us (2%)
    ppermute x8, starting transfers between devices, move(): return lax.ppermute(value, axes, pairs)  13.1 us
    ppermute x8, waiting for transfers between devices, move(): return lax.ppermute(value, axes, pairs)  5.79 us
    ppermute x8, waiting for transfers between devices, across(): return lax.ppermute(value, 'col', [(i, i ^ 1) for i in range(cols)])  3.2 us
    ppermute x8, starting transfers between devices, across(): return lax.ppermute(value, 'col', [(i, i ^ 1) for i in range(cols)])  2.01 us
    pallas_call x2, Pallas kernels, call(): pl.pallas_call(body, out_shape=outs, in_specs=[pl.BlockSpec(memory_space=...  1.51 us
    dot_general x1, matrix products, dot(): lax.dot_general(a, b, (contract, ((), ())), preferred_element_type=F32)  1.11 us
    mul x1, other arithmetic, shards(): return (grad_feat, summed * (slab_rows * rows * cols) ** (-0.5))  0.66 us
  transfers between devices with their start and end apart: 16, of which 10 were waited for; matrix products, arithmetic and copies ran while one was open for 1% of the time, Pallas kernels for 3%

profile of v8, /device:TPU:0, one launch (start us, length us, event | category | flops | bytes accessed | tf_op | source)
XLA Modules:
  0.0 28.9 jit_solution(541726870164451369)
XLA Ops:
  0.6 1.1 %convolution_convert_fusion = bf16[128,512]{1,0:T(8,128)(2,1)S(1)} fusion(bf16[128,128]{1,0:T(8,128)(2,1)} %constant.65.clone, bf16[128,128]{1,0:T(8,128)(2,1)} %param.15, bf16[128,128]{1,0:T(8,128)(2,1)} %param.14, bf16[128,128]{1,0:T(8,128)(2,1)} %param.13, s32[128]{0:T(128)} %param.20), kind=kOutput, calls=%fused_computation | convolution fusion | flops 17383424 | bytes 262656 | tf_op jit(solution)/shard_map/dot_general | solution.py:39
  1.8 0.5 %collective-permute-start = (bf16[128,128]{1,0:T(8,128)(2,1)S(1)}, bf16[128,128]{1,0:T(8,128)(2,1)S(1)}, u32[]{:S(2)}, u32[]{:S(2)}) collective-permute-start(bf16[128,128]{1,0:T(8,128)(2,1)S(1)} %get-tuple-element.50), channel_id=1, source_target_pairs={{0,1},{1,0},{2,3},{3,2},{4,5},{5,4},{6,7},{7,6},{8,9},{9,8},{10,11... | collective-permute-start | bytes 98312 | tf_op jit(solution)/shard_map/ppermute | solution.py:129
  2.3 0.9 %collective-permute-done = bf16[128,128]{1,0:T(8,128)(2,1)S(1)} collective-permute-done((bf16[128,128]{1,0:T(8,128)(2,1)S(1)}, bf16[128,128]{1,0:T(8,128)(2,1)S(1)}, u32[]{:S(2)}, u32[]{:S(2)}) %collective-permute-start) | collective-permute-done | bytes 32800 | tf_op jit(solution)/shard_map/ppermute | solution.py:129
  3.2 3.9 %collective-permute-start.3 = (bf16[256,128]{1,0:T(8,128)(2,1)S(1)}, bf16[256,128]{1,0:T(8,128)(2,1)S(1)}, u32[]{:S(2)}, u32[]{:S(2)}) collective-permute-start(bf16[256,128]{1,0:T(8,128)(2,1)S(1)} %pad_maximum_fusion.refs_2_), channel_id=1, source_target_pairs={{0,24},{1,5},{2,26},{3,7},{4,28},{5,1},{6,30},{7,3},{8,16},{9,13},... | collective-permute-start | bytes 196616 | tf_op jit(solution)/shard_map/ppermute | solution.py:139
  7.0 0.5 %collective-permute-start.2 = (bf16[256,128]{1,0:T(8,128)(2,1)S(1)}, bf16[256,128]{1,0:T(8,128)(2,1)S(1)}, u32[]{:S(2)}, u32[]{:S(2)}) collective-permute-start(bf16[256,128]{1,0:T(8,128)(2,1)S(1)} %pad_maximum_fusion.refs_2_), channel_id=1, source_target_pairs={{0,8},{1,7},{2,10},{3,5},{4,12},{5,3},{6,14},{7,1},{8,0},{9,15},{1... | collective-permute-start | bytes 196616 | tf_op jit(solution)/shard_map/ppermute | solution.py:139
  7.9 0.6 %copy-done.2 = s32[1,1,8,2]{2,3,1,0:T(2,128)S(1)} copy-done((s32[1,1,8,2]{2,3,1,0:T(2,128)S(1)}, s32[1,1,8,2]{2,3,1,0:T(2,128)}, u32[]{:S(2)}) %copy-start.2) | copy-done | bytes 88
  8.4 0.6 %collective-permute-start.4 = (bf16[256,128]{1,0:T(8,128)(2,1)S(1)}, bf16[256,128]{1,0:T(8,128)(2,1)S(1)}, u32[]{:S(2)}, u32[]{:S(2)}) collective-permute-start(bf16[256,128]{1,0:T(8,128)(2,1)S(1)} %pad_maximum_fusion.refs_2_), channel_id=1, source_target_pairs={{0,1},{1,0},{2,3},{3,2},{4,5},{5,4},{6,7},{7,6},{8,9},{9,8},{10,11... | collective-permute-start | bytes 196616 | tf_op jit(solution)/shard_map/ppermute | solution.py:129
  9.3 2.0 %collective-permute-done.2.refs_4_ = bf16[256,128]{1,0:T(8,128)(2,1)S(1)} collective-permute-done((bf16[256,128]{1,0:T(8,128)(2,1)S(1)}, bf16[256,128]{1,0:T(8,128)(2,1)S(1)}, u32[]{:S(2)}, u32[]{:S(2)}) %collective-permute-start.2) | collective-permute-done | bytes 65568 | tf_op jit(solution)/shard_map/ppermute | solution.py:139
  11.3 0.6 %collective-permute-start.6 = (bf16[256,128]{1,0:T(8,128)(2,1)S(1)}, bf16[256,128]{1,0:T(8,128)(2,1)S(1)}, u32[]{:S(2)}, u32[]{:S(2)}) collective-permute-start(bf16[256,128]{1,0:T(8,128)(2,1)S(1)} %collective-permute-done.2.refs_4_), channel_id=1, source_target_pairs={{0,1},{1,0},{2,3},{3,2},{4,5},{5,4},{6,7},{7,6},{8,9},{9,8},{10,11... | collective-permute-start | bytes 196616 | tf_op jit(solution)/shard_map/ppermute | solution.py:129
  11.9 0.9 %collective-permute-done.6.refs_8_ = bf16[256,128]{1,0:T(8,128)(2,1)S(1)} collective-permute-done((bf16[256,128]{1,0:T(8,128)(2,1)S(1)}, bf16[256,128]{1,0:T(8,128)(2,1)S(1)}, u32[]{:S(2)}, u32[]{:S(2)}) %collective-permute-start.6) | collective-permute-done | bytes 65568 | tf_op jit(solution)/shard_map/ppermute | solution.py:129
  12.8 0.4 %collective-permute-done.5.refs_7_ = bf16[256,128]{1,0:T(8,128)(2,1)S(1)} collective-permute-done((bf16[256,128]{1,0:T(8,128)(2,1)S(1)}, bf16[256,128]{1,0:T(8,128)(2,1)S(1)}, u32[]{:S(2)}, u32[]{:S(2)}) %collective-permute-start.5) | collective-permute-done | bytes 65568 | tf_op jit(solution)/shard_map/ppermute | solution.py:129
  13.2 0.6 %shard_map.104 = (bf16[128,128]{1,0:T(8,128)(2,1)S(1)}, f32[128,128]{1,0:T(8,128)S(1)}, bf16[256,128]{1,0:T(8,128)(2,1)S(1)}, bf16[256,128]{1,0:T(8,128)(2,1)S(1)}, bf16[256,128]{1,0:T(8,128)(2,1)S(1)}) custom-call(s32[2,8]{1,0:T(2,128)S(1)} %compare_select_fusion.1.refs_0_, bf16[8,2,128,128]{3,2,1,0:T(8,128)(2,1)S(1)} %bitcast_select_fusion.refs_1_, ...), custom_call_target="tpu_custom_call" | custom-call | tf_op jit(solution)/shard_map/pallas_call | solution.py:43
  14.0 1.1 %collective-permute-done.9 = f32[128,128]{1,0:T(8,128)S(1)} collective-permute-done((f32[128,128]{1,0:T(8,128)S(1)}, f32[128,128]{1,0:T(8,128)S(1)}, u32[]{:S(2)}, u32[]{:S(2)}) %collective-permute-start.9) | collective-permute-done | bytes 65568 | tf_op jit(solution)/shard_map/ppermute | solution.py:129
  15.1 1.6 %collective-permute-start.10 = (bf16[256,128]{1,0:T(8,128)(2,1)S(1)}, bf16[256,128]{1,0:T(8,128)(2,1)S(1)}, u32[]{:S(2)}, u32[]{:S(2)}) collective-permute-start(bf16[256,128]{1,0:T(8,128)(2,1)S(1)} %constant_dynamic-update-slice_fusion.1), channel_id=1, source_target_pairs={{0,16},{1,9},{2,18},{3,11},{4,20},{5,13},{6,22},{7,15},{8,24},{9,1... | collective-permute-start | bytes 196616 | tf_op jit(solution)/shard_map/ppermute | solution.py:139
  16.7 1.4 %collective-permute-start.11 = (bf16[256,128]{1,0:T(8,128)(2,1)S(1)}, bf16[256,128]{1,0:T(8,128)(2,1)S(1)}, u32[]{:S(2)}, u32[]{:S(2)}) collective-permute-start(bf16[256,128]{1,0:T(8,128)(2,1)S(1)} %get-tuple-element.46), channel_id=1, source_target_pairs={{0,24},{1,25},{2,26},{3,27},{4,28},{5,29},{6,30},{7,31},{8,16},{9,... | collective-permute-start | bytes 196616 | tf_op jit(solution)/shard_map/ppermute | solution.py:139
  18.2 1.3 %collective-permute-done.10.refs_2_ = bf16[256,128]{1,0:T(8,128)(2,1)S(1)} collective-permute-done((bf16[256,128]{1,0:T(8,128)(2,1)S(1)}, bf16[256,128]{1,0:T(8,128)(2,1)S(1)}, u32[]{:S(2)}, u32[]{:S(2)}) %collective-permute-start.10) | collective-permute-done | bytes 65568 | tf_op jit(solution)/shard_map/ppermute | solution.py:139
  19.5 1.6 %collective-permute-start.8 = (bf16[256,128]{1,0:T(8,128)(2,1)S(1)}, bf16[256,128]{1,0:T(8,128)(2,1)S(1)}, u32[]{:S(2)}, u32[]{:S(2)}) collective-permute-start(bf16[256,128]{1,0:T(8,128)(2,1)S(1)} %get-tuple-element.42), channel_id=1, source_target_pairs={{0,8},{1,17},{2,10},{3,19},{4,12},{5,21},{6,14},{7,23},{8,0},{9,25... | collective-permute-start | bytes 196616 | tf_op jit(solution)/shard_map/ppermute | solution.py:139
  21.0 0.8 %collective-permute-done.11.refs_3_ = bf16[256,128]{1,0:T(8,128)(2,1)S(1)} collective-permute-done((bf16[256,128]{1,0:T(8,128)(2,1)S(1)}, bf16[256,128]{1,0:T(8,128)(2,1)S(1)}, u32[]{:S(2)}, u32[]{:S(2)}) %collective-permute-start.11) | collective-permute-done | bytes 65568 | tf_op jit(solution)/shard_map/ppermute | solution.py:139
  21.9 2.4 %collective-permute-start.14 = (bf16[128,128]{1,0:T(8,128)(2,1)S(1)}, bf16[128,128]{1,0:T(8,128)(2,1)S(1)}, u32[]{:S(2)}, u32[]{:S(2)}) collective-permute-start(bf16[128,128]{1,0:T(8,128)(2,1)S(1)} %add_convert_fusion), channel_id=1, source_target_pairs={{0,4},{1,7},{2,6},{3,5},{4,0},{5,3},{6,2},{7,1},{8,12},{9,15},{10,... | collective-permute-start | bytes 98312 | tf_op jit(solution)/shard_map/ppermute | solution.py:139
  24.3 1.6 %collective-permute-start.13 = (bf16[128,128]{1,0:T(8,128)(2,1)S(1)}, bf16[128,128]{1,0:T(8,128)(2,1)S(1)}, u32[]{:S(2)}, u32[]{:S(2)}) collective-permute-start(bf16[128,128]{1,0:T(8,128)(2,1)S(1)} %add_convert_fusion), channel_id=1, source_target_pairs={{0,2},{1,3},{2,0},{3,1},{4,6},{5,7},{6,4},{7,5},{8,10},{9,11},{10,... | collective-permute-start | bytes 98312 | tf_op jit(solution)/shard_map/ppermute | solution.py:139
  25.9 0.9 %collective-permute-done.14 = bf16[128,128]{1,0:T(8,128)(2,1)S(1)} collective-permute-done((bf16[128,128]{1,0:T(8,128)(2,1)S(1)}, bf16[128,128]{1,0:T(8,128)(2,1)S(1)}, u32[]{:S(2)}, u32[]{:S(2)}) %collective-permute-start.14) | collective-permute-done | bytes 32800 | tf_op jit(solution)/shard_map/ppermute | solution.py:139
  26.8 0.9 %shard_map.105 = bf16[128,128]{1,0:T(8,128)(2,1)} custom-call(bf16[128,128]{1,0:T(8,128)(2,1)S(1)} %get-tuple-element.49.place_ref, bf16[128,128]{1,0:T(8,128)(2,1)S(1)} %copy-done, bf16[128,128]{1,0:T(8,128)(2,1)S(1)} %get-tuple-element.41.refs_0_, bf16[256,128]{1,0:T(8,128)(2,1)S(1)} %collective-permute-done.8.refs_1_, ...), custom_call_target="tpu_custom_call" | custom-call | tf_op jit(solution)/shard_map/pallas_call | solution.py:43
  27.7 0.5 %collective-permute-done.13 = bf16[128,128]{1,0:T(8,128)(2,1)S(1)} collective-permute-done((bf16[128,128]{1,0:T(8,128)(2,1)S(1)}, bf16[128,128]{1,0:T(8,128)(2,1)S(1)}, u32[]{:S(2)}, u32[]{:S(2)}) %collective-permute-start.13) | collective-permute-done | bytes 32800 | tf_op jit(solution)/shard_map/ppermute | solution.py:139
  28.3 0.7 %add_multiply_fusion = f32[128,128]{1,0:T(8,128)} fusion(bf16[128,128]{1,0:T(8,128)(2,1)S(1)} %collective-permute-done.13, bf16[128,128]{1,0:T(8,128)(2,1)S(1)} %add_convert_fusion, bf16[128,128]{1,0:T(8,128)(2,1)S(1)} %collective-permute-done.15, bf16[128,128]{1,0:T(8,128)(2,1)S(1)} %collective-permute-done.14, pred[]{:T(512)S(6)} %eq.13), kind=kLoop, calls=%fused_computation.10 | loop fusion | flops 163840 | bytes 196609 | tf_op jit(solution)/shard_map/mul | solution.py:203
  (29 shorter events, 0.8 us)
Async XLA Ops:
  0.6 7.1 %copy-start.1 = (bf16[1,1,8,2,128,128]{5,4,3,2,1,0:T(8,128)(2,1)S(1)}, bf16[1,1,8,2,128,128]{5,4,3,2,1,0:T(8,128)(2,1)}, u32[]{:S(2)}) copy-start(bf16[1,1,8,2,128,128]{5,4,3,2,1,0:T(8,128)(2,1)} %param.17) | copy-start | bytes 1572868
  1.8 1.4 %collective-permute-start = (bf16[128,128]{1,0:T(8,128)(2,1)S(1)}, bf16[128,128]{1,0:T(8,128)(2,1)S(1)}, u32[]{:S(2)}, u32[]{:S(2)}) collective-permute-start(bf16[128,128]{1,0:T(8,128)(2,1)S(1)} %get-tuple-element.50), channel_id=1, source_target_pairs={{0,1},{1,0},{2,3},{3,2},{4,5},{5,4},{6,7},{7,6},{8,9},{9,8},{10,11... | collective-permute-start | bytes 98312 | tf_op jit(solution)/shard_map/ppermute | solution.py:129
  3.2 4.5 %copy-start.3 = (s32[1,1,8]{2,1,0:T(1,128)S(1)}, s32[1,1,8]{2,1,0:T(1,128)}, u32[]{:S(2)}) copy-start(s32[1,1,8]{2,1,0:T(1,128)} %param.19) | copy-start | bytes 100
  3.2 6.1 %collective-permute-start.3 = (bf16[256,128]{1,0:T(8,128)(2,1)S(1)}, bf16[256,128]{1,0:T(8,128)(2,1)S(1)}, u32[]{:S(2)}, u32[]{:S(2)}) collective-permute-start(bf16[256,128]{1,0:T(8,128)(2,1)S(1)} %pad_maximum_fusion.refs_2_), channel_id=1, source_target_pairs={{0,24},{1,5},{2,26},{3,7},{4,28},{5,1},{6,30},{7,3},{8,16},{9,13},... | collective-permute-start | bytes 196616 | tf_op jit(solution)/shard_map/ppermute | solution.py:139
  7.0 4.3 %collective-permute-start.2 = (bf16[256,128]{1,0:T(8,128)(2,1)S(1)}, bf16[256,128]{1,0:T(8,128)(2,1)S(1)}, u32[]{:S(2)}, u32[]{:S(2)}) collective-permute-start(bf16[256,128]{1,0:T(8,128)(2,1)S(1)} %pad_maximum_fusion.refs_2_), channel_id=1, source_target_pairs={{0,8},{1,7},{2,10},{3,5},{4,12},{5,3},{6,14},{7,1},{8,0},{9,15},{1... | collective-permute-start | bytes 196616 | tf_op jit(solution)/shard_map/ppermute | solution.py:139
  7.6 4.4 %collective-permute-start.1 = (bf16[256,128]{1,0:T(8,128)(2,1)S(1)}, bf16[256,128]{1,0:T(8,128)(2,1)S(1)}, u32[]{:S(2)}, u32[]{:S(2)}) collective-permute-start(bf16[256,128]{1,0:T(8,128)(2,1)S(1)} %pad_maximum_fusion.refs_2_), channel_id=1, source_target_pairs={{0,16},{1,3},{2,18},{3,1},{4,20},{5,7},{6,22},{7,5},{8,24},{9,11},... | collective-permute-start | bytes 196616 | tf_op jit(solution)/shard_map/ppermute | solution.py:139
  7.7 0.7 %copy-start.2 = (s32[1,1,8,2]{2,3,1,0:T(2,128)S(1)}, s32[1,1,8,2]{2,3,1,0:T(2,128)}, u32[]{:S(2)}) copy-start(s32[1,1,8,2]{2,3,1,0:T(2,128)} %param.18) | copy-start | bytes 196
  8.4 3.5 %collective-permute-start.4 = (bf16[256,128]{1,0:T(8,128)(2,1)S(1)}, bf16[256,128]{1,0:T(8,128)(2,1)S(1)}, u32[]{:S(2)}, u32[]{:S(2)}) collective-permute-start(bf16[256,128]{1,0:T(8,128)(2,1)S(1)} %pad_maximum_fusion.refs_2_), channel_id=1, source_target_pairs={{0,1},{1,0},{2,3},{3,2},{4,5},{5,4},{6,7},{7,6},{8,9},{9,8},{10,11... | collective-permute-start | bytes 196616 | tf_op jit(solution)/shard_map/ppermute | solution.py:129
  9.3 2.7 %collective-permute-start.7 = (bf16[256,128]{1,0:T(8,128)(2,1)S(1)}, bf16[256,128]{1,0:T(8,128)(2,1)S(1)}, u32[]{:S(2)}, u32[]{:S(2)}) collective-permute-start(bf16[256,128]{1,0:T(8,128)(2,1)S(1)} %collective-permute-done.3.refs_5_), channel_id=1, source_target_pairs={{0,1},{1,0},{2,3},{3,2},{4,5},{5,4},{6,7},{7,6},{8,9},{9,8},{10,11... | collective-permute-start | bytes 196616 | tf_op jit(solution)/shard_map/ppermute | solution.py:129
  11.3 1.5 %collective-permute-start.6 = (bf16[256,128]{1,0:T(8,128)(2,1)S(1)}, bf16[256,128]{1,0:T(8,128)(2,1)S(1)}, u32[]{:S(2)}, u32[]{:S(2)}) collective-permute-start(bf16[256,128]{1,0:T(8,128)(2,1)S(1)} %collective-permute-done.2.refs_4_), channel_id=1, source_target_pairs={{0,1},{1,0},{2,3},{3,2},{4,5},{5,4},{6,7},{7,6},{8,9},{9,8},{10,11... | collective-permute-start | bytes 196616 | tf_op jit(solution)/shard_map/ppermute | solution.py:129
  11.9 1.3 %collective-permute-start.5 = (bf16[256,128]{1,0:T(8,128)(2,1)S(1)}, bf16[256,128]{1,0:T(8,128)(2,1)S(1)}, u32[]{:S(2)}, u32[]{:S(2)}) collective-permute-start(bf16[256,128]{1,0:T(8,128)(2,1)S(1)} %collective-permute-done.1.refs_3_), channel_id=1, source_target_pairs={{0,1},{1,0},{2,3},{3,2},{4,5},{5,4},{6,7},{7,6},{8,9},{9,8},{10,11... | collective-permute-start | bytes 196616 | tf_op jit(solution)/shard_map/ppermute | solution.py:129
  13.8 1.3 %collective-permute-start.9 = (f32[128,128]{1,0:T(8,128)S(1)}, f32[128,128]{1,0:T(8,128)S(1)}, u32[]{:S(2)}, u32[]{:S(2)}) collective-permute-start(f32[128,128]{1,0:T(8,128)S(1)} %get-tuple-element.44), channel_id=1, source_target_pairs={{0,1},{1,0},{2,3},{3,2},{4,5},{5,4},{6,7},{7,6},{8,9},{9,8},{10,11... | collective-permute-start | bytes 196616 | tf_op jit(solution)/shard_map/ppermute | solution.py:129
  15.1 4.3 %collective-permute-start.10 = (bf16[256,128]{1,0:T(8,128)(2,1)S(1)}, bf16[256,128]{1,0:T(8,128)(2,1)S(1)}, u32[]{:S(2)}, u32[]{:S(2)}) collective-permute-start(bf16[256,128]{1,0:T(8,128)(2,1)S(1)} %constant_dynamic-update-slice_fusion.1), channel_id=1, source_target_pairs={{0,16},{1,9},{2,18},{3,11},{4,20},{5,13},{6,22},{7,15},{8,24},{9,1... | collective-permute-start | bytes 196616 | tf_op jit(solution)/shard_map/ppermute | solution.py:139
  16.7 5.2 %collective-permute-start.11 = (bf16[256,128]{1,0:T(8,128)(2,1)S(1)}, bf16[256,128]{1,0:T(8,128)(2,1)S(1)}, u32[]{:S(2)}, u32[]{:S(2)}) collective-permute-start(bf16[256,128]{1,0:T(8,128)(2,1)S(1)} %get-tuple-element.46), channel_id=1, source_target_pairs={{0,24},{1,25},{2,26},{3,27},{4,28},{5,29},{6,30},{7,31},{8,16},{9,... | collective-permute-start | bytes 196616 | tf_op jit(solution)/shard_map/ppermute | solution.py:139
  19.5 2.4 %collective-permute-start.12 = (bf16[128,128]{1,0:T(8,128)(2,1)S(1)}, bf16[128,128]{1,0:T(8,128)(2,1)S(1)}, u32[]{:S(2)}, u32[]{:S(2)}) collective-permute-start(bf16[128,128]{1,0:T(8,128)(2,1)S(1)} %slice.62), channel_id=1, source_target_pairs={{0,1},{1,0},{2,3},{3,2},{4,5},{5,4},{6,7},{7,6},{8,9},{9,8},{10,11... | collective-permute-start | bytes 98312 | tf_op jit(solution)/shard_map/ppermute | solution.py:129
  19.5 7.3 %copy-start = (bf16[128,128]{1,0:T(8,128)(2,1)S(1)}, bf16[128,128]{1,0:T(8,128)(2,1)}, u32[]{:S(2)}) copy-start(bf16[128,128]{1,0:T(8,128)(2,1)} %weight_ref.1) | copy-start | bytes 98308
  19.5 7.3 %collective-permute-start.8 = (bf16[256,128]{1,0:T(8,128)(2,1)S(1)}, bf16[256,128]{1,0:T(8,128)(2,1)S(1)}, u32[]{:S(2)}, u32[]{:S(2)}) collective-permute-start(bf16[256,128]{1,0:T(8,128)(2,1)S(1)} %get-tuple-element.42), channel_id=1, source_target_pairs={{0,8},{1,17},{2,10},{3,19},{4,12},{5,21},{6,14},{7,23},{8,0},{9,25... | collective-permute-start | bytes 196616 | tf_op jit(solution)/shard_map/ppermute | solution.py:139
  21.9 4.9 %collective-permute-start.14 = (bf16[128,128]{1,0:T(8,128)(2,1)S(1)}, bf16[128,128]{1,0:T(8,128)(2,1)S(1)}, u32[]{:S(2)}, u32[]{:S(2)}) collective-permute-start(bf16[128,128]{1,0:T(8,128)(2,1)S(1)} %add_convert_fusion), channel_id=1, source_target_pairs={{0,4},{1,7},{2,6},{3,5},{4,0},{5,3},{6,2},{7,1},{8,12},{9,15},{10,... | collective-permute-start | bytes 98312 | tf_op jit(solution)/shard_map/ppermute | solution.py:139
  24.3 3.9 %collective-permute-start.13 = (bf16[128,128]{1,0:T(8,128)(2,1)S(1)}, bf16[128,128]{1,0:T(8,128)(2,1)S(1)}, u32[]{:S(2)}, u32[]{:S(2)}) collective-permute-start(bf16[128,128]{1,0:T(8,128)(2,1)S(1)} %add_convert_fusion), channel_id=1, source_target_pairs={{0,2},{1,3},{2,0},{3,1},{4,6},{5,7},{6,4},{7,5},{8,10},{9,11},{10,... | collective-permute-start | bytes 98312 | tf_op jit(solution)/shard_map/ppermute | solution.py:139
  26.8 1.5 %collective-permute-start.15 = (bf16[128,128]{1,0:T(8,128)(2,1)S(1)}, bf16[128,128]{1,0:T(8,128)(2,1)S(1)}, u32[]{:S(2)}, u32[]{:S(2)}) collective-permute-start(bf16[128,128]{1,0:T(8,128)(2,1)S(1)} %collective-permute-done.14), channel_id=1, source_target_pairs={{0,1},{1,0},{2,3},{3,2},{4,5},{5,4},{6,7},{7,6},{8,9},{9,8},{10,11... | collective-permute-start | bytes 98312 | tf_op jit(solution)/shard_map/ppermute | solution.py:129

commit v9 on v8

--- a/solution.py
+++ b/solution.py
@@ -32,7 +32,7 @@
 
 
 def row_slots(rows):
-    return [0, 2, 1, *range(3, rows)]
+    return [0, *range(2, rows), 1]
 
 
 def dot(a, b, contract):
@@ -113,6 +113,11 @@
     out_ref[...] = dot(place_ref[...], grad, ((0,), (0,))).astype(BF)
 
 
+def last_kernel(scale, grad_ref, weight_ref, grad_out, weight_out):
+    grad_out[...] = grad_ref[...]
+    weight_out[...] = weight_ref[...] * scale
+
+
 def shards(grad_out, pre_act, features, weight, blocks, block_cols, block_counts, order):
     slab_rows = grad_out.shape[0]
     rows = lax.axis_size("row")
@@ -166,11 +171,12 @@
     message = jnp.concatenate([jnp.where(even, feat, masked), across(jnp.where(even, masked, feat))], axis=0)
     message, counts = lax.optimization_barrier((message, block_counts))
     filled = jnp.arange(K, dtype=jnp.int32)[:, None] < counts[0, 0][None, :]
-    targets = jnp.where(filled, block_cols[0, 0].T, 0)
+    used = jnp.arange(K, dtype=jnp.int32)[:, None] < block_counts[0, 0][None, :]
+    targets = jnp.where(used, block_cols[0, 0].T, 0)
     blocks = jnp.where(filled.T[:, :, None, None], blocks[0, 0], jnp.zeros((), BF))
     steps = max(rows, depth)
     own = [message] + [both(message, slot) for slot in range(1, steps)]
-    held, targets, blocks = lax.optimization_barrier((message, targets, blocks))
+    held, blocks = lax.optimization_barrier((message, blocks))
     other = [across(value) for value in (held, *own[1:])]
     term, weight_term, *messages = call(
         functools.partial(product_kernel, rows, depth),
@@ -199,8 +205,12 @@
     weights = {step: along_depth(row_weight, (step, step)) for step in range(1, first)}
     swapped = across(mine)
     weights.update({0: row_weight, first: jnp.where(even, mine, swapped), second: jnp.where(even, swapped, mine)})
+    scale = (slab_rows * rows * cols) ** (-0.5)
     summed = sum_in_order([weights[step] for step in range(depth)], z, depth)
-    return grad_feat, summed * (slab_rows * rows * cols) ** (-0.5)
+    grad_feat, summed = call(
+        functools.partial(last_kernel, scale), [slab, jax.ShapeDtypeStruct((F, F), F32)], (grad_feat, summed), [pltpu.VMEM] * 2
+    )
+    return grad_feat, summed
 
 
 def solution(mesh):

time: 29.1 us -> 29.1 us (level)
  waiting for transfers between devices: 8.99 us -> 9.99 us
  other arithmetic: 0.9 us -> 0.27 us
  local copies, waits for them, and re-layouts: 0.59 us -> 0.03 us
    ppermute x8, waiting for transfers between devices: 5.79 us -> 6.8 us  [move(): return lax.ppermute(value, axes, pairs)]
    mul x1 -> x0, other arithmetic: 0.66 us -> none  [shards(): return (grad_feat, summed * (slab_rows * rows * cols) ** (-0.5))]
    unnamed x8, local copies, waits for them, and re-layouts: 0.58 us -> 0.02 us
    pallas_call x2 -> x3, Pallas kernels: 1.51 us -> 1.54 us  [call(): pl.pallas_call(body, out_shape=outs, in_specs=[pl.BlockSpec(memory_space=...]
  transfers between devices with their start and end apart: 16 -> 16, of which waited for: 10 -> 9; matrix products, arithmetic and copies ran while one was open for 1% -> 1% of each run, Pallas kernels for 3% -> 1%
where the time goes in v9:
time: 29.1 us; the launch traced here: 28.9 us
  starting transfers between devices  15.2 us (52%)
  waiting for transfers between devices  9.99 us (34%)
  Pallas kernels  1.54 us (5%)
  matrix products  1.11 us (4%)
  between operations  0.75 us (3%)
    ppermute x8, starting transfers between devices, move(): return lax.ppermute(value, axes, pairs)  13 us
    ppermute x8, waiting for transfers between devices, move(): return lax.ppermute(value, axes, pairs)  6.8 us
    ppermute x8, waiting for transfers between devices, across(): return lax.ppermute(value, 'col', [(i, i ^ 1) for i in range(cols)])  3.19 us
    ppermute x8, starting transfers between devices, across(): return lax.ppermute(value, 'col', [(i, i ^ 1) for i in range(cols)])  2.26 us
    pallas_call x3, Pallas kernels, call(): pl.pallas_call(body, out_shape=outs, in_specs=[pl.BlockSpec(memory_space=...  1.54 us
    dot_general x1, matrix products, dot(): lax.dot_general(a, b, (contract, ((), ())), preferred_element_type=F32)  1.11 us
  transfers between devices with their start and end apart: 16, of which 9 were waited for; matrix products, arithmetic and copies ran while one was open for 1% of the time, Pallas kernels for 1%

profile of v9, /device:TPU:0, one launch (start us, length us, event | category | flops | bytes accessed | tf_op | source)
XLA Modules:
  0.0 28.9 jit_solution(194857446893435557)
XLA Ops:
  0.6 1.1 %convolution_convert_fusion = bf16[128,512]{1,0:T(8,128)(2,1)S(1)} fusion(bf16[128,128]{1,0:T(8,128)(2,1)} %constant.63.clone, bf16[128,128]{1,0:T(8,128)(2,1)} %param.15, bf16[128,128]{1,0:T(8,128)(2,1)} %param.14, bf16[128,128]{1,0:T(8,128)(2,1)} %param.13, s32[128]{0:T(128)} %param.20), kind=kOutput, calls=%fused_computation | convolution fusion | flops 17383424 | bytes 262656 | tf_op jit(solution)/shard_map/dot_general | solution.py:39
  1.8 0.5 %collective-permute-start = (bf16[128,128]{1,0:T(8,128)(2,1)S(1)}, bf16[128,128]{1,0:T(8,128)(2,1)S(1)}, u32[]{:S(2)}, u32[]{:S(2)}) collective-permute-start(bf16[128,128]{1,0:T(8,128)(2,1)S(1)} %get-tuple-element.48), channel_id=1, source_target_pairs={{0,1},{1,0},{2,3},{3,2},{4,5},{5,4},{6,7},{7,6},{8,9},{9,8},{10,11... | collective-permute-start | bytes 98312 | tf_op jit(solution)/shard_map/ppermute | solution.py:134
  2.3 0.9 %collective-permute-done = bf16[128,128]{1,0:T(8,128)(2,1)S(1)} collective-permute-done((bf16[128,128]{1,0:T(8,128)(2,1)S(1)}, bf16[128,128]{1,0:T(8,128)(2,1)S(1)}, u32[]{:S(2)}, u32[]{:S(2)}) %collective-permute-start) | collective-permute-done | bytes 32800 | tf_op jit(solution)/shard_map/ppermute | solution.py:134
  3.2 2.9 %collective-permute-start.3 = (bf16[256,128]{1,0:T(8,128)(2,1)S(1)}, bf16[256,128]{1,0:T(8,128)(2,1)S(1)}, u32[]{:S(2)}, u32[]{:S(2)}) collective-permute-start(bf16[256,128]{1,0:T(8,128)(2,1)S(1)} %pad_maximum_fusion.refs_2_), channel_id=1, source_target_pairs={{0,8},{1,5},{2,10},{3,7},{4,12},{5,1},{6,14},{7,3},{8,0},{9,13},{1... | collective-permute-start | bytes 196616 | tf_op jit(solution)/shard_map/ppermute | solution.py:144
  6.1 1.5 %collective-permute-start.2 = (bf16[256,128]{1,0:T(8,128)(2,1)S(1)}, bf16[256,128]{1,0:T(8,128)(2,1)S(1)}, u32[]{:S(2)}, u32[]{:S(2)}) collective-permute-start(bf16[256,128]{1,0:T(8,128)(2,1)S(1)} %pad_maximum_fusion.refs_2_), channel_id=1, source_target_pairs={{0,24},{1,7},{2,26},{3,5},{4,28},{5,3},{6,30},{7,1},{8,16},{9,15},... | collective-permute-start | bytes 196616 | tf_op jit(solution)/shard_map/ppermute | solution.py:144
  7.8 0.8 %collective-permute-start.4 = (bf16[256,128]{1,0:T(8,128)(2,1)S(1)}, bf16[256,128]{1,0:T(8,128)(2,1)S(1)}, u32[]{:S(2)}, u32[]{:S(2)}) collective-permute-start(bf16[256,128]{1,0:T(8,128)(2,1)S(1)} %pad_maximum_fusion.refs_2_), channel_id=1, source_target_pairs={{0,1},{1,0},{2,3},{3,2},{4,5},{5,4},{6,7},{7,6},{8,9},{9,8},{10,11... | collective-permute-start | bytes 196616 | tf_op jit(solution)/shard_map/ppermute | solution.py:134
  8.7 2.6 %collective-permute-done.2.refs_4_ = bf16[256,128]{1,0:T(8,128)(2,1)S(1)} collective-permute-done((bf16[256,128]{1,0:T(8,128)(2,1)S(1)}, bf16[256,128]{1,0:T(8,128)(2,1)S(1)}, u32[]{:S(2)}, u32[]{:S(2)}) %collective-permute-start.2) | collective-permute-done | bytes 65568 | tf_op jit(solution)/shard_map/ppermute | solution.py:144
  11.2 0.7 %collective-permute-start.6 = (bf16[256,128]{1,0:T(8,128)(2,1)S(1)}, bf16[256,128]{1,0:T(8,128)(2,1)S(1)}, u32[]{:S(2)}, u32[]{:S(2)}) collective-permute-start(bf16[256,128]{1,0:T(8,128)(2,1)S(1)} %collective-permute-done.2.refs_4_), channel_id=1, source_target_pairs={{0,1},{1,0},{2,3},{3,2},{4,5},{5,4},{6,7},{7,6},{8,9},{9,8},{10,11... | collective-permute-start | bytes 196616 | tf_op jit(solution)/shard_map/ppermute | solution.py:134
  12.0 0.8 %collective-permute-done.6.refs_8_ = bf16[256,128]{1,0:T(8,128)(2,1)S(1)} collective-permute-done((bf16[256,128]{1,0:T(8,128)(2,1)S(1)}, bf16[256,128]{1,0:T(8,128)(2,1)S(1)}, u32[]{:S(2)}, u32[]{:S(2)}) %collective-permute-start.6) | collective-permute-done | bytes 65568 | tf_op jit(solution)/shard_map/ppermute | solution.py:134
  12.8 0.4 %collective-permute-done.5.refs_7_ = bf16[256,128]{1,0:T(8,128)(2,1)S(1)} collective-permute-done((bf16[256,128]{1,0:T(8,128)(2,1)S(1)}, bf16[256,128]{1,0:T(8,128)(2,1)S(1)}, u32[]{:S(2)}, u32[]{:S(2)}) %collective-permute-start.5) | collective-permute-done | bytes 65568 | tf_op jit(solution)/shard_map/ppermute | solution.py:134
  13.2 0.6 %shard_map.104 = (bf16[128,128]{1,0:T(8,128)(2,1)S(1)}, f32[128,128]{1,0:T(8,128)S(1)}, bf16[256,128]{1,0:T(8,128)(2,1)S(1)}, bf16[256,128]{1,0:T(8,128)(2,1)S(1)}, bf16[256,128]{1,0:T(8,128)(2,1)S(1)}) custom-call(s32[2,8]{1,0:T(2,128)S(1)} %compare_select_fusion.1.refs_0_, bf16[8,2,128,128]{3,2,1,0:T(8,128)(2,1)S(1)} %bitcast_select_fusion.refs_1_, ...), custom_call_target="tpu_custom_call" | custom-call | tf_op jit(solution)/shard_map/pallas_call | solution.py:43
  13.8 0.2 collective-permute-start.9
  14.0 1.1 %collective-permute-done.9 = f32[128,128]{1,0:T(8,128)S(1)} collective-permute-done((f32[128,128]{1,0:T(8,128)S(1)}, f32[128,128]{1,0:T(8,128)S(1)}, u32[]{:S(2)}, u32[]{:S(2)}) %collective-permute-start.9) | collective-permute-done | bytes 65568 | tf_op jit(solution)/shard_map/ppermute | solution.py:134
  15.2 1.6 %collective-permute-start.10 = (bf16[256,128]{1,0:T(8,128)(2,1)S(1)}, bf16[256,128]{1,0:T(8,128)(2,1)S(1)}, u32[]{:S(2)}, u32[]{:S(2)}) collective-permute-start(bf16[256,128]{1,0:T(8,128)(2,1)S(1)} %constant_dynamic-update-slice_fusion.1), channel_id=1, source_target_pairs={{0,16},{1,9},{2,18},{3,11},{4,20},{5,13},{6,22},{7,15},{8,24},{9,1... | collective-permute-start | bytes 196616 | tf_op jit(solution)/shard_map/ppermute | solution.py:144
  16.7 1.4 %collective-permute-start.11 = (bf16[256,128]{1,0:T(8,128)(2,1)S(1)}, bf16[256,128]{1,0:T(8,128)(2,1)S(1)}, u32[]{:S(2)}, u32[]{:S(2)}) collective-permute-start(bf16[256,128]{1,0:T(8,128)(2,1)S(1)} %get-tuple-element.44), channel_id=1, source_target_pairs={{0,24},{1,25},{2,26},{3,27},{4,28},{5,29},{6,30},{7,31},{8,16},{9,... | collective-permute-start | bytes 196616 | tf_op jit(solution)/shard_map/ppermute | solution.py:144
  18.2 1.3 %collective-permute-done.10.refs_2_ = bf16[256,128]{1,0:T(8,128)(2,1)S(1)} collective-permute-done((bf16[256,128]{1,0:T(8,128)(2,1)S(1)}, bf16[256,128]{1,0:T(8,128)(2,1)S(1)}, u32[]{:S(2)}, u32[]{:S(2)}) %collective-permute-start.10) | collective-permute-done | bytes 65568 | tf_op jit(solution)/shard_map/ppermute | solution.py:144
  19.5 1.5 %collective-permute-start.8 = (bf16[256,128]{1,0:T(8,128)(2,1)S(1)}, bf16[256,128]{1,0:T(8,128)(2,1)S(1)}, u32[]{:S(2)}, u32[]{:S(2)}) collective-permute-start(bf16[256,128]{1,0:T(8,128)(2,1)S(1)} %get-tuple-element.40), channel_id=1, source_target_pairs={{0,8},{1,17},{2,10},{3,19},{4,12},{5,21},{6,14},{7,23},{8,0},{9,25... | collective-permute-start | bytes 196616 | tf_op jit(solution)/shard_map/ppermute | solution.py:144
  21.0 0.8 %collective-permute-done.11.refs_3_ = bf16[256,128]{1,0:T(8,128)(2,1)S(1)} collective-permute-done((bf16[256,128]{1,0:T(8,128)(2,1)S(1)}, bf16[256,128]{1,0:T(8,128)(2,1)S(1)}, u32[]{:S(2)}, u32[]{:S(2)}) %collective-permute-start.11) | collective-permute-done | bytes 65568 | tf_op jit(solution)/shard_map/ppermute | solution.py:144
  21.9 2.4 %collective-permute-start.14 = (bf16[128,128]{1,0:T(8,128)(2,1)S(1)}, bf16[128,128]{1,0:T(8,128)(2,1)S(1)}, u32[]{:S(2)}, u32[]{:S(2)}) collective-permute-start(bf16[128,128]{1,0:T(8,128)(2,1)S(1)} %add_convert_fusion), channel_id=1, source_target_pairs={{0,4},{1,7},{2,6},{3,5},{4,0},{5,3},{6,2},{7,1},{8,12},{9,15},{10,... | collective-permute-start | bytes 98312 | tf_op jit(solution)/shard_map/ppermute | solution.py:144
  24.3 1.6 %collective-permute-start.13 = (bf16[128,128]{1,0:T(8,128)(2,1)S(1)}, bf16[128,128]{1,0:T(8,128)(2,1)S(1)}, u32[]{:S(2)}, u32[]{:S(2)}) collective-permute-start(bf16[128,128]{1,0:T(8,128)(2,1)S(1)} %add_convert_fusion), channel_id=1, source_target_pairs={{0,2},{1,3},{2,0},{3,1},{4,6},{5,7},{6,4},{7,5},{8,10},{9,11},{10,... | collective-permute-start | bytes 98312 | tf_op jit(solution)/shard_map/ppermute | solution.py:144
  25.9 0.9 %collective-permute-done.14 = bf16[128,128]{1,0:T(8,128)(2,1)S(1)} collective-permute-done((bf16[128,128]{1,0:T(8,128)(2,1)S(1)}, bf16[128,128]{1,0:T(8,128)(2,1)S(1)}, u32[]{:S(2)}, u32[]{:S(2)}) %collective-permute-start.14) | collective-permute-done | bytes 32800 | tf_op jit(solution)/shard_map/ppermute | solution.py:144
  26.8 0.3 %shard_map.105.grad_ref = bf16[128,128]{1,0:T(8,128)(2,1)S(1)} custom-call(bf16[128,128]{1,0:T(8,128)(2,1)S(1)} %get-tuple-element.47.place_ref, bf16[128,128]{1,0:T(8,128)(2,1)S(1)} %copy-done, bf16[128,128]{1,0:T(8,128)(2,1)S(1)} %get-tuple-element.39.refs_0_, bf16[256,128]{1,0:T(8,128)(2,1)S(1)} %collective-permute-done.8.refs_1_, ...), custom_call_target="tpu_custom_call" | custom-call | tf_op jit(solution)/shard_map/pallas_call | solution.py:43
  27.1 1.1 %collective-permute-done.13 = bf16[128,128]{1,0:T(8,128)(2,1)S(1)} collective-permute-done((bf16[128,128]{1,0:T(8,128)(2,1)S(1)}, bf16[128,128]{1,0:T(8,128)(2,1)S(1)}, u32[]{:S(2)}, u32[]{:S(2)}) %collective-permute-start.13) | collective-permute-done | bytes 32800 | tf_op jit(solution)/shard_map/ppermute | solution.py:144
  28.3 0.6 %shard_map.106 = (bf16[128,128]{1,0:T(8,128)(2,1)}, f32[128,128]{1,0:T(8,128)}) custom-call(bf16[128,128]{1,0:T(8,128)(2,1)S(1)} %shard_map.105.grad_ref, f32[128,128]{1,0:T(8,128)S(1)} %add_add_fusion.weight_ref), custom_call_target="tpu_custom_call" | custom-call | tf_op jit(solution)/shard_map/pallas_call | solution.py:43
  (30 shorter events, 0.5 us)
Async XLA Ops:
  0.6 7.1 %copy-start.1 = (bf16[1,1,8,2,128,128]{5,4,3,2,1,0:T(8,128)(2,1)S(1)}, bf16[1,1,8,2,128,128]{5,4,3,2,1,0:T(8,128)(2,1)}, u32[]{:S(2)}) copy-start(bf16[1,1,8,2,128,128]{5,4,3,2,1,0:T(8,128)(2,1)} %param.17) | copy-start | bytes 1572868
  1.8 1.4 %collective-permute-start = (bf16[128,128]{1,0:T(8,128)(2,1)S(1)}, bf16[128,128]{1,0:T(8,128)(2,1)S(1)}, u32[]{:S(2)}, u32[]{:S(2)}) collective-permute-start(bf16[128,128]{1,0:T(8,128)(2,1)S(1)} %get-tuple-element.48), channel_id=1, source_target_pairs={{0,1},{1,0},{2,3},{3,2},{4,5},{5,4},{6,7},{7,6},{8,9},{9,8},{10,11... | collective-permute-start | bytes 98312 | tf_op jit(solution)/shard_map/ppermute | solution.py:134
  3.2 4.4 %copy-start.3 = (s32[1,1,8]{2,1,0:T(1,128)S(1)}, s32[1,1,8]{2,1,0:T(1,128)}, u32[]{:S(2)}) copy-start(s32[1,1,8]{2,1,0:T(1,128)} %param.19) | copy-start | bytes 100
  3.2 5.4 %collective-permute-start.3 = (bf16[256,128]{1,0:T(8,128)(2,1)S(1)}, bf16[256,128]{1,0:T(8,128)(2,1)S(1)}, u32[]{:S(2)}, u32[]{:S(2)}) collective-permute-start(bf16[256,128]{1,0:T(8,128)(2,1)S(1)} %pad_maximum_fusion.refs_2_), channel_id=1, source_target_pairs={{0,8},{1,5},{2,10},{3,7},{4,12},{5,1},{6,14},{7,3},{8,0},{9,13},{1... | collective-permute-start | bytes 196616 | tf_op jit(solution)/shard_map/ppermute | solution.py:144
  6.1 5.2 %collective-permute-start.2 = (bf16[256,128]{1,0:T(8,128)(2,1)S(1)}, bf16[256,128]{1,0:T(8,128)(2,1)S(1)}, u32[]{:S(2)}, u32[]{:S(2)}) collective-permute-start(bf16[256,128]{1,0:T(8,128)(2,1)S(1)} %pad_maximum_fusion.refs_2_), channel_id=1, source_target_pairs={{0,24},{1,7},{2,26},{3,5},{4,28},{5,3},{6,30},{7,1},{8,16},{9,15},... | collective-permute-start | bytes 196616 | tf_op jit(solution)/shard_map/ppermute | solution.py:144
  7.6 4.4 %collective-permute-start.1 = (bf16[256,128]{1,0:T(8,128)(2,1)S(1)}, bf16[256,128]{1,0:T(8,128)(2,1)S(1)}, u32[]{:S(2)}, u32[]{:S(2)}) collective-permute-start(bf16[256,128]{1,0:T(8,128)(2,1)S(1)} %pad_maximum_fusion.refs_2_), channel_id=1, source_target_pairs={{0,16},{1,3},{2,18},{3,1},{4,20},{5,7},{6,22},{7,5},{8,24},{9,11},... | collective-permute-start | bytes 196616 | tf_op jit(solution)/shard_map/ppermute | solution.py:144
  7.8 4.1 %copy-start.2 = (s32[1,1,8,2]{2,3,1,0:T(2,128)S(1)}, s32[1,1,8,2]{2,3,1,0:T(2,128)}, u32[]{:S(2)}) copy-start(s32[1,1,8,2]{2,3,1,0:T(2,128)} %param.18) | copy-start | bytes 196
  7.8 4.1 %collective-permute-start.4 = (bf16[256,128]{1,0:T(8,128)(2,1)S(1)}, bf16[256,128]{1,0:T(8,128)(2,1)S(1)}, u32[]{:S(2)}, u32[]{:S(2)}) collective-permute-start(bf16[256,128]{1,0:T(8,128)(2,1)S(1)} %pad_maximum_fusion.refs_2_), channel_id=1, source_target_pairs={{0,1},{1,0},{2,3},{3,2},{4,5},{5,4},{6,7},{7,6},{8,9},{9,8},{10,11... | collective-permute-start | bytes 196616 | tf_op jit(solution)/shard_map/ppermute | solution.py:134
  8.6 3.4 %collective-permute-start.7 = (bf16[256,128]{1,0:T(8,128)(2,1)S(1)}, bf16[256,128]{1,0:T(8,128)(2,1)S(1)}, u32[]{:S(2)}, u32[]{:S(2)}) collective-permute-start(bf16[256,128]{1,0:T(8,128)(2,1)S(1)} %collective-permute-done.3.refs_5_), channel_id=1, source_target_pairs={{0,1},{1,0},{2,3},{3,2},{4,5},{5,4},{6,7},{7,6},{8,9},{9,8},{10,11... | collective-permute-start | bytes 196616 | tf_op jit(solution)/shard_map/ppermute | solution.py:134
  11.2 1.6 %collective-permute-start.6 = (bf16[256,128]{1,0:T(8,128)(2,1)S(1)}, bf16[256,128]{1,0:T(8,128)(2,1)S(1)}, u32[]{:S(2)}, u32[]{:S(2)}) collective-permute-start(bf16[256,128]{1,0:T(8,128)(2,1)S(1)} %collective-permute-done.2.refs_4_), channel_id=1, source_target_pairs={{0,1},{1,0},{2,3},{3,2},{4,5},{5,4},{6,7},{7,6},{8,9},{9,8},{10,11... | collective-permute-start | bytes 196616 | tf_op jit(solution)/shard_map/ppermute | solution.py:134
  11.9 1.3 %collective-permute-start.5 = (bf16[256,128]{1,0:T(8,128)(2,1)S(1)}, bf16[256,128]{1,0:T(8,128)(2,1)S(1)}, u32[]{:S(2)}, u32[]{:S(2)}) collective-permute-start(bf16[256,128]{1,0:T(8,128)(2,1)S(1)} %collective-permute-done.1.refs_3_), channel_id=1, source_target_pairs={{0,1},{1,0},{2,3},{3,2},{4,5},{5,4},{6,7},{7,6},{8,9},{9,8},{10,11... | collective-permute-start | bytes 196616 | tf_op jit(solution)/shard_map/ppermute | solution.py:134
  13.8 1.3 %collective-permute-start.9 = (f32[128,128]{1,0:T(8,128)S(1)}, f32[128,128]{1,0:T(8,128)S(1)}, u32[]{:S(2)}, u32[]{:S(2)}) collective-permute-start(f32[128,128]{1,0:T(8,128)S(1)} %get-tuple-element.42), channel_id=1, source_target_pairs={{0,1},{1,0},{2,3},{3,2},{4,5},{5,4},{6,7},{7,6},{8,9},{9,8},{10,11... | collective-permute-start | bytes 196616 | tf_op jit(solution)/shard_map/ppermute | solution.py:134
  15.2 4.3 %collective-permute-start.10 = (bf16[256,128]{1,0:T(8,128)(2,1)S(1)}, bf16[256,128]{1,0:T(8,128)(2,1)S(1)}, u32[]{:S(2)}, u32[]{:S(2)}) collective-permute-start(bf16[256,128]{1,0:T(8,128)(2,1)S(1)} %constant_dynamic-update-slice_fusion.1), channel_id=1, source_target_pairs={{0,16},{1,9},{2,18},{3,11},{4,20},{5,13},{6,22},{7,15},{8,24},{9,1... | collective-permute-start | bytes 196616 | tf_op jit(solution)/shard_map/ppermute | solution.py:144
  16.7 5.2 %collective-permute-start.11 = (bf16[256,128]{1,0:T(8,128)(2,1)S(1)}, bf16[256,128]{1,0:T(8,128)(2,1)S(1)}, u32[]{:S(2)}, u32[]{:S(2)}) collective-permute-start(bf16[256,128]{1,0:T(8,128)(2,1)S(1)} %get-tuple-element.44), channel_id=1, source_target_pairs={{0,24},{1,25},{2,26},{3,27},{4,28},{5,29},{6,30},{7,31},{8,16},{9,... | collective-permute-start | bytes 196616 | tf_op jit(solution)/shard_map/ppermute | solution.py:144
  19.5 2.4 %collective-permute-start.12 = (bf16[128,128]{1,0:T(8,128)(2,1)S(1)}, bf16[128,128]{1,0:T(8,128)(2,1)S(1)}, u32[]{:S(2)}, u32[]{:S(2)}) collective-permute-start(bf16[128,128]{1,0:T(8,128)(2,1)S(1)} %slice.62), channel_id=1, source_target_pairs={{0,1},{1,0},{2,3},{3,2},{4,5},{5,4},{6,7},{7,6},{8,9},{9,8},{10,11... | collective-permute-start | bytes 98312 | tf_op jit(solution)/shard_map/ppermute | solution.py:134
  19.5 7.3 %copy-start = (bf16[128,128]{1,0:T(8,128)(2,1)S(1)}, bf16[128,128]{1,0:T(8,128)(2,1)}, u32[]{:S(2)}) copy-start(bf16[128,128]{1,0:T(8,128)(2,1)} %weight_ref.1) | copy-start | bytes 98308
  19.5 7.3 %collective-permute-start.8 = (bf16[256,128]{1,0:T(8,128)(2,1)S(1)}, bf16[256,128]{1,0:T(8,128)(2,1)S(1)}, u32[]{:S(2)}, u32[]{:S(2)}) collective-permute-start(bf16[256,128]{1,0:T(8,128)(2,1)S(1)} %get-tuple-element.40), channel_id=1, source_target_pairs={{0,8},{1,17},{2,10},{3,19},{4,12},{5,21},{6,14},{7,23},{8,0},{9,25... | collective-permute-start | bytes 196616 | tf_op jit(solution)/shard_map/ppermute | solution.py:144
  21.9 4.9 %collective-permute-start.14 = (bf16[128,128]{1,0:T(8,128)(2,1)S(1)}, bf16[128,128]{1,0:T(8,128)(2,1)S(1)}, u32[]{:S(2)}, u32[]{:S(2)}) collective-permute-start(bf16[128,128]{1,0:T(8,128)(2,1)S(1)} %add_convert_fusion), channel_id=1, source_target_pairs={{0,4},{1,7},{2,6},{3,5},{4,0},{5,3},{6,2},{7,1},{8,12},{9,15},{10,... | collective-permute-start | bytes 98312 | tf_op jit(solution)/shard_map/ppermute | solution.py:144
  24.3 3.9 %collective-permute-start.13 = (bf16[128,128]{1,0:T(8,128)(2,1)S(1)}, bf16[128,128]{1,0:T(8,128)(2,1)S(1)}, u32[]{:S(2)}, u32[]{:S(2)}) collective-permute-start(bf16[128,128]{1,0:T(8,128)(2,1)S(1)} %add_convert_fusion), channel_id=1, source_target_pairs={{0,2},{1,3},{2,0},{3,1},{4,6},{5,7},{6,4},{7,5},{8,10},{9,11},{10,... | collective-permute-start | bytes 98312 | tf_op jit(solution)/shard_map/ppermute | solution.py:144
  26.8 1.5 %collective-permute-start.15 = (bf16[128,128]{1,0:T(8,128)(2,1)S(1)}, bf16[128,128]{1,0:T(8,128)(2,1)S(1)}, u32[]{:S(2)}, u32[]{:S(2)}) collective-permute-start(bf16[128,128]{1,0:T(8,128)(2,1)S(1)} %collective-permute-done.14), channel_id=1, source_target_pairs={{0,1},{1,0},{2,3},{3,2},{4,5},{5,4},{6,7},{7,6},{8,9},{9,8},{10,11... | collective-permute-start | bytes 98312 | tf_op jit(solution)/shard_map/ppermute | solution.py:134

commit v10 on v9

--- a/solution.py
+++ b/solution.py
@@ -86,7 +86,7 @@
         feat = jnp.where(even, own[slot][0:B], other[slot][B : 2 * B])
         weight += dot(feat, terms[step], ((0,), (0,)))
     term_ref[...] = terms[0]
-    weight_ref[...] = weight
+    weight_ref[...] = weight.astype(BF)
     sent = terms if swaps(rows) else [terms[-step] for step in range(rows)]
     for out, (first, second) in zip(outs, row_steps(rows)):
         out[0:B] = jnp.where(even, sent[first], sent[second])
@@ -180,7 +180,7 @@
     other = [across(value) for value in (held, *own[1:])]
     term, weight_term, *messages = call(
         functools.partial(product_kernel, rows, depth),
-        [slab, jax.ShapeDtypeStruct((F, F), F32), pair] + [pair] * (rows - 2),
+        [slab, slab, pair] + [pair] * (rows - 2),
         (targets, blocks, *own, *other),
         [pltpu.VMEM] * (2 + 2 * steps),
         scratch=[
@@ -188,7 +188,7 @@
         ],
         limit=limit,
     )
-    chip_weight = (weight_term + across(weight_term)).astype(BF)
+    chip_weight = (weight_term.astype(F32) + across(weight_term).astype(F32)).astype(BF)
     plan = row_steps(rows)
     terms = [along_row(messages[0], plan[0])]
     terms += [along_row(m.at[B:].set(chip_weight), plan[i]) for i, m in enumerate(messages) if i > 0]

time: 29.1 us -> 29 us (level)
  no operation moved by 1% of the time
where the time goes in v10:
time: 29 us; the launch traced here: 28.9 us
  starting transfers between devices  15.3 us (53%)
  waiting for transfers between devices  9.93 us (34%)
  Pallas kernels  1.55 us (5%)
  matrix products  1.11 us (4%)
  between operations  0.75 us (3%)
    ppermute x8, starting transfers between devices, move(): return lax.ppermute(value, axes, pairs)  13 us
    ppermute x8, waiting for transfers between devices, move(): return lax.ppermute(value, axes, pairs)  6.79 us
    ppermute x8, waiting for transfers between devices, across(): return lax.ppermute(value, 'col', [(i, i ^ 1) for i in range(cols)])  3.14 us
    ppermute x8, starting transfers between devices, across(): return lax.ppermute(value, 'col', [(i, i ^ 1) for i in range(cols)])  2.27 us
    pallas_call x3, Pallas kernels, call(): pl.pallas_call(body, out_shape=outs, in_specs=[pl.BlockSpec(memory_space=...  1.55 us
    dot_general x1, matrix products, dot(): lax.dot_general(a, b, (contract, ((), ())), preferred_element_type=F32)  1.11 us
  transfers between devices with their start and end apart: 16, of which 9 were waited for; matrix products, arithmetic and copies ran while one was open for 1% of the time, Pallas kernels for 1%

profile of v10, /device:TPU:0, one launch (start us, length us, event | category | flops | bytes accessed | tf_op | source)
XLA Modules:
  0.0 28.9 jit_solution(790096931476396733)
XLA Ops:
  0.6 1.1 %convolution_convert_fusion = bf16[128,512]{1,0:T(8,128)(2,1)S(1)} fusion(bf16[128,128]{1,0:T(8,128)(2,1)} %constant.63.clone, bf16[128,128]{1,0:T(8,128)(2,1)} %param.15, bf16[128,128]{1,0:T(8,128)(2,1)} %param.14, bf16[128,128]{1,0:T(8,128)(2,1)} %param.13, s32[128]{0:T(128)} %param.20), kind=kOutput, calls=%fused_computation | convolution fusion | flops 17383424 | bytes 262656 | tf_op jit(solution)/shard_map/dot_general | solution.py:39
  1.8 0.5 %collective-permute-start = (bf16[128,128]{1,0:T(8,128)(2,1)S(1)}, bf16[128,128]{1,0:T(8,128)(2,1)S(1)}, u32[]{:S(2)}, u32[]{:S(2)}) collective-permute-start(bf16[128,128]{1,0:T(8,128)(2,1)S(1)} %get-tuple-element.46), channel_id=1, source_target_pairs={{0,1},{1,0},{2,3},{3,2},{4,5},{5,4},{6,7},{7,6},{8,9},{9,8},{10,11... | collective-permute-start | bytes 98312 | tf_op jit(solution)/shard_map/ppermute | solution.py:134
  2.3 0.9 %collective-permute-done = bf16[128,128]{1,0:T(8,128)(2,1)S(1)} collective-permute-done((bf16[128,128]{1,0:T(8,128)(2,1)S(1)}, bf16[128,128]{1,0:T(8,128)(2,1)S(1)}, u32[]{:S(2)}, u32[]{:S(2)}) %collective-permute-start) | collective-permute-done | bytes 32800 | tf_op jit(solution)/shard_map/ppermute | solution.py:134
  3.2 2.9 %collective-permute-start.3 = (bf16[256,128]{1,0:T(8,128)(2,1)S(1)}, bf16[256,128]{1,0:T(8,128)(2,1)S(1)}, u32[]{:S(2)}, u32[]{:S(2)}) collective-permute-start(bf16[256,128]{1,0:T(8,128)(2,1)S(1)} %pad_maximum_fusion.refs_2_), channel_id=1, source_target_pairs={{0,8},{1,5},{2,10},{3,7},{4,12},{5,1},{6,14},{7,3},{8,0},{9,13},{1... | collective-permute-start | bytes 196616 | tf_op jit(solution)/shard_map/ppermute | solution.py:144
  6.1 1.5 %collective-permute-start.2 = (bf16[256,128]{1,0:T(8,128)(2,1)S(1)}, bf16[256,128]{1,0:T(8,128)(2,1)S(1)}, u32[]{:S(2)}, u32[]{:S(2)}) collective-permute-start(bf16[256,128]{1,0:T(8,128)(2,1)S(1)} %pad_maximum_fusion.refs_2_), channel_id=1, source_target_pairs={{0,24},{1,7},{2,26},{3,5},{4,28},{5,3},{6,30},{7,1},{8,16},{9,15},... | collective-permute-start | bytes 196616 | tf_op jit(solution)/shard_map/ppermute | solution.py:144
  7.8 0.8 %collective-permute-start.4 = (bf16[256,128]{1,0:T(8,128)(2,1)S(1)}, bf16[256,128]{1,0:T(8,128)(2,1)S(1)}, u32[]{:S(2)}, u32[]{:S(2)}) collective-permute-start(bf16[256,128]{1,0:T(8,128)(2,1)S(1)} %pad_maximum_fusion.refs_2_), channel_id=1, source_target_pairs={{0,1},{1,0},{2,3},{3,2},{4,5},{5,4},{6,7},{7,6},{8,9},{9,8},{10,11... | collective-permute-start | bytes 196616 | tf_op jit(solution)/shard_map/ppermute | solution.py:134
  8.7 2.6 %collective-permute-done.2.refs_4_ = bf16[256,128]{1,0:T(8,128)(2,1)S(1)} collective-permute-done((bf16[256,128]{1,0:T(8,128)(2,1)S(1)}, bf16[256,128]{1,0:T(8,128)(2,1)S(1)}, u32[]{:S(2)}, u32[]{:S(2)}) %collective-permute-start.2) | collective-permute-done | bytes 65568 | tf_op jit(solution)/shard_map/ppermute | solution.py:144
  11.2 0.7 %collective-permute-start.6 = (bf16[256,128]{1,0:T(8,128)(2,1)S(1)}, bf16[256,128]{1,0:T(8,128)(2,1)S(1)}, u32[]{:S(2)}, u32[]{:S(2)}) collective-permute-start(bf16[256,128]{1,0:T(8,128)(2,1)S(1)} %collective-permute-done.2.refs_4_), channel_id=1, source_target_pairs={{0,1},{1,0},{2,3},{3,2},{4,5},{5,4},{6,7},{7,6},{8,9},{9,8},{10,11... | collective-permute-start | bytes 196616 | tf_op jit(solution)/shard_map/ppermute | solution.py:134
  12.0 0.8 %collective-permute-done.6.refs_8_ = bf16[256,128]{1,0:T(8,128)(2,1)S(1)} collective-permute-done((bf16[256,128]{1,0:T(8,128)(2,1)S(1)}, bf16[256,128]{1,0:T(8,128)(2,1)S(1)}, u32[]{:S(2)}, u32[]{:S(2)}) %collective-permute-start.6) | collective-permute-done | bytes 65568 | tf_op jit(solution)/shard_map/ppermute | solution.py:134
  12.8 0.4 %collective-permute-done.5.refs_7_ = bf16[256,128]{1,0:T(8,128)(2,1)S(1)} collective-permute-done((bf16[256,128]{1,0:T(8,128)(2,1)S(1)}, bf16[256,128]{1,0:T(8,128)(2,1)S(1)}, u32[]{:S(2)}, u32[]{:S(2)}) %collective-permute-start.5) | collective-permute-done | bytes 65568 | tf_op jit(solution)/shard_map/ppermute | solution.py:134
  13.2 0.6 %shard_map.104 = (bf16[128,128]{1,0:T(8,128)(2,1)S(1)}, bf16[128,128]{1,0:T(8,128)(2,1)S(1)}, bf16[256,128]{1,0:T(8,128)(2,1)S(1)}, bf16[256,128]{1,0:T(8,128)(2,1)S(1)}, bf16[256,128]{1,0:T(8,128)(2,1)S(1)}) custom-call(s32[2,8]{1,0:T(2,128)S(1)} %compare_select_fusion.1.refs_0_, bf16[8,2,128,128]{3,2,1,0:T(8,128)(2,1)S(1)} %bitcast_select_fusion.refs_1_, ...), custom_call_target="tpu_custom_call" | custom-call | tf_op jit(solution)/shard_map/pallas_call | solution.py:43
  13.8 0.2 collective-permute-start.9
  14.0 1.0 %collective-permute-done.9 = bf16[128,128]{1,0:T(8,128)(2,1)S(1)} collective-permute-done((bf16[128,128]{1,0:T(8,128)(2,1)S(1)}, bf16[128,128]{1,0:T(8,128)(2,1)S(1)}, u32[]{:S(2)}, u32[]{:S(2)}) %collective-permute-start.9) | collective-permute-done | bytes 32800 | tf_op jit(solution)/shard_map/ppermute | solution.py:134
  15.1 1.6 %collective-permute-start.10 = (bf16[256,128]{1,0:T(8,128)(2,1)S(1)}, bf16[256,128]{1,0:T(8,128)(2,1)S(1)}, u32[]{:S(2)}, u32[]{:S(2)}) collective-permute-start(bf16[256,128]{1,0:T(8,128)(2,1)S(1)} %get-tuple-element.48), channel_id=1, source_target_pairs={{0,16},{1,9},{2,18},{3,11},{4,20},{5,13},{6,22},{7,15},{8,24},{9,1... | collective-permute-start | bytes 196616 | tf_op jit(solution)/shard_map/ppermute | solution.py:144
  16.7 1.4 %collective-permute-start.11 = (bf16[256,128]{1,0:T(8,128)(2,1)S(1)}, bf16[256,128]{1,0:T(8,128)(2,1)S(1)}, u32[]{:S(2)}, u32[]{:S(2)}) collective-permute-start(bf16[256,128]{1,0:T(8,128)(2,1)S(1)} %get-tuple-element.47), channel_id=1, source_target_pairs={{0,24},{1,25},{2,26},{3,27},{4,28},{5,29},{6,30},{7,31},{8,16},{9,... | collective-permute-start | bytes 196616 | tf_op jit(solution)/shard_map/ppermute | solution.py:144
  18.1 1.3 %collective-permute-done.10.refs_2_ = bf16[256,128]{1,0:T(8,128)(2,1)S(1)} collective-permute-done((bf16[256,128]{1,0:T(8,128)(2,1)S(1)}, bf16[256,128]{1,0:T(8,128)(2,1)S(1)}, u32[]{:S(2)}, u32[]{:S(2)}) %collective-permute-start.10) | collective-permute-done | bytes 65568 | tf_op jit(solution)/shard_map/ppermute | solution.py:144
  19.4 1.5 %collective-permute-start.8 = (bf16[256,128]{1,0:T(8,128)(2,1)S(1)}, bf16[256,128]{1,0:T(8,128)(2,1)S(1)}, u32[]{:S(2)}, u32[]{:S(2)}) collective-permute-start(bf16[256,128]{1,0:T(8,128)(2,1)S(1)} %get-tuple-element.40), channel_id=1, source_target_pairs={{0,8},{1,17},{2,10},{3,19},{4,12},{5,21},{6,14},{7,23},{8,0},{9,25... | collective-permute-start | bytes 196616 | tf_op jit(solution)/shard_map/ppermute | solution.py:144
  21.0 0.8 %collective-permute-done.11.refs_3_ = bf16[256,128]{1,0:T(8,128)(2,1)S(1)} collective-permute-done((bf16[256,128]{1,0:T(8,128)(2,1)S(1)}, bf16[256,128]{1,0:T(8,128)(2,1)S(1)}, u32[]{:S(2)}, u32[]{:S(2)}) %collective-permute-start.11) | collective-permute-done | bytes 65568 | tf_op jit(solution)/shard_map/ppermute | solution.py:144
  21.9 2.4 %collective-permute-start.14 = (bf16[128,128]{1,0:T(8,128)(2,1)S(1)}, bf16[128,128]{1,0:T(8,128)(2,1)S(1)}, u32[]{:S(2)}, u32[]{:S(2)}) collective-permute-start(bf16[128,128]{1,0:T(8,128)(2,1)S(1)} %add_convert_fusion), channel_id=1, source_target_pairs={{0,4},{1,7},{2,6},{3,5},{4,0},{5,3},{6,2},{7,1},{8,12},{9,15},{10,... | collective-permute-start | bytes 98312 | tf_op jit(solution)/shard_map/ppermute | solution.py:144
  24.3 1.6 %collective-permute-start.13 = (bf16[128,128]{1,0:T(8,128)(2,1)S(1)}, bf16[128,128]{1,0:T(8,128)(2,1)S(1)}, u32[]{:S(2)}, u32[]{:S(2)}) collective-permute-start(bf16[128,128]{1,0:T(8,128)(2,1)S(1)} %add_convert_fusion), channel_id=1, source_target_pairs={{0,2},{1,3},{2,0},{3,1},{4,6},{5,7},{6,4},{7,5},{8,10},{9,11},{10,... | collective-permute-start | bytes 98312 | tf_op jit(solution)/shard_map/ppermute | solution.py:144
  25.9 0.9 %collective-permute-done.14 = bf16[128,128]{1,0:T(8,128)(2,1)S(1)} collective-permute-done((bf16[128,128]{1,0:T(8,128)(2,1)S(1)}, bf16[128,128]{1,0:T(8,128)(2,1)S(1)}, u32[]{:S(2)}, u32[]{:S(2)}) %collective-permute-start.14) | collective-permute-done | bytes 32800 | tf_op jit(solution)/shard_map/ppermute | solution.py:144
  26.8 0.3 %shard_map.105.grad_ref = bf16[128,128]{1,0:T(8,128)(2,1)S(1)} custom-call(bf16[128,128]{1,0:T(8,128)(2,1)S(1)} %get-tuple-element.45.place_ref, bf16[128,128]{1,0:T(8,128)(2,1)S(1)} %copy-done, bf16[128,128]{1,0:T(8,128)(2,1)S(1)} %get-tuple-element.39.refs_0_, bf16[256,128]{1,0:T(8,128)(2,1)S(1)} %collective-permute-done.8.refs_1_, ...), custom_call_target="tpu_custom_call" | custom-call | tf_op jit(solution)/shard_map/pallas_call | solution.py:43
  27.1 1.1 %collective-permute-done.13 = bf16[128,128]{1,0:T(8,128)(2,1)S(1)} collective-permute-done((bf16[128,128]{1,0:T(8,128)(2,1)S(1)}, bf16[128,128]{1,0:T(8,128)(2,1)S(1)}, u32[]{:S(2)}, u32[]{:S(2)}) %collective-permute-start.13) | collective-permute-done | bytes 32800 | tf_op jit(solution)/shard_map/ppermute | solution.py:144
  28.2 0.6 %shard_map.106 = (bf16[128,128]{1,0:T(8,128)(2,1)}, f32[128,128]{1,0:T(8,128)}) custom-call(bf16[128,128]{1,0:T(8,128)(2,1)S(1)} %shard_map.105.grad_ref, f32[128,128]{1,0:T(8,128)S(1)} %add_add_fusion.weight_ref), custom_call_target="tpu_custom_call" | custom-call | tf_op jit(solution)/shard_map/pallas_call | solution.py:43
  (29 shorter events, 0.5 us)
Async XLA Ops:
  0.6 7.1 %copy-start.1 = (bf16[1,1,8,2,128,128]{5,4,3,2,1,0:T(8,128)(2,1)S(1)}, bf16[1,1,8,2,128,128]{5,4,3,2,1,0:T(8,128)(2,1)}, u32[]{:S(2)}) copy-start(bf16[1,1,8,2,128,128]{5,4,3,2,1,0:T(8,128)(2,1)} %param.17) | copy-start | bytes 1572868
  1.8 1.4 %collective-permute-start = (bf16[128,128]{1,0:T(8,128)(2,1)S(1)}, bf16[128,128]{1,0:T(8,128)(2,1)S(1)}, u32[]{:S(2)}, u32[]{:S(2)}) collective-permute-start(bf16[128,128]{1,0:T(8,128)(2,1)S(1)} %get-tuple-element.46), channel_id=1, source_target_pairs={{0,1},{1,0},{2,3},{3,2},{4,5},{5,4},{6,7},{7,6},{8,9},{9,8},{10,11... | collective-permute-start | bytes 98312 | tf_op jit(solution)/shard_map/ppermute | solution.py:134
  3.2 4.4 %copy-start.3 = (s32[1,1,8]{2,1,0:T(1,128)S(1)}, s32[1,1,8]{2,1,0:T(1,128)}, u32[]{:S(2)}) copy-start(s32[1,1,8]{2,1,0:T(1,128)} %param.19) | copy-start | bytes 100
  3.2 5.4 %collective-permute-start.3 = (bf16[256,128]{1,0:T(8,128)(2,1)S(1)}, bf16[256,128]{1,0:T(8,128)(2,1)S(1)}, u32[]{:S(2)}, u32[]{:S(2)}) collective-permute-start(bf16[256,128]{1,0:T(8,128)(2,1)S(1)} %pad_maximum_fusion.refs_2_), channel_id=1, source_target_pairs={{0,8},{1,5},{2,10},{3,7},{4,12},{5,1},{6,14},{7,3},{8,0},{9,13},{1... | collective-permute-start | bytes 196616 | tf_op jit(solution)/shard_map/ppermute | solution.py:144
  6.1 5.2 %collective-permute-start.2 = (bf16[256,128]{1,0:T(8,128)(2,1)S(1)}, bf16[256,128]{1,0:T(8,128)(2,1)S(1)}, u32[]{:S(2)}, u32[]{:S(2)}) collective-permute-start(bf16[256,128]{1,0:T(8,128)(2,1)S(1)} %pad_maximum_fusion.refs_2_), channel_id=1, source_target_pairs={{0,24},{1,7},{2,26},{3,5},{4,28},{5,3},{6,30},{7,1},{8,16},{9,15},... | collective-permute-start | bytes 196616 | tf_op jit(solution)/shard_map/ppermute | solution.py:144
  7.6 4.4 %collective-permute-start.1 = (bf16[256,128]{1,0:T(8,128)(2,1)S(1)}, bf16[256,128]{1,0:T(8,128)(2,1)S(1)}, u32[]{:S(2)}, u32[]{:S(2)}) collective-permute-start(bf16[256,128]{1,0:T(8,128)(2,1)S(1)} %pad_maximum_fusion.refs_2_), channel_id=1, source_target_pairs={{0,16},{1,3},{2,18},{3,1},{4,20},{5,7},{6,22},{7,5},{8,24},{9,11},... | collective-permute-start | bytes 196616 | tf_op jit(solution)/shard_map/ppermute | solution.py:144
  7.8 4.1 %copy-start.2 = (s32[1,1,8,2]{2,3,1,0:T(2,128)S(1)}, s32[1,1,8,2]{2,3,1,0:T(2,128)}, u32[]{:S(2)}) copy-start(s32[1,1,8,2]{2,3,1,0:T(2,128)} %param.18) | copy-start | bytes 196
  7.8 4.1 %collective-permute-start.4 = (bf16[256,128]{1,0:T(8,128)(2,1)S(1)}, bf16[256,128]{1,0:T(8,128)(2,1)S(1)}, u32[]{:S(2)}, u32[]{:S(2)}) collective-permute-start(bf16[256,128]{1,0:T(8,128)(2,1)S(1)} %pad_maximum_fusion.refs_2_), channel_id=1, source_target_pairs={{0,1},{1,0},{2,3},{3,2},{4,5},{5,4},{6,7},{7,6},{8,9},{9,8},{10,11... | collective-permute-start | bytes 196616 | tf_op jit(solution)/shard_map/ppermute | solution.py:134
  8.6 3.4 %collective-permute-start.7 = (bf16[256,128]{1,0:T(8,128)(2,1)S(1)}, bf16[256,128]{1,0:T(8,128)(2,1)S(1)}, u32[]{:S(2)}, u32[]{:S(2)}) collective-permute-start(bf16[256,128]{1,0:T(8,128)(2,1)S(1)} %collective-permute-done.3.refs_5_), channel_id=1, source_target_pairs={{0,1},{1,0},{2,3},{3,2},{4,5},{5,4},{6,7},{7,6},{8,9},{9,8},{10,11... | collective-permute-start | bytes 196616 | tf_op jit(solution)/shard_map/ppermute | solution.py:134
  11.2 1.6 %collective-permute-start.6 = (bf16[256,128]{1,0:T(8,128)(2,1)S(1)}, bf16[256,128]{1,0:T(8,128)(2,1)S(1)}, u32[]{:S(2)}, u32[]{:S(2)}) collective-permute-start(bf16[256,128]{1,0:T(8,128)(2,1)S(1)} %collective-permute-done.2.refs_4_), channel_id=1, source_target_pairs={{0,1},{1,0},{2,3},{3,2},{4,5},{5,4},{6,7},{7,6},{8,9},{9,8},{10,11... | collective-permute-start | bytes 196616 | tf_op jit(solution)/shard_map/ppermute | solution.py:134
  11.9 1.3 %collective-permute-start.5 = (bf16[256,128]{1,0:T(8,128)(2,1)S(1)}, bf16[256,128]{1,0:T(8,128)(2,1)S(1)}, u32[]{:S(2)}, u32[]{:S(2)}) collective-permute-start(bf16[256,128]{1,0:T(8,128)(2,1)S(1)} %collective-permute-done.1.refs_3_), channel_id=1, source_target_pairs={{0,1},{1,0},{2,3},{3,2},{4,5},{5,4},{6,7},{7,6},{8,9},{9,8},{10,11... | collective-permute-start | bytes 196616 | tf_op jit(solution)/shard_map/ppermute | solution.py:134
  13.8 1.3 %collective-permute-start.9 = (bf16[128,128]{1,0:T(8,128)(2,1)S(1)}, bf16[128,128]{1,0:T(8,128)(2,1)S(1)}, u32[]{:S(2)}, u32[]{:S(2)}) collective-permute-start(bf16[128,128]{1,0:T(8,128)(2,1)S(1)} %get-tuple-element.42), channel_id=1, source_target_pairs={{0,1},{1,0},{2,3},{3,2},{4,5},{5,4},{6,7},{7,6},{8,9},{9,8},{10,11... | collective-permute-start | bytes 98312 | tf_op jit(solution)/shard_map/ppermute | solution.py:134
  15.1 4.3 %collective-permute-start.10 = (bf16[256,128]{1,0:T(8,128)(2,1)S(1)}, bf16[256,128]{1,0:T(8,128)(2,1)S(1)}, u32[]{:S(2)}, u32[]{:S(2)}) collective-permute-start(bf16[256,128]{1,0:T(8,128)(2,1)S(1)} %get-tuple-element.48), channel_id=1, source_target_pairs={{0,16},{1,9},{2,18},{3,11},{4,20},{5,13},{6,22},{7,15},{8,24},{9,1... | collective-permute-start | bytes 196616 | tf_op jit(solution)/shard_map/ppermute | solution.py:144
  16.7 5.2 %collective-permute-start.11 = (bf16[256,128]{1,0:T(8,128)(2,1)S(1)}, bf16[256,128]{1,0:T(8,128)(2,1)S(1)}, u32[]{:S(2)}, u32[]{:S(2)}) collective-permute-start(bf16[256,128]{1,0:T(8,128)(2,1)S(1)} %get-tuple-element.47), channel_id=1, source_target_pairs={{0,24},{1,25},{2,26},{3,27},{4,28},{5,29},{6,30},{7,31},{8,16},{9,... | collective-permute-start | bytes 196616 | tf_op jit(solution)/shard_map/ppermute | solution.py:144
  19.4 2.4 %collective-permute-start.12 = (bf16[128,128]{1,0:T(8,128)(2,1)S(1)}, bf16[128,128]{1,0:T(8,128)(2,1)S(1)}, u32[]{:S(2)}, u32[]{:S(2)}) collective-permute-start(bf16[128,128]{1,0:T(8,128)(2,1)S(1)} %slice.62), channel_id=1, source_target_pairs={{0,1},{1,0},{2,3},{3,2},{4,5},{5,4},{6,7},{7,6},{8,9},{9,8},{10,11... | collective-permute-start | bytes 98312 | tf_op jit(solution)/shard_map/ppermute | solution.py:134
  19.4 7.3 %copy-start = (bf16[128,128]{1,0:T(8,128)(2,1)S(1)}, bf16[128,128]{1,0:T(8,128)(2,1)}, u32[]{:S(2)}) copy-start(bf16[128,128]{1,0:T(8,128)(2,1)} %weight_ref.1) | copy-start | bytes 98308
  19.4 7.3 %collective-permute-start.8 = (bf16[256,128]{1,0:T(8,128)(2,1)S(1)}, bf16[256,128]{1,0:T(8,128)(2,1)S(1)}, u32[]{:S(2)}, u32[]{:S(2)}) collective-permute-start(bf16[256,128]{1,0:T(8,128)(2,1)S(1)} %get-tuple-element.40), channel_id=1, source_target_pairs={{0,8},{1,17},{2,10},{3,19},{4,12},{5,21},{6,14},{7,23},{8,0},{9,25... | collective-permute-start | bytes 196616 | tf_op jit(solution)/shard_map/ppermute | solution.py:144
  21.9 4.9 %collective-permute-start.14 = (bf16[128,128]{1,0:T(8,128)(2,1)S(1)}, bf16[128,128]{1,0:T(8,128)(2,1)S(1)}, u32[]{:S(2)}, u32[]{:S(2)}) collective-permute-start(bf16[128,128]{1,0:T(8,128)(2,1)S(1)} %add_convert_fusion), channel_id=1, source_target_pairs={{0,4},{1,7},{2,6},{3,5},{4,0},{5,3},{6,2},{7,1},{8,12},{9,15},{10,... | collective-permute-start | bytes 98312 | tf_op jit(solution)/shard_map/ppermute | solution.py:144
  24.3 3.9 %collective-permute-start.13 = (bf16[128,128]{1,0:T(8,128)(2,1)S(1)}, bf16[128,128]{1,0:T(8,128)(2,1)S(1)}, u32[]{:S(2)}, u32[]{:S(2)}) collective-permute-start(bf16[128,128]{1,0:T(8,128)(2,1)S(1)} %add_convert_fusion), channel_id=1, source_target_pairs={{0,2},{1,3},{2,0},{3,1},{4,6},{5,7},{6,4},{7,5},{8,10},{9,11},{10,... | collective-permute-start | bytes 98312 | tf_op jit(solution)/shard_map/ppermute | solution.py:144
  26.8 1.4 %collective-permute-start.15 = (bf16[128,128]{1,0:T(8,128)(2,1)S(1)}, bf16[128,128]{1,0:T(8,128)(2,1)S(1)}, u32[]{:S(2)}, u32[]{:S(2)}) collective-permute-start(bf16[128,128]{1,0:T(8,128)(2,1)S(1)} %collective-permute-done.14), channel_id=1, source_target_pairs={{0,1},{1,0},{2,3},{3,2},{4,5},{5,4},{6,7},{7,6},{8,9},{9,8},{10,11... | collective-permute-start | bytes 98312 | tf_op jit(solution)/shard_map/ppermute | solution.py:134
